TPU v7x, 32 devices: a whole 2x2x4 slice. The times are simulated.
32 devices in a mesh: space: 8 (over z, y), depth: 4 (over x, core).
Axes of the slice: x: 2, y: 2, z: 4, core: 2. Of those that a mesh axis runs over, the one named last changes fastest.
Arguments:
- features: bfloat16 [8, 4, 512, 128], P('space', 'depth'), may hold values from -6 to 6
- cotangent: bfloat16 [8, 4, 512, 128], P('space', 'depth'), may hold values from -6 to 6
- first_kernel: bfloat16 [27, 128, 128], replicated, may hold values from -0.109375 to 0.109375
- second_kernel: bfloat16 [27, 128, 128], replicated, may hold values from -0.109375 to 0.109375
- slot_tile: int32 [8, 4], P('space'), may hold values from 0 to 3, as said below
- slot_used: int32 [8, 4], P('space'), may hold values from 0 to 1, as said below
Outputs:
- input_grad: bfloat16 [8, 4, 512, 128], P('space', 'depth')
- first_kernel_grad: float32 [442368], P(('space', 'depth'))
- second_kernel_grad: float32 [442368], P(('space', 'depth'))
Inputs may be any that keep to these rules, and one draw needn't show every extreme that they name: `slot_tile`: in each column the used slots hold distinct z positions that form one unbroken run; in some column every slot is used. `slot_used`: every column has at least one used slot.
All inputs are finite; a program needn't handle non-finite values.
Results may differ from a plain program's by a relative error of at most 0.006.
Values may be sent and summed in bfloat16 or wider, within the bound.
No kernel may reach another device: no remote copies, remote signals or barrier semaphores. Data moves between devices by JAX's collectives and lax.ppermute only.
A program may use at most 64 MiB of HBM per device.

v0:
```python
import jax
import jax.numpy as jnp
from jax import lax
from jax.sharding import PartitionSpec as P

TE = 8
GY = 8


SLOPE_COEF = 0.7978845608028654
CUBIC_COEF = 0.044715


def from_behind(block, axis, distance):
    devices = range(lax.axis_size(axis))
    route = [(i - distance, i) for i in devices if i - distance in devices]
    return lax.ppermute(block, axis, route)


def gelu_pair(values):
    inner_arg = SLOPE_COEF * (values + CUBIC_COEF * values * values * values)
    tangent = jnp.tanh(inner_arg)
    output = 0.5 * values * (1.0 + tangent)
    derivative = 0.5 * (1.0 + tangent) + 0.5 * values * (1.0 - tangent * tangent) * SLOPE_COEF * (
        1.0 + 3.0 * CUBIC_COEF * values * values
    )
    return (output, derivative)


def gelu_slope(values):
    inner_arg = SLOPE_COEF * (values + CUBIC_COEF * values * values * values)
    tangent = jnp.tanh(inner_arg)
    return 0.5 * (1.0 + tangent) + 0.5 * values * (1.0 - tangent * tangent) * SLOPE_COEF * (
        1.0 + 3.0 * CUBIC_COEF * values * values
    )


def place_matrix(slot_tile, slot_used, position_count):
    positions = jnp.arange(position_count, dtype=jnp.int32)
    matches = (slot_tile[0][None, :] == positions[:, None]) & (slot_used[0][None, :] == 1)
    return matches.astype(jnp.bfloat16)


def dense_column(tile_rows, placement):
    summed = jnp.einsum(
        "tj,jvc->tvc",
        placement,
        lax.all_gather(tile_rows, "depth", axis=0, tiled=True),
        preferred_element_type=jnp.float32,
    )
    return summed.astype(jnp.bfloat16).reshape(-1, TE, TE, summed.shape[-1])


def extend_sides(own_block, move_face, space_index):
    y_coord = space_index % GY
    below = move_face(own_block[:, :, -1:, :], 1) * (y_coord > 0).astype(own_block.dtype)
    above = move_face(own_block[:, :, :1, :], -1) * (y_coord < GY - 1).astype(own_block.dtype)
    widened = jnp.concatenate([below, own_block, above], axis=2)
    behind = move_face(widened[:, -1:, :, :], GY)
    ahead = move_face(widened[:, :1, :, :], -GY)
    return jnp.concatenate([behind, widened, ahead], axis=1)


def pad_depth(own_block):
    return jnp.pad(own_block, ((1, 1), (0, 0), (0, 0), (0, 0)))


def windows_at(padded, positions):

    def one_window(z_index):
        return lax.dynamic_slice_in_dim(padded, z_index * TE, TE + 2, 0)

    return jax.vmap(one_window)(positions)


def unfold(windows, flipped):
    pieces = []
    for kernel_tap in range(27):
        z_step, x_step, y_step = (kernel_tap // 9, kernel_tap // 3 % 3, kernel_tap % 3)
        if flipped:
            z_step, x_step, y_step = (2 - z_step, 2 - x_step, 2 - y_step)
        pieces.append(
            windows[:, z_step : z_step + TE, x_step : x_step + TE, y_step : y_step + TE, :]
        )
    stacked = jnp.concatenate(pieces, axis=-1)
    return stacked.reshape(-1, stacked.shape[-1])


def tile_sum(columns, delta):
    return lax.dot_general(
        columns, delta, (((0,), (0,)), ((), ())), preferred_element_type=jnp.float32
    )


def on_device(features, cotangent, first_kernel, second_kernel, slot_tile, slot_used):
    depth_index = lax.axis_index("depth")
    space_index = lax.axis_index("space")
    slot_count = features.shape[1]
    voxels = features.shape[2]
    channels = features.shape[3]
    position_count = slot_tile.shape[1]
    placement = place_matrix(slot_tile, slot_used, position_count)
    own_first = depth_index * slot_count
    own_tiles = lax.dynamic_slice_in_dim(slot_tile[0], own_first, slot_count, 0)
    own_used = lax.dynamic_slice_in_dim(slot_used[0], own_first, slot_count, 0).astype(jnp.float32)
    feature_slots = features[0]
    upstream_slots = cotangent[0]

    def column_move(face, offset):
        return from_behind(face, "space", offset)

    def halo_of(tile_rows):
        column = dense_column(tile_rows.reshape(slot_count, voxels, channels), placement)
        return pad_depth(extend_sides(column, column_move, space_index))

    upstream = upstream_slots.reshape(-1, channels)
    source_column = halo_of(feature_slots)
    alive_rows = jnp.repeat(own_used, voxels)[:, None]
    forward_one = first_kernel.reshape(-1, channels)
    forward_two = second_kernel.reshape(-1, channels)
    backward_one = jnp.transpose(first_kernel, (0, 2, 1)).reshape(-1, channels)
    backward_two = jnp.transpose(second_kernel, (0, 2, 1)).reshape(-1, channels)
    source_cols = unfold(windows_at(source_column, own_tiles), False)
    pre_one = jnp.dot(source_cols, forward_one, preferred_element_type=jnp.float32)
    act_value, slope_one = gelu_pair(pre_one)
    act_one = (act_value * alive_rows).astype(jnp.bfloat16)
    act_cols = unfold(windows_at(halo_of(act_one), own_tiles), False)
    pre_two = jnp.dot(act_cols, forward_two, preferred_element_type=jnp.float32)
    slope_two = gelu_slope(pre_two)
    delta_two = (upstream.astype(jnp.float32) * slope_two * alive_rows).astype(jnp.bfloat16)
    second_grad = tile_sum(act_cols, delta_two).reshape(-1) * (1.0 / voxels)
    back_one = jnp.dot(
        unfold(windows_at(halo_of(delta_two), own_tiles), True),
        backward_two,
        preferred_element_type=jnp.float32,
    )
    delta_one = (back_one * slope_one * alive_rows).astype(jnp.bfloat16)
    first_grad = tile_sum(source_cols, delta_one).reshape(-1) * (1.0 / voxels)
    back_zero = jnp.dot(
        unfold(windows_at(halo_of(delta_one), own_tiles), True),
        backward_one,
        preferred_element_type=jnp.float32,
    )
    used_rows = jnp.repeat(own_used, voxels)[:, None]
    input_grad = (back_zero * used_rows).astype(jnp.bfloat16).reshape(features.shape)
    first_share, second_share = (
        lax.psum_scatter(first_grad, ("space", "depth"), scatter_dimension=0, tiled=True),
        lax.psum_scatter(second_grad, ("space", "depth"), scatter_dimension=0, tiled=True),
    )
    return (input_grad, first_share, second_share)


def solution(mesh):
    return jax.shard_map(
        on_device,
        mesh=mesh,
        in_specs=(
            P("space", "depth", None, None),
            P("space", "depth", None, None),
            P(),
            P(),
            P("space", None),
            P("space", None),
        ),
        out_specs=(P("space", "depth", None, None), P(("space", "depth")), P(("space", "depth"))),
        check_vma=False,
    )
```

profile of v0, /device:TPU:0, one launch (start us, length us, event | category | flops | bytes accessed | tf_op | source)
XLA Modules:
  0.0 275.2 jit_solution(10029815441061926559)
XLA Ops:
  7.2 0.7 compare_bitcast_fusion
  7.9 8.8 %all-gather = bf16[4,1,512,128]{3,2,1,0:T(8,128)(2,1)S(1)} all-gather(bf16[1,1,512,128]{3,2,1,0:T(8,128)(2,1)} %param.6), channel_id=2, replica_groups=mesh['space'=8,'depth'=4] {'depth'}, dimensions={0}, use_global_device_ids=true | all-gather | bytes 655360 | tf_op jit(solution)/shard_map/all_gather | solution.py:48
  16.7 0.7 fusion.76
  17.4 0.5 convolution_convert_fusion.3
  18.1 3.4 %collective-permute-start = (bf16[32,8,1,128]{3,2,1,0:T(2,128)(2,1)S(1)}, bf16[32,8,1,128]{3,2,1,0:T(2,128)(2,1)S(1)}, u32[]{:S(2)}, u32[]{:S(2)}) collective-permute-start(bf16[32,8,1,128]{3,2,1,0:T(2,128)(2,1)S(1)} %get-tuple-element.65), channel_id=1, source_target_pairs={{0,4},{4,8},{8,12},{12,16},{16,20},{20,24},{24,28},{1,5},{5,9},{9,... | collective-permute-start | bytes 196616 | tf_op jit(solution)/shard_map/ppermute | solution.py:17
  21.6 1.3 collective-permute-start.1
  22.9 1.9 collective-permute-done
  25.0 4.0 %collective-permute-done.1 = bf16[32,8,1,128]{3,2,1,0:T(2,128)(2,1)S(1)} collective-permute-done((bf16[32,8,1,128]{3,2,1,0:T(2,128)(2,1)S(1)}, bf16[32,8,1,128]{3,2,1,0:T(2,128)(2,1)S(1)}, u32[]{:S(2)}, u32[]{:S(2)}) %collective-permute-start.1) | collective-permute-done | bytes 65568 | tf_op jit(solution)/shard_map/ppermute | solution.py:17
  29.2 0.7 collective-permute-start.2
  29.9 0.7 collective-permute-start.3
  31.0 0.6 fusion.86
  33.5 0.6 fusion.53
  35.9 2.5 multiply_convert_fusion
  38.4 6.8 %all-gather.1 = bf16[2048,128]{1,0:T(8,128)(2,1)S(1)} all-gather(bf16[512,128]{1,0:T(8,128)(2,1)S(1)} %get-tuple-element.67), channel_id=3, replica_groups=mesh['space'=8,'depth'=4] {'depth'}, dimensions={0}, use_global_device_ids=true | all-gather | bytes 655360 | tf_op jit(solution)/shard_map/all_gather | solution.py:48
  45.9 4.3 %collective-permute-start.4 = (bf16[32,8,1,128]{3,2,1,0:T(2,128)(2,1)S(1)}, bf16[32,8,1,128]{3,2,1,0:T(2,128)(2,1)S(1)}, u32[]{:S(2)}, u32[]{:S(2)}) collective-permute-start(bf16[32,8,1,128]{3,2,1,0:T(2,128)(2,1)S(1)} %get-tuple-element.63), channel_id=1, source_target_pairs={{0,4},{4,8},{8,12},{12,16},{16,20},{20,24},{24,28},{1,5},{5,9},{9,... | collective-permute-start | bytes 196616 | tf_op jit(solution)/shard_map/ppermute | solution.py:17
  50.3 1.3 collective-permute-start.5
  51.6 1.9 collective-permute-done.4
  53.6 4.0 %collective-permute-done.5 = bf16[32,8,1,128]{3,2,1,0:T(2,128)(2,1)S(1)} collective-permute-done((bf16[32,8,1,128]{3,2,1,0:T(2,128)(2,1)S(1)}, bf16[32,8,1,128]{3,2,1,0:T(2,128)(2,1)S(1)}, u32[]{:S(2)}, u32[]{:S(2)}) %collective-permute-start.5) | collective-permute-done | bytes 65568 | tf_op jit(solution)/shard_map/ppermute | solution.py:17
  57.9 0.7 collective-permute-start.6
  58.6 0.7 collective-permute-start.7
  61.6 2.6 fusion.63
  64.2 6.6 %all-gather.2 = bf16[2048,128]{1,0:T(8,128)(2,1)S(1)} all-gather(bf16[512,128]{1,0:T(8,128)(2,1)S(1)} %get-tuple-element.69), channel_id=4, replica_groups=mesh['space'=8,'depth'=4] {'depth'}, dimensions={0}, use_global_device_ids=true | all-gather | bytes 655360 | tf_op jit(solution)/shard_map/all_gather | solution.py:48
  71.6 4.1 %collective-permute-start.8 = (bf16[32,8,1,128]{3,2,1,0:T(2,128)(2,1)S(1)}, bf16[32,8,1,128]{3,2,1,0:T(2,128)(2,1)S(1)}, u32[]{:S(2)}, u32[]{:S(2)}) collective-permute-start(bf16[32,8,1,128]{3,2,1,0:T(2,128)(2,1)S(1)} %get-tuple-element.61), channel_id=1, source_target_pairs={{0,4},{4,8},{8,12},{12,16},{16,20},{20,24},{24,28},{1,5},{5,9},{9,... | collective-permute-start | bytes 196616 | tf_op jit(solution)/shard_map/ppermute | solution.py:17
  75.7 1.3 collective-permute-start.9
  77.0 1.9 collective-permute-done.8
  79.1 4.0 %collective-permute-done.9 = bf16[32,8,1,128]{3,2,1,0:T(2,128)(2,1)S(1)} collective-permute-done((bf16[32,8,1,128]{3,2,1,0:T(2,128)(2,1)S(1)}, bf16[32,8,1,128]{3,2,1,0:T(2,128)(2,1)S(1)}, u32[]{:S(2)}, u32[]{:S(2)}) %collective-permute-start.9) | collective-permute-done | bytes 65568 | tf_op jit(solution)/shard_map/ppermute | solution.py:17
  83.2 0.9 pad_maximum_fusion.5
  84.1 1.3 collective-permute-start.10
  85.4 1.3 collective-permute-start.11
  86.7 2.2 copy.32
  88.9 2.2 copy.29
  91.2 1.6 fusion.51
  94.6 1.9 fusion.3
  96.5 6.7 %all-gather.3 = bf16[2048,128]{1,0:T(8,128)(2,1)S(1)} all-gather(bf16[512,128]{1,0:T(8,128)(2,1)S(1)} %fusion.3), channel_id=5, replica_groups=mesh['space'=8,'depth'=4] {'depth'}, dimensions={0}, use_global_device_ids=true | all-gather | bytes 655360 | tf_op jit(solution)/shard_map/all_gather | solution.py:48
  103.2 0.5 convolution_convert_fusion
  104.0 4.0 %collective-permute-start.12 = (bf16[32,8,1,128]{3,2,1,0:T(2,128)(2,1)S(1)}, bf16[32,8,1,128]{3,2,1,0:T(2,128)(2,1)S(1)}, u32[]{:S(2)}, u32[]{:S(2)}) collective-permute-start(bf16[32,8,1,128]{3,2,1,0:T(2,128)(2,1)S(1)} %get-tuple-element.59), channel_id=1, source_target_pairs={{0,4},{4,8},{8,12},{12,16},{16,20},{20,24},{24,28},{1,5},{5,9},{9,... | collective-permute-start | bytes 196616 | tf_op jit(solution)/shard_map/ppermute | solution.py:17
  108.0 3.2 %fusion = f32[442368]{0:T(1024)} fusion(bf16[512,3456]{1,0:T(8,128)(2,1)S(1)} %bitcast.81, f32[512,128]{1,0:T(8,128)S(1)} %copy-done.13, bf16[1,1,512,128]{3,2,1,0:T(8,128)(2,1)S(1)} %copy-done.15, f32[]{:T(128)} %bitcast.11), kind=kOutput, calls=%fused_computation.1 | convolution fusion | flops 454803456 | bytes 5701636 | tf_op jit(solution)/shard_map/dot_general | solution.py:90
  111.1 1.3 collective-permute-start.13
  112.6 5.9 %collective-permute-done.13 = bf16[32,8,1,128]{3,2,1,0:T(2,128)(2,1)S(1)} collective-permute-done((bf16[32,8,1,128]{3,2,1,0:T(2,128)(2,1)S(1)}, bf16[32,8,1,128]{3,2,1,0:T(2,128)(2,1)S(1)}, u32[]{:S(2)}, u32[]{:S(2)}) %collective-permute-start.13) | collective-permute-done | bytes 65568 | tf_op jit(solution)/shard_map/ppermute | solution.py:17
  118.7 0.9 pad_maximum_fusion.2
  119.5 1.3 collective-permute-start.14
  120.8 1.3 collective-permute-start.15
  122.1 2.4 fusion.1
  124.5 1.6 fusion.50
  127.9 2.4 fusion.5
  130.2 135.0 %all-reduce.9.cloned.1.call-done = (f32[442368]{0:T(1024)}, f32[442368]{0:T(1024)}) async-done(((f32[442368]{0:T(1024)}, f32[442368]{0:T(1024)}), (f32[442368]{0:T(1024)}, f32[442368]{0:T(1024)})) %all-reduce.9.cloned.1.call-update) | async-done | bytes 3538960
  265.2 1.5 dynamic-slice.18
  266.8 1.5 dynamic-slice.19
  (179 shorter events, 10.9 us)
Async XLA Ops:
  7.2 23.8 %copy-start.17 = (s32[1,4]{1,0:T(1,128)S(1)}, s32[1,4]{1,0:T(1,128)}, u32[]{:S(2)}) copy-start(s32[1,4]{1,0:T(1,128)} %param.11) | copy-start | bytes 52
  7.2 23.8 %copy-start.16 = (s32[1,4]{1,0:T(1,128)S(1)}, s32[1,4]{1,0:T(1,128)}, u32[]{:S(2)}) copy-start(s32[1,4]{1,0:T(1,128)} %param.10) | copy-start | bytes 52
  7.2 258.1 %all-reduce.9.cloned.1.call-start = ((), (), s32[]{:S(2)}) async-start(), calls=%async_computation | async-start | bytes 7077888
  18.1 6.7 %collective-permute-start = (bf16[32,8,1,128]{3,2,1,0:T(2,128)(2,1)S(1)}, bf16[32,8,1,128]{3,2,1,0:T(2,128)(2,1)S(1)}, u32[]{:S(2)}, u32[]{:S(2)}) collective-permute-start(bf16[32,8,1,128]{3,2,1,0:T(2,128)(2,1)S(1)} %get-tuple-element.65), channel_id=1, source_target_pairs={{0,4},{4,8},{8,12},{12,16},{16,20},{20,24},{24,28},{1,5},{5,9},{9,... | collective-permute-start | bytes 196616 | tf_op jit(solution)/shard_map/ppermute | solution.py:17
  21.6 7.4 %collective-permute-start.1 = (bf16[32,8,1,128]{3,2,1,0:T(2,128)(2,1)S(1)}, bf16[32,8,1,128]{3,2,1,0:T(2,128)(2,1)S(1)}, u32[]{:S(2)}, u32[]{:S(2)}) collective-permute-start(bf16[32,8,1,128]{3,2,1,0:T(2,128)(2,1)S(1)} %get-tuple-element.66), channel_id=1, source_target_pairs={{4,0},{8,4},{12,8},{16,12},{20,16},{24,20},{28,24},{5,1},{9,5},{13... | collective-permute-start | bytes 196616 | tf_op jit(solution)/shard_map/ppermute | solution.py:17
  29.2 4.3 %collective-permute-start.2 = (bf16[32,1,10,128]{3,2,1,0:T(8,128)(2,1)S(1)}, bf16[32,1,10,128]{3,2,1,0:T(8,128)(2,1)S(1)}, u32[]{:S(2)}, u32[]{:S(2)}) collective-permute-start(bf16[32,1,10,128]{3,2,1,0:T(8,128)(2,1)S(1)} %get-tuple-element.57), channel_id=1, source_target_pairs={} | collective-permute-start | bytes 245768 | tf_op jit(solution)/shard_map/ppermute | solution.py:17
  29.9 3.6 %collective-permute-start.3 = (bf16[32,1,10,128]{3,2,1,0:T(8,128)(2,1)S(1)}, bf16[32,1,10,128]{3,2,1,0:T(8,128)(2,1)S(1)}, u32[]{:S(2)}, u32[]{:S(2)}) collective-permute-start(bf16[32,1,10,128]{3,2,1,0:T(8,128)(2,1)S(1)} %get-tuple-element.58), channel_id=1, source_target_pairs={} | collective-permute-start | bytes 245768 | tf_op jit(solution)/shard_map/ppermute | solution.py:17
  34.1 25.2 %copy-start.4 = (pred[10,10,10,128]{3,2,1,0:T(8,128)(4,1)}, pred[10,10,10,128]{3,2,1,0:T(8,128)(4,1)S(1)}, u32[]{:S(2)}) copy-start(pred[10,10,10,128]{3,2,1,0:T(8,128)(4,1)S(1)} %get-tuple-element.50) | copy-start | bytes 384004
  34.1 1.8 copy-start.9
  45.9 7.6 %collective-permute-start.4 = (bf16[32,8,1,128]{3,2,1,0:T(2,128)(2,1)S(1)}, bf16[32,8,1,128]{3,2,1,0:T(2,128)(2,1)S(1)}, u32[]{:S(2)}, u32[]{:S(2)}) collective-permute-start(bf16[32,8,1,128]{3,2,1,0:T(2,128)(2,1)S(1)} %get-tuple-element.63), channel_id=1, source_target_pairs={{0,4},{4,8},{8,12},{12,16},{16,20},{20,24},{24,28},{1,5},{5,9},{9,... | collective-permute-start | bytes 196616 | tf_op jit(solution)/shard_map/ppermute | solution.py:17
  50.3 7.4 %collective-permute-start.5 = (bf16[32,8,1,128]{3,2,1,0:T(2,128)(2,1)S(1)}, bf16[32,8,1,128]{3,2,1,0:T(2,128)(2,1)S(1)}, u32[]{:S(2)}, u32[]{:S(2)}) collective-permute-start(bf16[32,8,1,128]{3,2,1,0:T(2,128)(2,1)S(1)} %get-tuple-element.64), channel_id=1, source_target_pairs={{4,0},{8,4},{12,8},{16,12},{20,16},{24,20},{28,24},{5,1},{9,5},{13... | collective-permute-start | bytes 196616 | tf_op jit(solution)/shard_map/ppermute | solution.py:17
  57.9 1.3 collective-permute-start.6
  58.6 0.7 collective-permute-start.7
  59.8 1.8 copy-start.10
  59.8 1.8 copy-start.14
  61.6 9.7 %copy-start.2 = (bf16[1,8,8,8,3456]{4,3,2,1,0:T(8,128)(2,1)}, bf16[1,8,8,8,3456]{4,3,2,1,0:T(8,128)(2,1)S(1)}, u32[]{:S(2)}) copy-start(bf16[1,8,8,8,3456]{4,3,2,1,0:T(8,128)(2,1)S(1)} %constant_dynamic-update-slice_fusion.27) | copy-start | bytes 10616836
  71.4 11.8 %copy-start.1 = (bf16[4,512,128]{2,1,0:T(8,128)(2,1)}, bf16[4,512,128]{2,1,0:T(8,128)(2,1)S(1)}, u32[]{:S(2)}) copy-start(bf16[4,512,128]{2,1,0:T(8,128)(2,1)S(1)} %copy.28) | copy-start | bytes 1572868
  71.6 7.3 %collective-permute-start.8 = (bf16[32,8,1,128]{3,2,1,0:T(2,128)(2,1)S(1)}, bf16[32,8,1,128]{3,2,1,0:T(2,128)(2,1)S(1)}, u32[]{:S(2)}, u32[]{:S(2)}) collective-permute-start(bf16[32,8,1,128]{3,2,1,0:T(2,128)(2,1)S(1)} %get-tuple-element.61), channel_id=1, source_target_pairs={{0,4},{4,8},{8,12},{12,16},{16,20},{20,24},{24,28},{1,5},{5,9},{9,... | collective-permute-start | bytes 196616 | tf_op jit(solution)/shard_map/ppermute | solution.py:17
  75.7 7.4 %collective-permute-start.9 = (bf16[32,8,1,128]{3,2,1,0:T(2,128)(2,1)S(1)}, bf16[32,8,1,128]{3,2,1,0:T(2,128)(2,1)S(1)}, u32[]{:S(2)}, u32[]{:S(2)}) collective-permute-start(bf16[32,8,1,128]{3,2,1,0:T(2,128)(2,1)S(1)} %get-tuple-element.62), channel_id=1, source_target_pairs={{4,0},{8,4},{12,8},{16,12},{20,16},{24,20},{28,24},{5,1},{9,5},{13... | collective-permute-start | bytes 196616 | tf_op jit(solution)/shard_map/ppermute | solution.py:17
  79.1 5.0 %copy-start.6 = (bf16[32,8,1,128]{3,2,1,0:T(2,128)(2,1)}, bf16[32,8,1,128]{3,2,1,0:T(2,128)(2,1)S(1)}, u32[]{:S(2)}) copy-start(bf16[32,8,1,128]{3,2,1,0:T(2,128)(2,1)S(1)} %broadcast_multiply_fusion.5) | copy-start | bytes 196612
  83.2 0.9 copy-start.8
  84.1 7.1 %collective-permute-start.10 = (bf16[32,1,10,128]{3,2,1,0:T(8,128)(2,1)}, bf16[32,1,10,128]{3,2,1,0:T(8,128)(2,1)}, u32[]{:S(2)}, u32[]{:S(2)}) collective-permute-start(bf16[32,1,10,128]{3,2,1,0:T(8,128)(2,1)} %get-tuple-element.53), channel_id=1, source_target_pairs={} | collective-permute-start | bytes 245768 | tf_op jit(solution)/shard_map/ppermute | solution.py:17
  85.4 5.8 %collective-permute-start.11 = (bf16[32,1,10,128]{3,2,1,0:T(8,128)(2,1)}, bf16[32,1,10,128]{3,2,1,0:T(8,128)(2,1)}, u32[]{:S(2)}, u32[]{:S(2)}) collective-permute-start(bf16[32,1,10,128]{3,2,1,0:T(8,128)(2,1)} %get-tuple-element.54), channel_id=1, source_target_pairs={} | collective-permute-start | bytes 245768 | tf_op jit(solution)/shard_map/ppermute | solution.py:17
  92.7 1.8 copy-start.12
  92.8 1.8 copy-start.18
  94.6 13.4 %copy-start.3 = (bf16[1,8,8,8,3456]{4,3,2,1,0:T(8,128)(2,1)S(1)}, bf16[1,8,8,8,3456]{4,3,2,1,0:T(8,128)(2,1)}, u32[]{:S(2)}) copy-start(bf16[1,8,8,8,3456]{4,3,2,1,0:T(8,128)(2,1)} %copy-done.2) | copy-start | bytes 10616836
  94.6 13.4 %copy-start.13 = (f32[512,128]{1,0:T(8,128)S(1)}, f32[512,128]{1,0:T(8,128)}, u32[]{:S(2)}) copy-start(f32[512,128]{1,0:T(8,128)} %get-tuple-element.70) | copy-start | bytes 786436
  94.6 13.4 %copy-start.15 = (bf16[1,1,512,128]{3,2,1,0:T(8,128)(2,1)S(1)}, bf16[1,1,512,128]{3,2,1,0:T(8,128)(2,1)}, u32[]{:S(2)}) copy-start(bf16[1,1,512,128]{3,2,1,0:T(8,128)(2,1)} %param.7) | copy-start | bytes 393220
  103.8 14.9 %copy-start = (bf16[4,512,128]{2,1,0:T(8,128)(2,1)}, bf16[4,512,128]{2,1,0:T(8,128)(2,1)S(1)}, u32[]{:S(2)}) copy-start(bf16[4,512,128]{2,1,0:T(8,128)(2,1)S(1)} %copy.31) | copy-start | bytes 1572868
  104.0 8.5 %collective-permute-start.12 = (bf16[32,8,1,128]{3,2,1,0:T(2,128)(2,1)S(1)}, bf16[32,8,1,128]{3,2,1,0:T(2,128)(2,1)S(1)}, u32[]{:S(2)}, u32[]{:S(2)}) collective-permute-start(bf16[32,8,1,128]{3,2,1,0:T(2,128)(2,1)S(1)} %get-tuple-element.59), channel_id=1, source_target_pairs={{0,4},{4,8},{8,12},{12,16},{16,20},{20,24},{24,28},{1,5},{5,9},{9,... | collective-permute-start | bytes 196616 | tf_op jit(solution)/shard_map/ppermute | solution.py:17
  111.1 7.4 %collective-permute-start.13 = (bf16[32,8,1,128]{3,2,1,0:T(2,128)(2,1)S(1)}, bf16[32,8,1,128]{3,2,1,0:T(2,128)(2,1)S(1)}, u32[]{:S(2)}, u32[]{:S(2)}) collective-permute-start(bf16[32,8,1,128]{3,2,1,0:T(2,128)(2,1)S(1)} %get-tuple-element.60), channel_id=1, source_target_pairs={{4,0},{8,4},{12,8},{16,12},{20,16},{24,20},{28,24},{5,1},{9,5},{13... | collective-permute-start | bytes 196616 | tf_op jit(solution)/shard_map/ppermute | solution.py:17
  112.6 6.9 %copy-start.5 = (bf16[32,8,1,128]{3,2,1,0:T(2,128)(2,1)}, bf16[32,8,1,128]{3,2,1,0:T(2,128)(2,1)S(1)}, u32[]{:S(2)}) copy-start(bf16[32,8,1,128]{3,2,1,0:T(2,128)(2,1)S(1)} %broadcast_multiply_fusion.4) | copy-start | bytes 196612
  118.7 0.9 copy-start.7
  119.5 5.0 %collective-permute-start.14 = (bf16[32,1,10,128]{3,2,1,0:T(8,128)(2,1)}, bf16[32,1,10,128]{3,2,1,0:T(8,128)(2,1)}, u32[]{:S(2)}, u32[]{:S(2)}) collective-permute-start(bf16[32,1,10,128]{3,2,1,0:T(8,128)(2,1)} %get-tuple-element.51), channel_id=1, source_target_pairs={} | collective-permute-start | bytes 245768 | tf_op jit(solution)/shard_map/ppermute | solution.py:17
  120.8 3.7 %collective-permute-start.15 = (bf16[32,1,10,128]{3,2,1,0:T(8,128)(2,1)}, bf16[32,1,10,128]{3,2,1,0:T(8,128)(2,1)}, u32[]{:S(2)}, u32[]{:S(2)}) collective-permute-start(bf16[32,1,10,128]{3,2,1,0:T(8,128)(2,1)} %get-tuple-element.52), channel_id=1, source_target_pairs={} | collective-permute-start | bytes 245768 | tf_op jit(solution)/shard_map/ppermute | solution.py:17
  126.1 1.8 copy-start.11
Sparse Core Ops, SparseCore 0:
  124.6 140.5 all-reduce.8
where the time goes:
time: 276 us; the launch traced here: 275 us
  waiting for transfers between devices  159 us (58%)
  starting transfers between devices  28.9 us (10%)
  blocking collectives  28.8 us (10%)
  between operations  17.1 us (6%)
  matrix products  16.9 us (6%)
  local copies, waits for them, and re-layouts  15.1 us (5%)
  other arithmetic  9.62 us (3%)
    unnamed x2, waiting for transfers between devices  135 us
    ppermute x16, starting transfers between devices, from_behind(): return lax.ppermute(block, axis, route)  28.9 us
    all_gather x4, blocking collectives, dense_column(): lax.all_gather(tile_rows, 'depth', axis=0, tiled=True)  28.8 us
    ppermute x16, waiting for transfers between devices, from_behind(): return lax.ppermute(block, axis, route)  23.6 us
    unnamed x146, local copies, waits for them, and re-layouts  13.9 us
  transfers between devices with their start and end apart: 17, of which 8 were waited for; matrix products, arithmetic and copies ran while one was open for 6% of the time, Pallas kernels for 0%

commit v1 on v0

--- a/solution.py
+++ b/solution.py
@@ -1,6 +1,8 @@
 import jax
 import jax.numpy as jnp
 from jax import lax
+from jax.experimental import pallas as pl
+from jax.experimental.pallas import tpu as pltpu
 from jax.sharding import PartitionSpec as P
 
 TE = 8
@@ -92,7 +94,7 @@
     )
 
 
-def on_device(features, cotangent, first_kernel, second_kernel, slot_tile, slot_used):
+def on_device_wide(features, cotangent, first_kernel, second_kernel, slot_tile, slot_used):
     depth_index = lax.axis_index("depth")
     space_index = lax.axis_index("space")
     slot_count = features.shape[1]
@@ -150,9 +152,379 @@
     return (input_grad, first_share, second_share)
 
 
+HALO = 4
+BF = jnp.bfloat16
+F32 = jnp.float32
+
+
+class Region:
+    def __init__(self, even, odd, z_size, y_size):
+        self.even, self.odd, self.z_size, self.y_size = even, odd, z_size, y_size
+
+    def planes(self, first):
+        return (self.odd, (first - 1) // 2) if first % 2 else (self.even, first // 2)
+
+    def store_row(self, y_pair, y_parity, column):
+        z_size, width, channels = column.shape
+        place = lax.broadcasted_iota(jnp.int32, column.shape, 1)
+        before = jnp.where(place == 0, 0.0, pltpu.roll(column, 1, 1))
+        after = jnp.where(place == width - 1, 0.0, pltpu.roll(column, width - 1, 1))
+        wide = jnp.concatenate([before, column, after], axis=-1)
+        self.even[:, y_pair, y_parity] = wide.reshape(z_size // 2, 2 * width, 3 * channels).astype(BF)
+        if self.odd is not None:
+            inner = wide[1:-1].reshape(z_size // 2 - 1, 2 * width, 3 * channels)
+            self.odd[:, y_pair, y_parity] = inner.astype(BF)
+
+    def tile_rows(self, z_first, y_first, lanes, lane_first, edge):
+        ref, q_first = self.planes(z_first)
+        parts = []
+        for y_at in range(y_first, y_first + edge):
+            part = ref[q_first : q_first + edge // 2, y_at // 2, y_at % 2, :, lane_first : lane_first + lanes]
+            parts.append(part.reshape(-1, lanes))
+        return jnp.concatenate(parts, axis=0)
+
+
+def region_shapes(z_size, y_size, width, channels, with_odd):
+    tail = (y_size // 2, 2, 2 * width, 3 * channels)
+    shapes = [pltpu.VMEM((z_size // 2,) + tail, BF)]
+    if with_odd:
+        shapes.append(pltpu.VMEM((z_size // 2 - 1,) + tail, BF))
+    return shapes
+
+
+def convolve_region(region, weights, transposed, result):
+    q_size, r_size = region.z_size // 2 - 1, region.y_size // 2 - 1
+    channels = region.even.shape[-1] // 3
+    pieces = []
+    for z_tap in range(3):
+        ref, q_first = region.planes(z_tap)
+        for x_tap in range(3):
+            for y_at in range(4):
+                piece = ref[
+                    q_first : q_first + q_size,
+                    y_at // 2 : y_at // 2 + r_size,
+                    y_at % 2,
+                    :,
+                    x_tap * channels : (x_tap + 1) * channels,
+                ]
+                pieces.append(piece.reshape(-1, channels))
+    left = jnp.concatenate(pieces, axis=1)
+    contract = (((1,), (1 if transposed else 0,)), ((), ()))
+    product = lax.dot_general(left, weights[...], contract, preferred_element_type=F32)
+    result[0:q_size, 0:r_size] = product.reshape(q_size, r_size, product.shape[0] // (q_size * r_size), -1)
+
+
+def kernel_copies(kernel, weights, sems, transposed):
+    channels = kernel.shape[-1]
+    copies = []
+    for z_tap in range(3):
+        for x_tap in range(3):
+            block = (z_tap * 3 + x_tap) * 4 * channels
+            for parity in range(2):
+                out = pl.ds(parity * channels, channels)
+                if transposed:
+                    for y_tap in range(3):
+                        tap = (2 - z_tap) * 9 + (2 - x_tap) * 3 + 2 - y_tap
+                        lanes = pl.ds(block + (parity + y_tap) * channels, channels)
+                        copies.append((kernel.at[tap], weights.at[out, lanes]))
+                else:
+                    tap = z_tap * 9 + x_tap * 3
+                    for y_tap in range(3):
+                        rows = pl.ds(block + (parity + y_tap) * channels, channels)
+                        copies.append((kernel.at[tap + y_tap], weights.at[rows, out]))
+    return [pltpu.make_async_copy(a, b, sems.at[n]) for n, (a, b) in enumerate(copies)]
+
+
+def clear_unused(weights, transposed):
+    channels = min(weights.shape) // 2
+    blank = jnp.zeros((channels, channels), BF)
+    for block in range(9):
+        for parity, y_at in ((0, 3), (1, 0)):
+            inner = pl.ds((block * 4 + y_at) * channels, channels)
+            out = pl.ds(parity * channels, channels)
+            if transposed:
+                weights[out, inner] = blank
+            else:
+                weights[inner, out] = blank
+
+
+def place_slots(slots, codes, sources, volume, mask):
+    raw, offset, stride, y_first, y_count, cls, lifted = sources
+    for block in range(len(raw)):
+        code = codes[cls, slots[block]]
+
+        @pl.when(code > 0)
+        def _():
+            z_first = HALO + (code - 1) * TE
+            rows = TE * TE * stride
+            lifted[0:rows] = raw[block][offset : offset + rows].astype(F32)
+            for z_at in range(TE):
+                for y_at in range(y_count):
+                    volume[z_first + z_at, y_first + y_at] = lifted[pl.ds(z_at * TE * stride + y_at, TE, stride=stride)]
+            if mask is not None:
+                mask[cls, pl.ds(z_first, TE)] = jnp.ones((TE,) + mask.shape[2:], F32)
+
+
+def backward_kernel(block_count, packs_per, channels, tiles, codes, depth_at, *refs):
+    own = refs[:block_count]
+    rims = refs[block_count : 2 * block_count]
+    first_kernel, second_kernel = refs[2 * block_count : 2 * block_count + 2]
+    input_grad, grads = refs[2 * block_count + 2 : 2 * block_count + 4]
+    rest = list(refs[2 * block_count + 4 :])
+
+    def take():
+        return rest.pop(0)
+
+    volume, upstream, mask, lifted, result, grad_rows = (take() for _ in range(6))
+    weights = [take() for _ in range(4)]
+    sems = [take() for _ in range(4)]
+    regions = []
+    for number in range(tiles):
+        halo = HALO - number
+        group = []
+        for layer in range(4):
+            size = TE + 2 * (halo - layer)
+            even = take()
+            odd = take() if size > TE else None
+            group.append(Region(even, odd, size, size))
+        regions.append(group)
+    slopes = [take() for _ in range(tiles)]
+
+    copies = [
+        kernel_copies(first_kernel, weights[0], sems[0], False),
+        kernel_copies(second_kernel, weights[1], sems[1], False),
+        kernel_copies(second_kernel, weights[2], sems[2], True),
+        kernel_copies(first_kernel, weights[3], sems[3], True),
+    ]
+    for group in copies:
+        for copy in group:
+            copy.start()
+    for at in range(4):
+        clear_unused(weights[at], at > 1)
+
+    me = depth_at[0]
+    slots = [me ^ block for block in range(block_count)]
+    voxels = TE * TE * TE
+    volume[...] = jnp.zeros_like(volume)
+    upstream[...] = jnp.zeros_like(upstream)
+    mask[...] = jnp.zeros_like(mask)
+    face, thin = voxels // 2, voxels // 4
+    rim_size = face + thin + 16
+    for cls, raw, offset, y_first in ((0, rims, 0, 0), (2, rims, rim_size, HALO + TE)):
+        place_slots(slots, codes, (raw, offset, HALO, y_first, HALO, cls, lifted), volume, mask)
+        place_slots(slots, codes, (raw, offset + face, 2, y_first if cls else 2, 2, cls, lifted), upstream, None)
+    place_slots(slots, codes, (own, 0, TE, HALO, TE, 1, lifted), volume, mask)
+    place_slots(slots, codes, (own, voxels, TE, HALO, TE, 1, lifted), upstream, None)
+
+    starts = []
+    alive = []
+    for number in range(tiles):
+        slot = slots[2 * number]
+        starts.append(codes[3, slot] * TE)
+        alive.append((codes[1, slot] > 0).astype(F32))
+
+    for number in range(tiles):
+        source = regions[number][0]
+        z_first = starts[number] + number
+
+        @pl.loop(0, source.y_size // 2)
+        def _(pair):
+            for parity in range(2):
+                source.store_row(pair, parity, volume[pl.ds(z_first, source.z_size), number + 2 * pair + parity])
+
+    def finish_layer(number, layer, kind):
+        region = regions[number][layer]
+        inset = number + layer
+        z_first = starts[number] + inset
+        q_size = region.z_size // 2
+
+        @pl.loop(0, region.y_size // 2)
+        def _(pair):
+            for parity in range(2):
+                y_at = inset + 2 * pair + parity
+                side = (y_at >= HALO).astype(jnp.int32) + (y_at >= HALO + TE).astype(jnp.int32)
+                window = pl.ds(z_first, region.z_size)
+                keep = mask[side, window]
+                value = result[0:q_size, pair, :, parity * channels : (parity + 1) * channels]
+                value = value.reshape(keep.shape)
+                if kind == "act":
+                    out, slope = gelu_pair(value)
+                    slopes[number][:, pair, parity] = slope * keep
+                    out = out * keep
+                elif kind == "delta_two":
+                    out = upstream[window, y_at] * gelu_slope(value) * keep
+                else:
+                    out = value * slopes[number][2 : 2 + region.z_size, pair + 1, parity]
+                region.store_row(pair, parity, out)
+
+    def wait(at):
+        for copy in copies[at]:
+            copy.wait()
+
+    def kernel_gradient(at, left, delta):
+        flipped = []
+        for number in range(tiles):
+            region = regions[number][delta]
+            inset = (region.z_size - TE) // 2
+            rows = region.tile_rows(inset, inset, channels, channels, TE).astype(F32) * (alive[number] * (1.0 / voxels))
+            flipped.append(rows.T.astype(BF))
+        flipped = jnp.concatenate(flipped, axis=1)
+        for z_tap in range(3):
+            columns = []
+            for number in range(tiles):
+                region = regions[number][left]
+                inset = (region.z_size - TE) // 2 - 1
+                shifted = [
+                    region.tile_rows(inset + z_tap, inset + y_tap, 3 * channels, 0, TE) for y_tap in range(3)
+                ]
+                columns.append(jnp.concatenate(shifted, axis=1))
+            product = jnp.dot(flipped, jnp.concatenate(columns, axis=0), preferred_element_type=F32)
+            for y_tap in range(3):
+                for x_tap in range(3):
+                    lane = (y_tap * 3 + x_tap) * channels
+                    row = (z_tap * 9 + x_tap * 3 + y_tap) * channels
+                    grad_rows[row : row + channels] = product[:, lane : lane + channels].T
+        share = 27 * channels // grads.shape[1]
+        padded = grads.shape[2]
+        for part in range(grads.shape[1]):
+            grads[at, part] = grad_rows[part * share : part * share + padded].astype(BF)
+
+    grad_rows[27 * channels :] = jnp.zeros_like(grad_rows[27 * channels :])
+    wait(0)
+    for number in range(tiles):
+        convolve_region(regions[number][0], weights[0], False, result)
+        finish_layer(number, 1, "act")
+    wait(1)
+    for number in range(tiles):
+        convolve_region(regions[number][1], weights[1], False, result)
+        finish_layer(number, 2, "delta_two")
+    kernel_gradient(1, 1, 2)
+    wait(2)
+    for number in range(tiles):
+        convolve_region(regions[number][2], weights[2], True, result)
+        finish_layer(number, 3, "delta_one")
+    kernel_gradient(0, 0, 3)
+    wait(3)
+    convolve_region(regions[0][3], weights[3], True, result)
+    for pair in range(TE // 2):
+        for parity in range(2):
+            value = result[0 : TE // 2, pair, :, parity * channels : (parity + 1) * channels] * alive[0]
+            value = value.reshape(TE, TE, channels)
+            for z_at in range(TE):
+                lifted[pl.ds(z_at * TE * TE + 2 * pair + parity, TE, stride=TE)] = value[z_at]
+    input_grad[...] = lifted[...].astype(BF)
+
+
+def backward_call(own, rims, first_kernel, second_kernel, codes, depth_at, shares, tiles):
+    channels = first_kernel.shape[-1]
+    voxels = TE * TE * TE
+    positions = codes.shape[1]
+    planes = positions * TE + 2 * HALO
+    span = TE + 2 * HALO
+    inner = span // 2 - 1
+    padded = -(-(27 * channels // shares) // 16) * 16
+    scratch = [
+        pltpu.VMEM((planes, span, TE, channels), F32),
+        pltpu.VMEM((planes, span, TE, channels), F32),
+        pltpu.VMEM((3, planes, TE, channels), F32),
+        pltpu.VMEM((voxels, channels), F32),
+        pltpu.VMEM((inner, inner, 2 * TE, 2 * channels), F32),
+        pltpu.VMEM((27 * channels + 16, channels), F32),
+    ]
+    scratch += [pltpu.VMEM((36 * channels, 2 * channels), BF)] * 2
+    scratch += [pltpu.VMEM((2 * channels, 36 * channels), BF)] * 2
+    scratch += [pltpu.SemaphoreType.DMA((54,))] * 4
+    for number in range(tiles):
+        for layer in range(4):
+            size = span - 2 * (number + layer)
+            scratch += region_shapes(size, size, TE, channels, size > TE)
+    for number in range(tiles):
+        size = span - 2 * (number + 1)
+        scratch.append(pltpu.VMEM((size, size // 2, 2, TE, channels), F32))
+    vmem = pl.BlockSpec(memory_space=pltpu.VMEM)
+    smem = pl.BlockSpec(memory_space=pltpu.SMEM)
+    hbm = pl.BlockSpec(memory_space=pl.ANY)
+
+    def body(codes_ref, depth_ref, *refs):
+        backward_kernel(len(own), 0, channels, tiles, codes_ref, depth_ref, *refs)
+
+    return pl.pallas_call(
+        body,
+        out_shape=[
+            jax.ShapeDtypeStruct((voxels, channels), BF),
+            jax.ShapeDtypeStruct((2, shares, padded, channels), BF),
+        ],
+        in_specs=[smem, smem] + [vmem] * (2 * len(own)) + [hbm, hbm],
+        out_specs=[vmem, vmem],
+        scratch_shapes=scratch,
+        compiler_params=pltpu.CompilerParams(vmem_limit_bytes=60 * 1024 * 1024),
+        name="tile_backward",
+    )(codes, depth_at, *own, *rims, first_kernel, second_kernel)
+
+
+def on_device_line(features, cotangent, first_kernel, second_kernel, slot_tile, slot_used):
+    voxels, channels = features.shape[2:]
+    depth_size, space_size = lax.axis_size("depth"), lax.axis_size("space")
+    depth_at, space_at = lax.axis_index("depth"), lax.axis_index("space")
+    feature_rows, upstream_rows = features[0, 0], cotangent[0, 0]
+    own_code = jnp.where(slot_used[0] == 1, slot_tile[0] + 1, 0)
+
+    code_rows = jnp.pad(own_code, (0, 16 - own_code.shape[0])).astype(BF)
+    code_rows = jnp.broadcast_to(code_rows[:, None], (16, channels))
+    feature_box = feature_rows.reshape(TE, TE, TE, channels)
+    upstream_box = upstream_rows.reshape(TE, TE, TE, channels)
+
+    def side(feature_part, upstream_part):
+        return jnp.concatenate(
+            [feature_part.reshape(-1, channels), upstream_part.reshape(-1, channels), code_rows], axis=0
+        )
+
+    from_below = from_behind(side(feature_box[:, :, TE - HALO :], upstream_box[:, :, TE - 2 :]), "space", 1)
+    from_above = from_behind(side(feature_box[:, :, :HALO], upstream_box[:, :, :2]), "space", -1)
+    own = jnp.concatenate([feature_rows, upstream_rows], axis=0)
+    rim = jnp.concatenate([from_below, from_above], axis=0)
+    rim_size = rim.shape[0] // 2
+
+    def swap(block, bit):
+        return lax.ppermute(block, "depth", [(i, i ^ bit) for i in range(depth_size)])
+
+    own_far, rim_far = swap(own, 2), swap(rim, 2)
+    own_blocks = [own, swap(own, 1), own_far, swap(own_far, 1)]
+    rim_blocks = [rim, swap(rim, 1), rim_far, swap(rim_far, 1)]
+
+    def side_code(first):
+        return rim[first : first + own_code.shape[0], 0].astype(jnp.int32)
+
+    codes = jnp.stack([side_code(rim_size - 16), own_code, side_code(2 * rim_size - 16), slot_tile[0]])
+    shares = depth_size * space_size
+    input_grad, grads = backward_call(
+        own_blocks,
+        rim_blocks,
+        first_kernel,
+        second_kernel,
+        codes,
+        depth_at.reshape(1),
+        shares,
+        2,
+    )
+    share = 27 * channels // shares
+    by_owner = grads.reshape(2, space_size, depth_size, grads.shape[2], channels)
+
+    def for_depth(owner):
+        return lax.dynamic_index_in_dim(by_owner, owner, 2, keepdims=False)
+
+    summed = for_depth(depth_at).astype(F32) + swap(for_depth(depth_at ^ 1), 1).astype(F32)
+    parts = lax.all_to_all(summed.astype(BF), "space", 1, 1, tiled=True)
+    total = jnp.sum(parts.astype(F32), axis=1)[:, :share]
+    first_share, second_share = total[0].reshape(-1), total[1].reshape(-1)
+    return (input_grad.reshape(features.shape), first_share, second_share)
+
+
 def solution(mesh):
+    line = mesh.shape["space"] == GY and mesh.shape["depth"] == 4
+    run = on_device_line if line else on_device_wide
     return jax.shard_map(
-        on_device,
+        run,
         mesh=mesh,
         in_specs=(
             P("space", "depth", None, None),

time: 276 us -> 79.7 us (0.29)
  waiting for transfers between devices: 159 us -> 9.95 us
  Pallas kernels: 0 us -> 29.8 us
  starting transfers between devices: 28.9 us -> 10.4 us
  matrix products: 16.9 us -> 0 us
  between operations: 17.1 us -> 0.76 us
  local copies, waits for them, and re-layouts: 15.1 us -> 4.83 us
  blocking collectives: 28.8 us -> 20.2 us
  other arithmetic: 9.62 us -> 3.46 us
    unnamed x2 -> x0, waiting for transfers between devices: 135 us -> none
    pallas_call x0 -> x1, Pallas kernels: none -> 29.8 us  [backward_call(): pl.pallas_call(body, out_shape=[jax.ShapeDtypeStruct((voxels, channels),...]
    all_gather x4 -> x0, blocking collectives: 28.8 us -> none  [dense_column(): lax.all_gather(tile_rows, 'depth', axis=0, tiled=True)]
    ppermute x16 -> x2, starting transfers between devices: 28.9 us -> 6.17 us  [from_behind(): return lax.ppermute(block, axis, route)]
    ppermute x16 -> x2, waiting for transfers between devices: 23.6 us -> 2.68 us  [from_behind(): return lax.ppermute(block, axis, route)]
    all_to_all x0 -> x1, blocking collectives: none -> 20.2 us  [on_device_line(): parts = lax.all_to_all(summed.astype(BF), 'space', 1, 1, tiled=True)]
    dot_general x10 -> x0, matrix products: 16.9 us -> none  [the longest x2 5.5 us: tile_sum(): lax.dot_general(columns, delta, (((0,), (0,)), ((), ())), preferred_eleme...]
    unnamed x146 -> x17, local copies, waits for them, and re-layouts: 13.9 us -> 0.83 us
  transfers between devices with their start and end apart: 17 -> 9, of which waited for: 8 -> 5; matrix products, arithmetic and copies ran while one was open for 6% -> 3% of each run, Pallas kernels for 0% -> 0%
where the time goes in v1:
time: 79.7 us; the launch traced here: 79.4 us
  Pallas kernels  29.8 us (37%)
  blocking collectives  20.2 us (25%)
  starting transfers between devices  10.4 us (13%)
  waiting for transfers between devices  9.95 us (12%)
  local copies, waits for them, and re-layouts  4.83 us (6%)
  other arithmetic  3.46 us (4%)
    pallas_call x1, Pallas kernels, backward_call(): pl.pallas_call(body, out_shape=[jax.ShapeDtypeStruct((voxels, channels),...  29.8 us
    all_to_all x1, blocking collectives, on_device_line(): parts = lax.all_to_all(summed.astype(BF), 'space', 1, 1, tiled=True)  20.2 us
    ppermute x7, waiting for transfers between devices, swap(): lax.ppermute(block, 'depth', [(i, i ^ bit) for i in range(depth_size)])  7.27 us
    ppermute x2, starting transfers between devices, from_behind(): return lax.ppermute(block, axis, route)  6.17 us
    ppermute x7, starting transfers between devices, swap(): lax.ppermute(block, 'depth', [(i, i ^ bit) for i in range(depth_size)])  4.2 us
    ppermute x2, waiting for transfers between devices, from_behind(): return lax.ppermute(block, axis, route)  2.68 us
  transfers between devices with their start and end apart: 9, of which 5 were waited for; matrix products, arithmetic and copies ran while one was open for 3% of the time, Pallas kernels for 0%

profile of v1, /device:TPU:0, one launch (start us, length us, event | category | flops | bytes accessed | tf_op | source)
XLA Modules:
  0.0 79.4 jit_solution(17827637762324442817)
XLA Ops:
  0.6 1.0 %fusion.2 = (bf16[8,8,4,128]{3,2,1,0:T(4,128)(2,1)S(1)}, bf16[8,8,4,128]{3,2,1,0:T(4,128)(2,1)S(1)}) fusion(bf16[8,8,8,128]{3,2,1,0:T(8,128)(2,1)} %bitcast.27), kind=kLoop, calls=%fused_computation.21 | loop fusion | bytes 262144 | tf_op jit(solution)/shard_map/slice | solution.py:482
  1.7 1.0 %fusion.3 = (bf16[8,8,2,128]{3,2,1,0:T(2,128)(2,1)S(1)}, bf16[8,8,2,128]{3,2,1,0:T(2,128)(2,1)S(1)}) fusion(bf16[8,8,8,128]{3,2,1,0:T(8,128)(2,1)} %bitcast.31), kind=kLoop, calls=%fused_computation.22 | loop fusion | bytes 131072 | tf_op jit(solution)/shard_map/slice | solution.py:482
  2.7 0.7 convert_bitcast_fusion
  3.4 0.1 maximum_maximum_fusion
  3.5 4.9 %collective-permute-start = (bf16[400,128]{1,0:T(8,128)(2,1)S(1)}, bf16[400,128]{1,0:T(8,128)(2,1)S(1)}, u32[]{:S(2)}, u32[]{:S(2)}) collective-permute-start(bf16[400,128]{1,0:T(8,128)(2,1)S(1)} %get-tuple-element.17), channel_id=1, source_target_pairs={{0,4},{4,8},{8,12},{12,16},{16,20},{20,24},{24,28},{1,5},{5,9},{9,... | collective-permute-start | bytes 307208 | tf_op jit(solution)/shard_map/ppermute | solution.py:19
  8.4 1.3 %collective-permute-start.1 = (bf16[400,128]{1,0:T(8,128)(2,1)S(1)}, bf16[400,128]{1,0:T(8,128)(2,1)S(1)}, u32[]{:S(2)}, u32[]{:S(2)}) collective-permute-start(bf16[400,128]{1,0:T(8,128)(2,1)S(1)} %get-tuple-element.18), channel_id=1, source_target_pairs={{4,0},{8,4},{12,8},{16,12},{20,16},{24,20},{28,24},{5,1},{9,5},{13... | collective-permute-start | bytes 307208 | tf_op jit(solution)/shard_map/ppermute | solution.py:19
  9.7 1.0 %pad_maximum_fusion.refs_0_ = bf16[1024,128]{1,0:T(8,128)(2,1)S(1)} fusion(bf16[512,128]{1,0:T(8,128)(2,1)} %bitcast.32, bf16[512,128]{1,0:T(8,128)(2,1)} %bitcast.28), kind=kLoop, calls=%fused_computation.5 | loop fusion | flops 524288 | bytes 524288 | tf_op jit(solution)/shard_map/concatenate | solution.py:484
  10.7 0.0 copy-start
  10.7 1.6 %collective-permute-start.3 = (bf16[1024,128]{1,0:T(8,128)(2,1)S(1)}, bf16[1024,128]{1,0:T(8,128)(2,1)S(1)}, u32[]{:S(2)}, u32[]{:S(2)}) collective-permute-start(bf16[1024,128]{1,0:T(8,128)(2,1)S(1)} %pad_maximum_fusion.refs_0_), channel_id=1, source_target_pairs={{0,2},{1,3},{2,0},{3,1},{4,6},{5,7},{6,4},{7,5},{8,10},{9,11},{10,... | collective-permute-start | bytes 786440 | tf_op jit(solution)/shard_map/ppermute | solution.py:489
  12.3 0.0 collective-permute-done
  12.3 2.7 %collective-permute-done.1 = bf16[400,128]{1,0:T(8,128)(2,1)S(1)} collective-permute-done((bf16[400,128]{1,0:T(8,128)(2,1)S(1)}, bf16[400,128]{1,0:T(8,128)(2,1)S(1)}, u32[]{:S(2)}, u32[]{:S(2)}) %collective-permute-start.1) | collective-permute-done | bytes 102432 | tf_op jit(solution)/shard_map/ppermute | solution.py:19
  15.0 0.0 copy-start.1
  15.0 1.6 %collective-permute-start.6 = (bf16[800,128]{1,0:T(8,128)(2,1)S(1)}, bf16[800,128]{1,0:T(8,128)(2,1)S(1)}, u32[]{:S(2)}, u32[]{:S(2)}) collective-permute-start(bf16[800,128]{1,0:T(8,128)(2,1)S(1)} %constant_dynamic-update-slice_fusion.refs_4_), channel_id=1, source_target_pairs={{0,2},{1,3},{2,0},{3,1},{4,6},{5,7},{6,4},{7,5},{8,10},{9,11},{10,... | collective-permute-start | bytes 614408 | tf_op jit(solution)/shard_map/ppermute | solution.py:489
  16.6 0.0 collective-permute-start.2
  16.6 0.5 collective-permute-start.5
  17.1 2.9 %collective-permute-done.3.refs_2_ = bf16[1024,128]{1,0:T(8,128)(2,1)S(1)} collective-permute-done((bf16[1024,128]{1,0:T(8,128)(2,1)S(1)}, bf16[1024,128]{1,0:T(8,128)(2,1)S(1)}, u32[]{:S(2)}, u32[]{:S(2)}) %collective-permute-start.3) | collective-permute-done | bytes 262176 | tf_op jit(solution)/shard_map/ppermute | solution.py:489
  20.0 0.0 copy-start.2
  20.0 0.0 collective-permute-start.4
  20.0 0.1 convert_reduce_fusion.2
  20.1 2.8 %collective-permute-done.6.refs_6_ = bf16[800,128]{1,0:T(8,128)(2,1)S(1)} collective-permute-done((bf16[800,128]{1,0:T(8,128)(2,1)S(1)}, bf16[800,128]{1,0:T(8,128)(2,1)S(1)}, u32[]{:S(2)}, u32[]{:S(2)}) %collective-permute-start.6) | collective-permute-done | bytes 204832 | tf_op jit(solution)/shard_map/ppermute | solution.py:489
  22.9 0.0 copy-start.5
  22.9 0.0 collective-permute-start.7
  22.9 0.1 convert_reduce_fusion.1
  23.1 1.2 %pad_add_fusion.codes_ref = s32[4,4]{1,0:T(4,128)} fusion(s32[1,4]{1,0:T(1,128)} %param.10, s32[1,4]{1,0:T(1,128)S(1)} %bitcast.38, s32[1,4]{1,0:T(1,128)S(1)} %get-tuple-element.8, s32[1,4]{1,0:T(1,128)S(1)} %bitcast.37), kind=kLoop, calls=%fused_computation.13 | loop fusion | flops 48 | bytes 128 | tf_op jit(solution)/shard_map/stack | solution.py:498
  24.3 0.0 collective-permute-done.2.refs_1_
  24.3 0.0 copy-start.3
  24.3 0.0 collective-permute-done.5.refs_5_
  24.3 0.0 copy-start.6
  24.3 0.1 collective-permute-done.7.refs_7_
  24.4 0.0 copy-start.7
  24.4 0.0 collective-permute-done.4.refs_3_
  24.4 0.0 copy-start.4
  24.4 0.0 copy-done
  24.4 0.0 copy-done.1
  24.4 0.0 copy-done.2
  24.4 0.0 copy-done.5
  24.4 0.6 copy-done.3
  25.0 0.1 copy-done.6
  25.1 0.1 copy-done.7
  25.1 0.1 copy-done.4
  25.2 29.8 %tile_backward.1 = (bf16[512,128]{1,0:T(8,128)(2,1)}, bf16[2,32,112,128]{3,2,1,0:T(8,128)(2,1)}) custom-call(s32[4,4]{1,0:T(4,128)} %pad_add_fusion.codes_ref, s32[1]{0:T(128)} %bitcast.7.depth_ref, bf16[1024,128]{1,0:T(8,128)(2,1)} %copy-done, bf16[1024,128]{1,0:T(8,128)(2,1)} %copy-done.3, bf16[1024,128]{1,0:T(8,128)(2,1)} %copy-done.2, ...), custom_call_target="tpu_custom_call" | custom-call | tf_op jit(solution)/shard_map/tile_backward/pallas_call | solution.py:451
  55.1 1.2 %constant_dynamic-slice_fusion.1 = (bf16[2,8,1,112,128]{4,3,2,1,0:T(8,128)(2,1)S(1)}, bf16[2,8,1,112,128]{4,3,2,1,0:T(8,128)(2,1)S(1)}) fusion(bf16[2,8,4,112,128]{4,3,2,1,0:T(8,128)(2,1)} %bitcast.29, s32[]{:T(128)S(6)} %select_n.17, s32[]{:T(128)S(6)} %select_n.18), kind=kLoop, calls=%fused_computation.20 | loop fusion | bytes 1835016 | tf_op jit(solution)/shard_map/jit(dynamic_index_in_dim)/dynamic_slice | solution.py:514
  56.4 0.6 collective-permute-start.8
  56.9 1.4 %collective-permute-done.8 = bf16[2,8,112,128]{3,2,0,1:T(8,128)(2,1)S(1)} collective-permute-done((bf16[2,8,112,128]{3,2,0,1:T(8,128)(2,1)S(1)}, bf16[2,8,112,128]{3,2,0,1:T(8,128)(2,1)S(1)}, u32[]{:S(2)}, u32[]{:S(2)}) %collective-permute-start.8) | collective-permute-done | bytes 458784 | tf_op jit(solution)/shard_map/ppermute | solution.py:489
  58.4 0.1 fusion
  58.5 20.2 %all_to_all.5 = bf16[2,8,112,128]{3,2,0,1:T(8,128)(2,1)S(1)} all-to-all(bf16[2,8,112,128]{3,2,0,1:T(8,128)(2,1)S(1)} %fusion), channel_id=1, replica_groups=mesh['space'=8,'depth'=4] {'space'}, dimensions={1} | all-to-all | bytes 917504 | tf_op jit(solution)/shard_map/all_to_all | solution.py:517
  78.7 0.1 convert_reduce_fusion
  78.8 0.6 slice_bitcast_fusion
  (4 shorter events, 0.1 us)
Async XLA Ops:
  3.5 8.7 %collective-permute-start = (bf16[400,128]{1,0:T(8,128)(2,1)S(1)}, bf16[400,128]{1,0:T(8,128)(2,1)S(1)}, u32[]{:S(2)}, u32[]{:S(2)}) collective-permute-start(bf16[400,128]{1,0:T(8,128)(2,1)S(1)} %get-tuple-element.17), channel_id=1, source_target_pairs={{0,4},{4,8},{8,12},{12,16},{16,20},{20,24},{24,28},{1,5},{5,9},{9,... | collective-permute-start | bytes 307208 | tf_op jit(solution)/shard_map/ppermute | solution.py:19
  8.4 6.6 %collective-permute-start.1 = (bf16[400,128]{1,0:T(8,128)(2,1)S(1)}, bf16[400,128]{1,0:T(8,128)(2,1)S(1)}, u32[]{:S(2)}, u32[]{:S(2)}) collective-permute-start(bf16[400,128]{1,0:T(8,128)(2,1)S(1)} %get-tuple-element.18), channel_id=1, source_target_pairs={{4,0},{8,4},{12,8},{16,12},{20,16},{24,20},{28,24},{5,1},{9,5},{13... | collective-permute-start | bytes 307208 | tf_op jit(solution)/shard_map/ppermute | solution.py:19
  10.7 13.7 %copy-start = (bf16[1024,128]{1,0:T(8,128)(2,1)}, bf16[1024,128]{1,0:T(8,128)(2,1)S(1)}, u32[]{:S(2)}) copy-start(bf16[1024,128]{1,0:T(8,128)(2,1)S(1)} %pad_maximum_fusion.refs_0_) | copy-start | bytes 786436
  10.7 9.3 %collective-permute-start.3 = (bf16[1024,128]{1,0:T(8,128)(2,1)S(1)}, bf16[1024,128]{1,0:T(8,128)(2,1)S(1)}, u32[]{:S(2)}, u32[]{:S(2)}) collective-permute-start(bf16[1024,128]{1,0:T(8,128)(2,1)S(1)} %pad_maximum_fusion.refs_0_), channel_id=1, source_target_pairs={{0,2},{1,3},{2,0},{3,1},{4,6},{5,7},{6,4},{7,5},{8,10},{9,11},{10,... | collective-permute-start | bytes 786440 | tf_op jit(solution)/shard_map/ppermute | solution.py:489
  15.0 9.4 %copy-start.1 = (bf16[800,128]{1,0:T(8,128)(2,1)}, bf16[800,128]{1,0:T(8,128)(2,1)S(1)}, u32[]{:S(2)}) copy-start(bf16[800,128]{1,0:T(8,128)(2,1)S(1)} %constant_dynamic-update-slice_fusion.refs_4_) | copy-start | bytes 614404
  15.0 7.9 %collective-permute-start.6 = (bf16[800,128]{1,0:T(8,128)(2,1)S(1)}, bf16[800,128]{1,0:T(8,128)(2,1)S(1)}, u32[]{:S(2)}, u32[]{:S(2)}) collective-permute-start(bf16[800,128]{1,0:T(8,128)(2,1)S(1)} %constant_dynamic-update-slice_fusion.refs_4_), channel_id=1, source_target_pairs={{0,2},{1,3},{2,0},{3,1},{4,6},{5,7},{6,4},{7,5},{8,10},{9,11},{10,... | collective-permute-start | bytes 614408 | tf_op jit(solution)/shard_map/ppermute | solution.py:489
  16.6 7.8 %collective-permute-start.2 = (bf16[1024,128]{1,0:T(8,128)(2,1)S(1)}, bf16[1024,128]{1,0:T(8,128)(2,1)S(1)}, u32[]{:S(2)}, u32[]{:S(2)}) collective-permute-start(bf16[1024,128]{1,0:T(8,128)(2,1)S(1)} %pad_maximum_fusion.refs_0_), channel_id=1, source_target_pairs={{0,1},{1,0},{2,3},{3,2},{4,5},{5,4},{6,7},{7,6},{8,9},{9,8},{10,11... | collective-permute-start | bytes 786440 | tf_op jit(solution)/shard_map/ppermute | solution.py:489
  16.6 7.8 %collective-permute-start.5 = (bf16[800,128]{1,0:T(8,128)(2,1)S(1)}, bf16[800,128]{1,0:T(8,128)(2,1)S(1)}, u32[]{:S(2)}, u32[]{:S(2)}) collective-permute-start(bf16[800,128]{1,0:T(8,128)(2,1)S(1)} %constant_dynamic-update-slice_fusion.refs_4_), channel_id=1, source_target_pairs={{0,1},{1,0},{2,3},{3,2},{4,5},{5,4},{6,7},{7,6},{8,9},{9,8},{10,11... | collective-permute-start | bytes 614408 | tf_op jit(solution)/shard_map/ppermute | solution.py:489
  20.0 4.4 %copy-start.2 = (bf16[1024,128]{1,0:T(8,128)(2,1)}, bf16[1024,128]{1,0:T(8,128)(2,1)S(1)}, u32[]{:S(2)}) copy-start(bf16[1024,128]{1,0:T(8,128)(2,1)S(1)} %collective-permute-done.3.refs_2_) | copy-start | bytes 786436
  20.0 4.4 %collective-permute-start.4 = (bf16[1024,128]{1,0:T(8,128)(2,1)S(1)}, bf16[1024,128]{1,0:T(8,128)(2,1)S(1)}, u32[]{:S(2)}, u32[]{:S(2)}) collective-permute-start(bf16[1024,128]{1,0:T(8,128)(2,1)S(1)} %collective-permute-done.3.refs_2_), channel_id=1, source_target_pairs={{0,1},{1,0},{2,3},{3,2},{4,5},{5,4},{6,7},{7,6},{8,9},{9,8},{10,11... | collective-permute-start | bytes 786440 | tf_op jit(solution)/shard_map/ppermute | solution.py:489
  22.9 1.5 %copy-start.5 = (bf16[800,128]{1,0:T(8,128)(2,1)}, bf16[800,128]{1,0:T(8,128)(2,1)S(1)}, u32[]{:S(2)}) copy-start(bf16[800,128]{1,0:T(8,128)(2,1)S(1)} %collective-permute-done.6.refs_6_) | copy-start | bytes 614404
  22.9 1.5 %collective-permute-start.7 = (bf16[800,128]{1,0:T(8,128)(2,1)S(1)}, bf16[800,128]{1,0:T(8,128)(2,1)S(1)}, u32[]{:S(2)}, u32[]{:S(2)}) collective-permute-start(bf16[800,128]{1,0:T(8,128)(2,1)S(1)} %collective-permute-done.6.refs_6_), channel_id=1, source_target_pairs={{0,1},{1,0},{2,3},{3,2},{4,5},{5,4},{6,7},{7,6},{8,9},{9,8},{10,11... | collective-permute-start | bytes 614408 | tf_op jit(solution)/shard_map/ppermute | solution.py:489
  24.3 0.7 copy-start.3
  24.3 0.8 copy-start.6
  24.4 0.8 copy-start.7
  24.4 0.8 %copy-start.4 = (bf16[1024,128]{1,0:T(8,128)(2,1)}, bf16[1024,128]{1,0:T(8,128)(2,1)S(1)}, u32[]{:S(2)}) copy-start(bf16[1024,128]{1,0:T(8,128)(2,1)S(1)} %collective-permute-done.4.refs_3_) | copy-start | bytes 786436
  56.4 2.0 %collective-permute-start.8 = (bf16[2,8,112,128]{3,2,0,1:T(8,128)(2,1)S(1)}, bf16[2,8,112,128]{3,2,0,1:T(8,128)(2,1)S(1)}, u32[]{:S(2)}, u32[]{:S(2)}) collective-permute-start(bf16[2,8,112,128]{3,2,0,1:T(8,128)(2,1)S(1)} %bitcast.30), channel_id=1, source_target_pairs={{0,1},{1,0},{2,3},{3,2},{4,5},{5,4},{6,7},{7,6},{8,9},{9,8},{10,11... | collective-permute-start | bytes 1376264 | tf_op jit(solution)/shard_map/ppermute | solution.py:489

commit v2 on v1

--- a/solution.py
+++ b/solution.py
@@ -196,56 +196,56 @@
     q_size, r_size = region.z_size // 2 - 1, region.y_size // 2 - 1
     channels = region.even.shape[-1] // 3
     pieces = []
-    for z_tap in range(3):
+    for block in range(9):
+        z_tap, x_tap = block // 3, block % 3
+        if transposed:
+            z_tap, x_tap = 2 - z_tap, 2 - x_tap
         ref, q_first = region.planes(z_tap)
-        for x_tap in range(3):
-            for y_at in range(4):
-                piece = ref[
-                    q_first : q_first + q_size,
-                    y_at // 2 : y_at // 2 + r_size,
-                    y_at % 2,
-                    :,
-                    x_tap * channels : (x_tap + 1) * channels,
-                ]
-                pieces.append(piece.reshape(-1, channels))
+        for y_at in range(4):
+            if transposed:
+                y_at = 3 - y_at
+            piece = ref[
+                q_first : q_first + q_size,
+                y_at // 2 : y_at // 2 + r_size,
+                y_at % 2,
+                :,
+                x_tap * channels : (x_tap + 1) * channels,
+            ]
+            pieces.append(piece.reshape(-1, channels))
     left = jnp.concatenate(pieces, axis=1)
-    contract = (((1,), (1 if transposed else 0,)), ((), ()))
-    product = lax.dot_general(left, weights[...], contract, preferred_element_type=F32)
+    if transposed:
+        right = jnp.concatenate([weights[at // 4, at % 4] for at in range(36)], axis=1)
+        contract = (((1,), (1,)), ((), ()))
+    else:
+        right = weights[...].reshape(36 * channels, 2 * channels)
+        contract = (((1,), (0,)), ((), ()))
+    product = lax.dot_general(left, right, contract, preferred_element_type=F32)
     result[0:q_size, 0:r_size] = product.reshape(q_size, r_size, product.shape[0] // (q_size * r_size), -1)
 
 
 def kernel_copies(kernel, weights, sems, transposed):
     channels = kernel.shape[-1]
     copies = []
-    for z_tap in range(3):
-        for x_tap in range(3):
-            block = (z_tap * 3 + x_tap) * 4 * channels
-            for parity in range(2):
-                out = pl.ds(parity * channels, channels)
-                if transposed:
-                    for y_tap in range(3):
-                        tap = (2 - z_tap) * 9 + (2 - x_tap) * 3 + 2 - y_tap
-                        lanes = pl.ds(block + (parity + y_tap) * channels, channels)
-                        copies.append((kernel.at[tap], weights.at[out, lanes]))
-                else:
-                    tap = z_tap * 9 + x_tap * 3
-                    for y_tap in range(3):
-                        rows = pl.ds(block + (parity + y_tap) * channels, channels)
-                        copies.append((kernel.at[tap + y_tap], weights.at[rows, out]))
-    return [pltpu.make_async_copy(a, b, sems.at[n]) for n, (a, b) in enumerate(copies)]
+    for parity in range(2):
+        out = pl.ds(parity * channels, channels)
+        if transposed:
+            place = weights.at[:, pl.ds(1 - parity, 3), out, :]
+        else:
+            place = weights.at[:, pl.ds(parity, 3), :, out]
+        copies.append(pltpu.make_async_copy(kernel, place, sems.at[parity]))
+    return copies
 
 
 def clear_unused(weights, transposed):
-    channels = min(weights.shape) // 2
+    channels = min(weights.shape[2:])
     blank = jnp.zeros((channels, channels), BF)
     for block in range(9):
-        for parity, y_at in ((0, 3), (1, 0)):
-            inner = pl.ds((block * 4 + y_at) * channels, channels)
-            out = pl.ds(parity * channels, channels)
-            if transposed:
-                weights[out, inner] = blank
-            else:
-                weights[inner, out] = blank
+        if transposed:
+            weights[block, 0, 0:channels, :] = blank
+            weights[block, 3, channels:, :] = blank
+        else:
+            weights[block, 3, :, 0:channels] = blank
+            weights[block, 0, :, channels:] = blank
 
 
 def place_slots(slots, codes, sources, volume, mask):
@@ -327,8 +327,7 @@
         source = regions[number][0]
         z_first = starts[number] + number
 
-        @pl.loop(0, source.y_size // 2)
-        def _(pair):
+        for pair in range(source.y_size // 2):
             for parity in range(2):
                 source.store_row(pair, parity, volume[pl.ds(z_first, source.z_size), number + 2 * pair + parity])
 
@@ -338,11 +337,10 @@
         z_first = starts[number] + inset
         q_size = region.z_size // 2
 
-        @pl.loop(0, region.y_size // 2)
-        def _(pair):
+        for pair in range(region.y_size // 2):
             for parity in range(2):
                 y_at = inset + 2 * pair + parity
-                side = (y_at >= HALO).astype(jnp.int32) + (y_at >= HALO + TE).astype(jnp.int32)
+                side = (y_at >= HALO) + (y_at >= HALO + TE)
                 window = pl.ds(z_first, region.z_size)
                 keep = mask[side, window]
                 value = result[0:q_size, pair, :, parity * channels : (parity + 1) * channels]
@@ -431,9 +429,9 @@
         pltpu.VMEM((inner, inner, 2 * TE, 2 * channels), F32),
         pltpu.VMEM((27 * channels + 16, channels), F32),
     ]
-    scratch += [pltpu.VMEM((36 * channels, 2 * channels), BF)] * 2
-    scratch += [pltpu.VMEM((2 * channels, 36 * channels), BF)] * 2
-    scratch += [pltpu.SemaphoreType.DMA((54,))] * 4
+    scratch += [pltpu.VMEM((9, 4, channels, 2 * channels), BF)] * 2
+    scratch += [pltpu.VMEM((9, 4, 2 * channels, channels), BF)] * 2
+    scratch += [pltpu.SemaphoreType.DMA((2,))] * 4
     for number in range(tiles):
         for layer in range(4):
             size = span - 2 * (number + layer)
@@ -459,7 +457,7 @@
         scratch_shapes=scratch,
         compiler_params=pltpu.CompilerParams(vmem_limit_bytes=60 * 1024 * 1024),
         name="tile_backward",
-    )(codes, depth_at, *own, *rims, first_kernel, second_kernel)
+    )(codes, depth_at, *own, *rims, *(kernel.reshape(9, 3, channels, channels) for kernel in (first_kernel, second_kernel)))
 
 
 def on_device_line(features, cotangent, first_kernel, second_kernel, slot_tile, slot_used):

time: 79.7 us -> 69.4 us (0.87)
  Pallas kernels: 29.8 us -> 19.5 us
    pallas_call x1, Pallas kernels: 29.8 us -> 19.5 us  [backward_call(): pl.pallas_call(body, out_shape=[jax.ShapeDtypeStruct((voxels, channels),...]
  transfers between devices with their start and end apart: 9 -> 9, of which waited for: 5 -> 5; matrix products, arithmetic and copies ran while one was open for 3% -> 4% of each run, Pallas kernels for 0% -> 0%
where the time goes in v2:
time: 69.4 us; the launch traced here: 69.1 us
  blocking collectives  20.2 us (29%)
  Pallas kernels  19.5 us (28%)
  starting transfers between devices  10.4 us (15%)
  waiting for transfers between devices  9.95 us (14%)
  local copies, waits for them, and re-layouts  4.83 us (7%)
  other arithmetic  3.46 us (5%)
  between operations  0.76 us (1%)
    all_to_all x1, blocking collectives, on_device_line(): parts = lax.all_to_all(summed.astype(BF), 'space', 1, 1, tiled=True)  20.2 us
    pallas_call x1, Pallas kernels, backward_call(): pl.pallas_call(body, out_shape=[jax.ShapeDtypeStruct((voxels, channels),...  19.5 us
    ppermute x7, waiting for transfers between devices, swap(): lax.ppermute(block, 'depth', [(i, i ^ bit) for i in range(depth_size)])  7.27 us
    ppermute x2, starting transfers between devices, from_behind(): return lax.ppermute(block, axis, route)  6.17 us
    ppermute x7, starting transfers between devices, swap(): lax.ppermute(block, 'depth', [(i, i ^ bit) for i in range(depth_size)])  4.2 us
    ppermute x2, waiting for transfers between devices, from_behind(): return lax.ppermute(block, axis, route)  2.68 us
  transfers between devices with their start and end apart: 9, of which 5 were waited for; matrix products, arithmetic and copies ran while one was open for 4% of the time, Pallas kernels for 0%

profile of v2, /device:TPU:0, one launch (start us, length us, event | category | flops | bytes accessed | tf_op | source)
XLA Modules:
  0.0 69.1 jit_solution(16746534173061942842)
XLA Ops:
  0.6 1.0 %fusion.2 = (bf16[8,8,4,128]{3,2,1,0:T(4,128)(2,1)S(1)}, bf16[8,8,4,128]{3,2,1,0:T(4,128)(2,1)S(1)}) fusion(bf16[8,8,8,128]{3,2,1,0:T(8,128)(2,1)} %bitcast.31), kind=kLoop, calls=%fused_computation.21 | loop fusion | bytes 262144 | tf_op jit(solution)/shard_map/slice | solution.py:480
  1.7 1.0 %fusion.3 = (bf16[8,8,2,128]{3,2,1,0:T(2,128)(2,1)S(1)}, bf16[8,8,2,128]{3,2,1,0:T(2,128)(2,1)S(1)}) fusion(bf16[8,8,8,128]{3,2,1,0:T(8,128)(2,1)} %bitcast.35), kind=kLoop, calls=%fused_computation.22 | loop fusion | bytes 131072 | tf_op jit(solution)/shard_map/slice | solution.py:480
  2.7 0.7 convert_bitcast_fusion
  3.4 0.1 maximum_maximum_fusion
  3.5 4.9 %collective-permute-start = (bf16[400,128]{1,0:T(8,128)(2,1)S(1)}, bf16[400,128]{1,0:T(8,128)(2,1)S(1)}, u32[]{:S(2)}, u32[]{:S(2)}) collective-permute-start(bf16[400,128]{1,0:T(8,128)(2,1)S(1)} %get-tuple-element.17), channel_id=1, source_target_pairs={{0,4},{4,8},{8,12},{12,16},{16,20},{20,24},{24,28},{1,5},{5,9},{9,... | collective-permute-start | bytes 307208 | tf_op jit(solution)/shard_map/ppermute | solution.py:19
  8.4 1.3 %collective-permute-start.1 = (bf16[400,128]{1,0:T(8,128)(2,1)S(1)}, bf16[400,128]{1,0:T(8,128)(2,1)S(1)}, u32[]{:S(2)}, u32[]{:S(2)}) collective-permute-start(bf16[400,128]{1,0:T(8,128)(2,1)S(1)} %get-tuple-element.18), channel_id=1, source_target_pairs={{4,0},{8,4},{12,8},{16,12},{20,16},{24,20},{28,24},{5,1},{9,5},{13... | collective-permute-start | bytes 307208 | tf_op jit(solution)/shard_map/ppermute | solution.py:19
  9.7 1.0 %pad_maximum_fusion.refs_0_ = bf16[1024,128]{1,0:T(8,128)(2,1)S(1)} fusion(bf16[512,128]{1,0:T(8,128)(2,1)} %bitcast.36, bf16[512,128]{1,0:T(8,128)(2,1)} %bitcast.32), kind=kLoop, calls=%fused_computation.5 | loop fusion | flops 524288 | bytes 524288 | tf_op jit(solution)/shard_map/concatenate | solution.py:482
  10.7 0.0 copy-start
  10.7 1.6 %collective-permute-start.3 = (bf16[1024,128]{1,0:T(8,128)(2,1)S(1)}, bf16[1024,128]{1,0:T(8,128)(2,1)S(1)}, u32[]{:S(2)}, u32[]{:S(2)}) collective-permute-start(bf16[1024,128]{1,0:T(8,128)(2,1)S(1)} %pad_maximum_fusion.refs_0_), channel_id=1, source_target_pairs={{0,2},{1,3},{2,0},{3,1},{4,6},{5,7},{6,4},{7,5},{8,10},{9,11},{10,... | collective-permute-start | bytes 786440 | tf_op jit(solution)/shard_map/ppermute | solution.py:487
  12.3 0.0 collective-permute-done
  12.3 2.7 %collective-permute-done.1 = bf16[400,128]{1,0:T(8,128)(2,1)S(1)} collective-permute-done((bf16[400,128]{1,0:T(8,128)(2,1)S(1)}, bf16[400,128]{1,0:T(8,128)(2,1)S(1)}, u32[]{:S(2)}, u32[]{:S(2)}) %collective-permute-start.1) | collective-permute-done | bytes 102432 | tf_op jit(solution)/shard_map/ppermute | solution.py:19
  15.0 0.0 copy-start.1
  15.0 1.6 %collective-permute-start.6 = (bf16[800,128]{1,0:T(8,128)(2,1)S(1)}, bf16[800,128]{1,0:T(8,128)(2,1)S(1)}, u32[]{:S(2)}, u32[]{:S(2)}) collective-permute-start(bf16[800,128]{1,0:T(8,128)(2,1)S(1)} %constant_dynamic-update-slice_fusion.refs_4_), channel_id=1, source_target_pairs={{0,2},{1,3},{2,0},{3,1},{4,6},{5,7},{6,4},{7,5},{8,10},{9,11},{10,... | collective-permute-start | bytes 614408 | tf_op jit(solution)/shard_map/ppermute | solution.py:487
  16.6 0.0 collective-permute-start.2
  16.6 0.5 collective-permute-start.5
  17.1 2.9 %collective-permute-done.3.refs_2_ = bf16[1024,128]{1,0:T(8,128)(2,1)S(1)} collective-permute-done((bf16[1024,128]{1,0:T(8,128)(2,1)S(1)}, bf16[1024,128]{1,0:T(8,128)(2,1)S(1)}, u32[]{:S(2)}, u32[]{:S(2)}) %collective-permute-start.3) | collective-permute-done | bytes 262176 | tf_op jit(solution)/shard_map/ppermute | solution.py:487
  20.0 0.0 copy-start.2
  20.0 0.0 collective-permute-start.4
  20.0 0.1 convert_reduce_fusion.2
  20.1 2.8 %collective-permute-done.6.refs_6_ = bf16[800,128]{1,0:T(8,128)(2,1)S(1)} collective-permute-done((bf16[800,128]{1,0:T(8,128)(2,1)S(1)}, bf16[800,128]{1,0:T(8,128)(2,1)S(1)}, u32[]{:S(2)}, u32[]{:S(2)}) %collective-permute-start.6) | collective-permute-done | bytes 204832 | tf_op jit(solution)/shard_map/ppermute | solution.py:487
  22.9 0.0 copy-start.5
  22.9 0.0 collective-permute-start.7
  22.9 0.1 convert_reduce_fusion.1
  23.1 1.2 %pad_add_fusion.codes_ref = s32[4,4]{1,0:T(4,128)} fusion(s32[1,4]{1,0:T(1,128)} %param.10, s32[1,4]{1,0:T(1,128)S(1)} %bitcast.42, s32[1,4]{1,0:T(1,128)S(1)} %get-tuple-element.8, s32[1,4]{1,0:T(1,128)S(1)} %bitcast.41), kind=kLoop, calls=%fused_computation.13 | loop fusion | flops 48 | bytes 128 | tf_op jit(solution)/shard_map/stack | solution.py:496
  24.3 0.0 collective-permute-done.2.refs_1_
  24.3 0.0 copy-start.3
  24.3 0.0 collective-permute-done.5.refs_5_
  24.3 0.0 copy-start.6
  24.3 0.1 collective-permute-done.7.refs_7_
  24.4 0.0 copy-start.7
  24.4 0.0 collective-permute-done.4.refs_3_
  24.4 0.0 copy-start.4
  24.4 0.0 copy-done
  24.4 0.0 copy-done.1
  24.4 0.0 copy-done.2
  24.4 0.0 copy-done.5
  24.4 0.6 copy-done.3
  25.0 0.1 copy-done.6
  25.1 0.1 copy-done.7
  25.1 0.1 copy-done.4
  25.2 19.5 %tile_backward.1 = (bf16[512,128]{1,0:T(8,128)(2,1)}, bf16[2,32,112,128]{3,2,1,0:T(8,128)(2,1)}) custom-call(s32[4,4]{1,0:T(4,128)} %pad_add_fusion.codes_ref, s32[1]{0:T(128)} %bitcast.7.depth_ref, bf16[1024,128]{1,0:T(8,128)(2,1)} %copy-done, bf16[1024,128]{1,0:T(8,128)(2,1)} %copy-done.3, bf16[1024,128]{1,0:T(8,128)(2,1)} %copy-done.2, ...), custom_call_target="tpu_custom_call" | custom-call | tf_op jit(solution)/shard_map/tile_backward/pallas_call | solution.py:449
  44.8 1.2 %constant_dynamic-slice_fusion.1 = (bf16[2,8,1,112,128]{4,3,2,1,0:T(8,128)(2,1)S(1)}, bf16[2,8,1,112,128]{4,3,2,1,0:T(8,128)(2,1)S(1)}) fusion(bf16[2,8,4,112,128]{4,3,2,1,0:T(8,128)(2,1)} %bitcast.33, s32[]{:T(128)S(6)} %select_n.17, s32[]{:T(128)S(6)} %select_n.18), kind=kLoop, calls=%fused_computation.20 | loop fusion | bytes 1835016 | tf_op jit(solution)/shard_map/jit(dynamic_index_in_dim)/dynamic_slice | solution.py:512
  46.1 0.6 collective-permute-start.8
  46.6 1.4 %collective-permute-done.8 = bf16[2,8,112,128]{3,2,0,1:T(8,128)(2,1)S(1)} collective-permute-done((bf16[2,8,112,128]{3,2,0,1:T(8,128)(2,1)S(1)}, bf16[2,8,112,128]{3,2,0,1:T(8,128)(2,1)S(1)}, u32[]{:S(2)}, u32[]{:S(2)}) %collective-permute-start.8) | collective-permute-done | bytes 458784 | tf_op jit(solution)/shard_map/ppermute | solution.py:487
  48.1 0.1 fusion
  48.2 20.2 %all_to_all.5 = bf16[2,8,112,128]{3,2,0,1:T(8,128)(2,1)S(1)} all-to-all(bf16[2,8,112,128]{3,2,0,1:T(8,128)(2,1)S(1)} %fusion), channel_id=1, replica_groups=mesh['space'=8,'depth'=4] {'space'}, dimensions={1} | all-to-all | bytes 917504 | tf_op jit(solution)/shard_map/all_to_all | solution.py:515
  68.4 0.1 convert_reduce_fusion
  68.5 0.6 slice_bitcast_fusion
  (4 shorter events, 0.1 us)
Async XLA Ops:
  3.5 8.7 %collective-permute-start = (bf16[400,128]{1,0:T(8,128)(2,1)S(1)}, bf16[400,128]{1,0:T(8,128)(2,1)S(1)}, u32[]{:S(2)}, u32[]{:S(2)}) collective-permute-start(bf16[400,128]{1,0:T(8,128)(2,1)S(1)} %get-tuple-element.17), channel_id=1, source_target_pairs={{0,4},{4,8},{8,12},{12,16},{16,20},{20,24},{24,28},{1,5},{5,9},{9,... | collective-permute-start | bytes 307208 | tf_op jit(solution)/shard_map/ppermute | solution.py:19
  8.4 6.6 %collective-permute-start.1 = (bf16[400,128]{1,0:T(8,128)(2,1)S(1)}, bf16[400,128]{1,0:T(8,128)(2,1)S(1)}, u32[]{:S(2)}, u32[]{:S(2)}) collective-permute-start(bf16[400,128]{1,0:T(8,128)(2,1)S(1)} %get-tuple-element.18), channel_id=1, source_target_pairs={{4,0},{8,4},{12,8},{16,12},{20,16},{24,20},{28,24},{5,1},{9,5},{13... | collective-permute-start | bytes 307208 | tf_op jit(solution)/shard_map/ppermute | solution.py:19
  10.7 13.7 %copy-start = (bf16[1024,128]{1,0:T(8,128)(2,1)}, bf16[1024,128]{1,0:T(8,128)(2,1)S(1)}, u32[]{:S(2)}) copy-start(bf16[1024,128]{1,0:T(8,128)(2,1)S(1)} %pad_maximum_fusion.refs_0_) | copy-start | bytes 786436
  10.7 9.3 %collective-permute-start.3 = (bf16[1024,128]{1,0:T(8,128)(2,1)S(1)}, bf16[1024,128]{1,0:T(8,128)(2,1)S(1)}, u32[]{:S(2)}, u32[]{:S(2)}) collective-permute-start(bf16[1024,128]{1,0:T(8,128)(2,1)S(1)} %pad_maximum_fusion.refs_0_), channel_id=1, source_target_pairs={{0,2},{1,3},{2,0},{3,1},{4,6},{5,7},{6,4},{7,5},{8,10},{9,11},{10,... | collective-permute-start | bytes 786440 | tf_op jit(solution)/shard_map/ppermute | solution.py:487
  15.0 9.4 %copy-start.1 = (bf16[800,128]{1,0:T(8,128)(2,1)}, bf16[800,128]{1,0:T(8,128)(2,1)S(1)}, u32[]{:S(2)}) copy-start(bf16[800,128]{1,0:T(8,128)(2,1)S(1)} %constant_dynamic-update-slice_fusion.refs_4_) | copy-start | bytes 614404
  15.0 7.9 %collective-permute-start.6 = (bf16[800,128]{1,0:T(8,128)(2,1)S(1)}, bf16[800,128]{1,0:T(8,128)(2,1)S(1)}, u32[]{:S(2)}, u32[]{:S(2)}) collective-permute-start(bf16[800,128]{1,0:T(8,128)(2,1)S(1)} %constant_dynamic-update-slice_fusion.refs_4_), channel_id=1, source_target_pairs={{0,2},{1,3},{2,0},{3,1},{4,6},{5,7},{6,4},{7,5},{8,10},{9,11},{10,... | collective-permute-start | bytes 614408 | tf_op jit(solution)/shard_map/ppermute | solution.py:487
  16.6 7.8 %collective-permute-start.2 = (bf16[1024,128]{1,0:T(8,128)(2,1)S(1)}, bf16[1024,128]{1,0:T(8,128)(2,1)S(1)}, u32[]{:S(2)}, u32[]{:S(2)}) collective-permute-start(bf16[1024,128]{1,0:T(8,128)(2,1)S(1)} %pad_maximum_fusion.refs_0_), channel_id=1, source_target_pairs={{0,1},{1,0},{2,3},{3,2},{4,5},{5,4},{6,7},{7,6},{8,9},{9,8},{10,11... | collective-permute-start | bytes 786440 | tf_op jit(solution)/shard_map/ppermute | solution.py:487
  16.6 7.8 %collective-permute-start.5 = (bf16[800,128]{1,0:T(8,128)(2,1)S(1)}, bf16[800,128]{1,0:T(8,128)(2,1)S(1)}, u32[]{:S(2)}, u32[]{:S(2)}) collective-permute-start(bf16[800,128]{1,0:T(8,128)(2,1)S(1)} %constant_dynamic-update-slice_fusion.refs_4_), channel_id=1, source_target_pairs={{0,1},{1,0},{2,3},{3,2},{4,5},{5,4},{6,7},{7,6},{8,9},{9,8},{10,11... | collective-permute-start | bytes 614408 | tf_op jit(solution)/shard_map/ppermute | solution.py:487
  20.0 4.4 %copy-start.2 = (bf16[1024,128]{1,0:T(8,128)(2,1)}, bf16[1024,128]{1,0:T(8,128)(2,1)S(1)}, u32[]{:S(2)}) copy-start(bf16[1024,128]{1,0:T(8,128)(2,1)S(1)} %collective-permute-done.3.refs_2_) | copy-start | bytes 786436
  20.0 4.4 %collective-permute-start.4 = (bf16[1024,128]{1,0:T(8,128)(2,1)S(1)}, bf16[1024,128]{1,0:T(8,128)(2,1)S(1)}, u32[]{:S(2)}, u32[]{:S(2)}) collective-permute-start(bf16[1024,128]{1,0:T(8,128)(2,1)S(1)} %collective-permute-done.3.refs_2_), channel_id=1, source_target_pairs={{0,1},{1,0},{2,3},{3,2},{4,5},{5,4},{6,7},{7,6},{8,9},{9,8},{10,11... | collective-permute-start | bytes 786440 | tf_op jit(solution)/shard_map/ppermute | solution.py:487
  22.9 1.5 %copy-start.5 = (bf16[800,128]{1,0:T(8,128)(2,1)}, bf16[800,128]{1,0:T(8,128)(2,1)S(1)}, u32[]{:S(2)}) copy-start(bf16[800,128]{1,0:T(8,128)(2,1)S(1)} %collective-permute-done.6.refs_6_) | copy-start | bytes 614404
  22.9 1.5 %collective-permute-start.7 = (bf16[800,128]{1,0:T(8,128)(2,1)S(1)}, bf16[800,128]{1,0:T(8,128)(2,1)S(1)}, u32[]{:S(2)}, u32[]{:S(2)}) collective-permute-start(bf16[800,128]{1,0:T(8,128)(2,1)S(1)} %collective-permute-done.6.refs_6_), channel_id=1, source_target_pairs={{0,1},{1,0},{2,3},{3,2},{4,5},{5,4},{6,7},{7,6},{8,9},{9,8},{10,11... | collective-permute-start | bytes 614408 | tf_op jit(solution)/shard_map/ppermute | solution.py:487
  24.3 0.7 %copy-start.3 = (bf16[1024,128]{1,0:T(8,128)(2,1)}, bf16[1024,128]{1,0:T(8,128)(2,1)S(1)}, u32[]{:S(2)}) copy-start(bf16[1024,128]{1,0:T(8,128)(2,1)S(1)} %collective-permute-done.2.refs_1_) | copy-start | bytes 786436
  24.3 0.8 %copy-start.6 = (bf16[800,128]{1,0:T(8,128)(2,1)}, bf16[800,128]{1,0:T(8,128)(2,1)S(1)}, u32[]{:S(2)}) copy-start(bf16[800,128]{1,0:T(8,128)(2,1)S(1)} %collective-permute-done.5.refs_5_) | copy-start | bytes 614404
  24.4 0.8 %copy-start.7 = (bf16[800,128]{1,0:T(8,128)(2,1)}, bf16[800,128]{1,0:T(8,128)(2,1)S(1)}, u32[]{:S(2)}) copy-start(bf16[800,128]{1,0:T(8,128)(2,1)S(1)} %collective-permute-done.7.refs_7_) | copy-start | bytes 614404
  24.4 0.8 %copy-start.4 = (bf16[1024,128]{1,0:T(8,128)(2,1)}, bf16[1024,128]{1,0:T(8,128)(2,1)S(1)}, u32[]{:S(2)}) copy-start(bf16[1024,128]{1,0:T(8,128)(2,1)S(1)} %collective-permute-done.4.refs_3_) | copy-start | bytes 786436
  46.1 2.0 %collective-permute-start.8 = (bf16[2,8,112,128]{3,2,0,1:T(8,128)(2,1)S(1)}, bf16[2,8,112,128]{3,2,0,1:T(8,128)(2,1)S(1)}, u32[]{:S(2)}, u32[]{:S(2)}) collective-permute-start(bf16[2,8,112,128]{3,2,0,1:T(8,128)(2,1)S(1)} %bitcast.34), channel_id=1, source_target_pairs={{0,1},{1,0},{2,3},{3,2},{4,5},{5,4},{6,7},{7,6},{8,9},{9,8},{10,11... | collective-permute-start | bytes 1376264 | tf_op jit(solution)/shard_map/ppermute | solution.py:487

commit v3 on v2

--- a/solution.py
+++ b/solution.py
@@ -153,6 +153,7 @@
 
 
 HALO = 4
+VMEM_LIMIT = 51 * 1024 * 1024
 BF = jnp.bfloat16
 F32 = jnp.float32
 
@@ -192,7 +193,7 @@
     return shapes
 
 
-def convolve_region(region, weights, transposed, result):
+def convolve_region(region, kernel, transposed, result):
     q_size, r_size = region.z_size // 2 - 1, region.y_size // 2 - 1
     channels = region.even.shape[-1] // 3
     pieces = []
@@ -213,71 +214,95 @@
             ]
             pieces.append(piece.reshape(-1, channels))
     left = jnp.concatenate(pieces, axis=1)
-    if transposed:
-        right = jnp.concatenate([weights[at // 4, at % 4] for at in range(36)], axis=1)
-        contract = (((1,), (1,)), ((), ()))
-    else:
-        right = weights[...].reshape(36 * channels, 2 * channels)
-        contract = (((1,), (0,)), ((), ()))
+    blank = jnp.zeros((channels, channels), BF)
+    blocks = []
+    for block in range(9):
+        taps = [kernel[block * 3 + y_tap] for y_tap in range(3)]
+        for near, far in zip(*((taps + [blank], [blank] + taps) if not transposed else ([blank] + taps, taps + [blank]))):
+            blocks.append(jnp.concatenate([near, far], axis=0 if transposed else 1))
+    right = jnp.concatenate(blocks, axis=1 if transposed else 0)
+    contract = (((1,), (1 if transposed else 0,)), ((), ()))
     product = lax.dot_general(left, right, contract, preferred_element_type=F32)
     result[0:q_size, 0:r_size] = product.reshape(q_size, r_size, product.shape[0] // (q_size * r_size), -1)
 
 
-def kernel_copies(kernel, weights, sems, transposed):
-    channels = kernel.shape[-1]
-    copies = []
-    for parity in range(2):
-        out = pl.ds(parity * channels, channels)
-        if transposed:
-            place = weights.at[:, pl.ds(1 - parity, 3), out, :]
-        else:
-            place = weights.at[:, pl.ds(parity, 3), :, out]
-        copies.append(pltpu.make_async_copy(kernel, place, sems.at[parity]))
-    return copies
-
-
-def clear_unused(weights, transposed):
-    channels = min(weights.shape[2:])
-    blank = jnp.zeros((channels, channels), BF)
-    for block in range(9):
-        if transposed:
-            weights[block, 0, 0:channels, :] = blank
-            weights[block, 3, channels:, :] = blank
-        else:
-            weights[block, 3, :, 0:channels] = blank
-            weights[block, 0, :, channels:] = blank
-
-
-def place_slots(slots, codes, sources, volume, mask):
-    raw, offset, stride, y_first, y_count, cls, lifted = sources
-    for block in range(len(raw)):
-        code = codes[cls, slots[block]]
+def place_slots(codes, blocks, offset, y_first, y_count, lifted, volume, mask, side):
+    for code, block in zip(codes, blocks):
 
         @pl.when(code > 0)
         def _():
             z_first = HALO + (code - 1) * TE
-            rows = TE * TE * stride
-            lifted[0:rows] = raw[block][offset : offset + rows].astype(F32)
+            rows = TE * TE * y_count
+            lifted[0:rows] = block[offset : offset + rows].astype(F32)
             for z_at in range(TE):
                 for y_at in range(y_count):
-                    volume[z_first + z_at, y_first + y_at] = lifted[pl.ds(z_at * TE * stride + y_at, TE, stride=stride)]
+                    row = z_at * TE * y_count + y_at
+                    volume[z_first + z_at, y_first + y_at] = lifted[pl.ds(row, TE, stride=y_count)]
             if mask is not None:
-                mask[cls, pl.ds(z_first, TE)] = jnp.ones((TE,) + mask.shape[2:], F32)
-
-
-def backward_kernel(block_count, packs_per, channels, tiles, codes, depth_at, *refs):
-    own = refs[:block_count]
-    rims = refs[block_count : 2 * block_count]
-    first_kernel, second_kernel = refs[2 * block_count : 2 * block_count + 2]
-    input_grad, grads = refs[2 * block_count + 2 : 2 * block_count + 4]
-    rest = list(refs[2 * block_count + 4 :])
+                mask[side, pl.ds(z_first, TE)] = jnp.ones((TE,) + mask.shape[2:], F32)
+
+
+def side_sizes():
+    face, thin = HALO * TE * TE, 2 * TE * TE
+    return face, thin, face + thin + 16
+
+
+def sides_kernel(tile, used, feature_rows, upstream_rows, to_above, to_below, own, lifted):
+    voxels, channels = feature_rows.shape
+    face = side_sizes()[0]
+    own[0:voxels] = feature_rows[...]
+    own[voxels : 2 * voxels] = upstream_rows[...]
+    for rows, width, offset in ((feature_rows, HALO, 0), (upstream_rows, 2, face)):
+        lifted[...] = rows[...].astype(F32).reshape(lifted.shape)
+        count = TE * TE * width
+        to_above[offset : offset + count] = lifted[:, TE - width :].reshape(count, channels).astype(BF)
+        to_below[offset : offset + count] = lifted[:, :width].reshape(count, channels).astype(BF)
+    place = lax.broadcasted_iota(jnp.int32, (16, channels), 0)
+    table = jnp.zeros((16, channels), F32)
+    for slot in range(tile.shape[1]):
+        code = jnp.where(used[0, slot] == 1, tile[0, slot] + 1, 0)
+        table = jnp.where(place == slot, code.astype(F32), table)
+    for out in (to_above, to_below, own):
+        out[out.shape[0] - 16 :] = table.astype(BF)
+
+
+def sides_call(slot_tile, slot_used, feature_rows, upstream_rows):
+    voxels, channels = feature_rows.shape
+    smem = pl.BlockSpec(memory_space=pltpu.SMEM)
+    vmem = pl.BlockSpec(memory_space=pltpu.VMEM)
+    side = jax.ShapeDtypeStruct((side_sizes()[2], channels), BF)
+    return pl.pallas_call(
+        sides_kernel,
+        out_shape=[side, side, jax.ShapeDtypeStruct((2 * voxels + 16, channels), BF)],
+        in_specs=[smem, smem, vmem, vmem],
+        out_specs=[vmem] * 3,
+        scratch_shapes=[pltpu.VMEM((TE * TE, TE, channels), F32)],
+        name="pack_sides",
+    )(slot_tile, slot_used, feature_rows, upstream_rows)
+
+
+def backward_kernel(block_count, tiles, depth_ref, *refs):
+    own, rims = refs[:block_count], refs[block_count : 2 * block_count]
+    far_kernels = refs[2 * block_count : 2 * block_count + 2]
+    input_grad, kept, given = refs[2 * block_count + 2 : 2 * block_count + 5]
+    rest = list(refs[2 * block_count + 5 :])
+    channels = own[0].shape[-1]
 
     def take():
         return rest.pop(0)
 
-    volume, upstream, mask, lifted, result, grad_rows = (take() for _ in range(6))
-    weights = [take() for _ in range(4)]
-    sems = [take() for _ in range(4)]
+    volume, upstream, mask, lifted, result, grad_rows, first_kernel, second_kernel, near_own, sems = (
+        take() for _ in range(10)
+    )
+    fetches = [
+        pltpu.make_async_copy(far, near, sems.at[at])
+        for at, (far, near) in enumerate(
+            ((own[0], near_own), (far_kernels[0], first_kernel), (far_kernels[1], second_kernel))
+        )
+    ]
+    for fetch in fetches:
+        fetch.start()
+    own = (near_own,) + own[1:]
     regions = []
     for number in range(tiles):
         halo = HALO - number
@@ -290,38 +315,35 @@
         regions.append(group)
     slopes = [take() for _ in range(tiles)]
 
-    copies = [
-        kernel_copies(first_kernel, weights[0], sems[0], False),
-        kernel_copies(second_kernel, weights[1], sems[1], False),
-        kernel_copies(second_kernel, weights[2], sems[2], True),
-        kernel_copies(first_kernel, weights[3], sems[3], True),
-    ]
-    for group in copies:
-        for copy in group:
-            copy.start()
-    for at in range(4):
-        clear_unused(weights[at], at > 1)
-
-    me = depth_at[0]
+    me = depth_ref[0]
     slots = [me ^ block for block in range(block_count)]
     voxels = TE * TE * TE
     volume[...] = jnp.zeros_like(volume)
     upstream[...] = jnp.zeros_like(upstream)
     mask[...] = jnp.zeros_like(mask)
-    face, thin = voxels // 2, voxels // 4
-    rim_size = face + thin + 16
-    for cls, raw, offset, y_first in ((0, rims, 0, 0), (2, rims, rim_size, HALO + TE)):
-        place_slots(slots, codes, (raw, offset, HALO, y_first, HALO, cls, lifted), volume, mask)
-        place_slots(slots, codes, (raw, offset + face, 2, y_first if cls else 2, 2, cls, lifted), upstream, None)
-    place_slots(slots, codes, (own, 0, TE, HALO, TE, 1, lifted), volume, mask)
-    place_slots(slots, codes, (own, voxels, TE, HALO, TE, 1, lifted), upstream, None)
+    face, thin, side_rows = side_sizes()
+
+    def table_at(block, first):
+        table = block[first : first + 16].astype(F32)
+        place = lax.broadcasted_iota(jnp.int32, table.shape, 0)
+        return [jnp.max(jnp.where(place == slot, table, 0.0)).astype(jnp.int32) for slot in slots]
+
+    fetches[0].wait()
+    held = table_at(own[0], 2 * voxels)
+    place_slots(held, own, 0, HALO, TE, lifted, volume, mask, 1)
+    place_slots(held, own, voxels, HALO, TE, lifted, upstream, None, 1)
+    codes = table_at(rims[0], face + thin)
+    place_slots(codes, rims, 0, 0, HALO, lifted, volume, mask, 0)
+    place_slots(codes, rims, face, HALO - 2, 2, lifted, upstream, None, 0)
+    codes = table_at(rims[0], side_rows + face + thin)
+    place_slots(codes, rims, side_rows, HALO + TE, HALO, lifted, volume, mask, 2)
+    place_slots(codes, rims, side_rows + face, HALO + TE, 2, lifted, upstream, None, 2)
 
     starts = []
     alive = []
     for number in range(tiles):
-        slot = slots[2 * number]
-        starts.append(codes[3, slot] * TE)
-        alive.append((codes[1, slot] > 0).astype(F32))
+        starts.append(jnp.maximum(held[2 * number] - 1, 0) * TE)
+        alive.append((held[2 * number] > 0).astype(F32))
 
     for number in range(tiles):
         source = regions[number][0]
@@ -354,10 +376,6 @@
                 else:
                     out = value * slopes[number][2 : 2 + region.z_size, pair + 1, parity]
                 region.store_row(pair, parity, out)
-
-    def wait(at):
-        for copy in copies[at]:
-            copy.wait()
 
     def kernel_gradient(at, left, delta):
         flipped = []
@@ -382,28 +400,30 @@
                     lane = (y_tap * 3 + x_tap) * channels
                     row = (z_tap * 9 + x_tap * 3 + y_tap) * channels
                     grad_rows[row : row + channels] = product[:, lane : lane + channels].T
-        share = 27 * channels // grads.shape[1]
-        padded = grads.shape[2]
-        for part in range(grads.shape[1]):
-            grads[at, part] = grad_rows[part * share : part * share + padded].astype(BF)
+        y_parts, z_parts, _, padded, _ = kept.shape
+        share = 27 * channels // (y_parts * z_parts * block_count)
+        for y_at in range(y_parts):
+            for z_at in range(z_parts):
+                column = (z_at * y_parts + y_at) * block_count
+                for out, owner in ((kept, me), (given, me ^ 1)):
+                    rows = grad_rows[pl.ds((column + owner) * share, padded)]
+                    out[y_at, z_at, at] = rows.astype(BF)
 
     grad_rows[27 * channels :] = jnp.zeros_like(grad_rows[27 * channels :])
-    wait(0)
-    for number in range(tiles):
-        convolve_region(regions[number][0], weights[0], False, result)
+    fetches[1].wait()
+    for number in range(tiles):
+        convolve_region(regions[number][0], first_kernel, False, result)
         finish_layer(number, 1, "act")
-    wait(1)
-    for number in range(tiles):
-        convolve_region(regions[number][1], weights[1], False, result)
+    fetches[2].wait()
+    for number in range(tiles):
+        convolve_region(regions[number][1], second_kernel, False, result)
         finish_layer(number, 2, "delta_two")
     kernel_gradient(1, 1, 2)
-    wait(2)
-    for number in range(tiles):
-        convolve_region(regions[number][2], weights[2], True, result)
+    for number in range(tiles):
+        convolve_region(regions[number][2], second_kernel, True, result)
         finish_layer(number, 3, "delta_one")
     kernel_gradient(0, 0, 3)
-    wait(3)
-    convolve_region(regions[0][3], weights[3], True, result)
+    convolve_region(regions[0][3], first_kernel, True, result)
     for pair in range(TE // 2):
         for parity in range(2):
             value = result[0 : TE // 2, pair, :, parity * channels : (parity + 1) * channels] * alive[0]
@@ -413,14 +433,13 @@
     input_grad[...] = lifted[...].astype(BF)
 
 
-def backward_call(own, rims, first_kernel, second_kernel, codes, depth_at, shares, tiles):
-    channels = first_kernel.shape[-1]
+def backward_call(own, rims, kernels, depth_at, columns, positions, tiles):
+    channels = own[0].shape[-1]
     voxels = TE * TE * TE
-    positions = codes.shape[1]
     planes = positions * TE + 2 * HALO
     span = TE + 2 * HALO
     inner = span // 2 - 1
-    padded = -(-(27 * channels // shares) // 16) * 16
+    padded = -(-(27 * channels // (columns * len(own))) // 16) * 16
     scratch = [
         pltpu.VMEM((planes, span, TE, channels), F32),
         pltpu.VMEM((planes, span, TE, channels), F32),
@@ -428,10 +447,11 @@
         pltpu.VMEM((voxels, channels), F32),
         pltpu.VMEM((inner, inner, 2 * TE, 2 * channels), F32),
         pltpu.VMEM((27 * channels + 16, channels), F32),
+        pltpu.VMEM((27, channels, channels), BF),
+        pltpu.VMEM((27, channels, channels), BF),
+        pltpu.VMEM(own[0].shape, BF),
+        pltpu.SemaphoreType.DMA((3,)),
     ]
-    scratch += [pltpu.VMEM((9, 4, channels, 2 * channels), BF)] * 2
-    scratch += [pltpu.VMEM((9, 4, 2 * channels, channels), BF)] * 2
-    scratch += [pltpu.SemaphoreType.DMA((2,))] * 4
     for number in range(tiles):
         for layer in range(4):
             size = span - 2 * (number + layer)
@@ -441,80 +461,61 @@
         scratch.append(pltpu.VMEM((size, size // 2, 2, TE, channels), F32))
     vmem = pl.BlockSpec(memory_space=pltpu.VMEM)
     smem = pl.BlockSpec(memory_space=pltpu.SMEM)
-    hbm = pl.BlockSpec(memory_space=pl.ANY)
-
-    def body(codes_ref, depth_ref, *refs):
-        backward_kernel(len(own), 0, channels, tiles, codes_ref, depth_ref, *refs)
-
+    hbm = pl.BlockSpec(memory_space=pltpu.HBM)
+
+    def body(*refs):
+        backward_kernel(len(own), tiles, *refs)
+
+    share = jax.ShapeDtypeStruct((2, columns // 2, 2, padded, channels), BF)
     return pl.pallas_call(
         body,
-        out_shape=[
-            jax.ShapeDtypeStruct((voxels, channels), BF),
-            jax.ShapeDtypeStruct((2, shares, padded, channels), BF),
-        ],
-        in_specs=[smem, smem] + [vmem] * (2 * len(own)) + [hbm, hbm],
-        out_specs=[vmem, vmem],
+        out_shape=[jax.ShapeDtypeStruct((voxels, channels), BF), share, share],
+        in_specs=[smem, hbm] + [vmem] * (2 * len(own) - 1) + [hbm, hbm],
+        out_specs=[vmem] * 3,
         scratch_shapes=scratch,
-        compiler_params=pltpu.CompilerParams(vmem_limit_bytes=60 * 1024 * 1024),
+        compiler_params=pltpu.CompilerParams(vmem_limit_bytes=VMEM_LIMIT),
         name="tile_backward",
-    )(codes, depth_at, *own, *rims, *(kernel.reshape(9, 3, channels, channels) for kernel in (first_kernel, second_kernel)))
+    )(depth_at.reshape(1), *own, *rims, *kernels)
 
 
 def on_device_line(features, cotangent, first_kernel, second_kernel, slot_tile, slot_used):
-    voxels, channels = features.shape[2:]
+    channels = features.shape[3]
     depth_size, space_size = lax.axis_size("depth"), lax.axis_size("space")
     depth_at, space_at = lax.axis_index("depth"), lax.axis_index("space")
-    feature_rows, upstream_rows = features[0, 0], cotangent[0, 0]
-    own_code = jnp.where(slot_used[0] == 1, slot_tile[0] + 1, 0)
-
-    code_rows = jnp.pad(own_code, (0, 16 - own_code.shape[0])).astype(BF)
-    code_rows = jnp.broadcast_to(code_rows[:, None], (16, channels))
-    feature_box = feature_rows.reshape(TE, TE, TE, channels)
-    upstream_box = upstream_rows.reshape(TE, TE, TE, channels)
-
-    def side(feature_part, upstream_part):
-        return jnp.concatenate(
-            [feature_part.reshape(-1, channels), upstream_part.reshape(-1, channels), code_rows], axis=0
-        )
-
-    from_below = from_behind(side(feature_box[:, :, TE - HALO :], upstream_box[:, :, TE - 2 :]), "space", 1)
-    from_above = from_behind(side(feature_box[:, :, :HALO], upstream_box[:, :, :2]), "space", -1)
-    own = jnp.concatenate([feature_rows, upstream_rows], axis=0)
-    rim = jnp.concatenate([from_below, from_above], axis=0)
-    rim_size = rim.shape[0] // 2
-
-    def swap(block, bit):
-        return lax.ppermute(block, "depth", [(i, i ^ bit) for i in range(depth_size)])
-
-    own_far, rim_far = swap(own, 2), swap(rim, 2)
-    own_blocks = [own, swap(own, 1), own_far, swap(own_far, 1)]
-    rim_blocks = [rim, swap(rim, 1), rim_far, swap(rim_far, 1)]
-
-    def side_code(first):
-        return rim[first : first + own_code.shape[0], 0].astype(jnp.int32)
-
-    codes = jnp.stack([side_code(rim_size - 16), own_code, side_code(2 * rim_size - 16), slot_tile[0]])
-    shares = depth_size * space_size
-    input_grad, grads = backward_call(
-        own_blocks,
-        rim_blocks,
-        first_kernel,
-        second_kernel,
-        codes,
-        depth_at.reshape(1),
-        shares,
+
+    def swap(block, axis, bits):
+        return lax.ppermute(block, axis, [(i, i ^ bits) for i in range(lax.axis_size(axis))])
+
+    to_above, to_below, own = sides_call(slot_tile, slot_used, features[0, 0], cotangent[0, 0])
+    own_far = swap(own, "depth", 2)
+    below, above = from_behind(to_above, "space", 1), from_behind(to_below, "space", -1)
+    rim = jnp.concatenate([below, above], axis=0)
+    rim_far = swap(rim, "depth", 2)
+
+    def with_sibling(near, far):
+        return [near, swap(near, "depth", 1), far, swap(far, "depth", 1)]
+
+    input_grad, kept, given = backward_call(
+        with_sibling(own, own_far),
+        with_sibling(rim, rim_far),
+        (first_kernel, second_kernel),
+        depth_at,
+        space_size,
+        slot_tile.shape[1],
         2,
     )
-    share = 27 * channels // shares
-    by_owner = grads.reshape(2, space_size, depth_size, grads.shape[2], channels)
-
-    def for_depth(owner):
-        return lax.dynamic_index_in_dim(by_owner, owner, 2, keepdims=False)
-
-    summed = for_depth(depth_at).astype(F32) + swap(for_depth(depth_at ^ 1), 1).astype(F32)
-    parts = lax.all_to_all(summed.astype(BF), "space", 1, 1, tiled=True)
-    total = jnp.sum(parts.astype(F32), axis=1)[:, :share]
-    first_share, second_share = total[0].reshape(-1), total[1].reshape(-1)
+    share = 27 * channels // (depth_size * space_size)
+
+    def part(block, at):
+        return lax.dynamic_index_in_dim(block, at, 0, keepdims=False)
+
+    y_at, z_at = space_at % 2, space_at // 2
+    column_sum = kept.astype(F32) + swap(given, "depth", 1).astype(F32)
+    line = part(column_sum, y_at) + swap(part(column_sum, 1 - y_at).astype(BF), "space", 1).astype(F32)
+    total = part(line, z_at)
+    for step in range(1, space_size // 2):
+        total = total + swap(part(line, z_at ^ step).astype(BF), "space", 2 * step).astype(F32)
+    first_share, second_share = (total[at, :share].reshape(-1) for at in range(2))
     return (input_grad.reshape(features.shape), first_share, second_share)
 
 

time: 69.4 us -> 59.3 us (0.85)
  blocking collectives: 20.2 us -> 0 us
  waiting for transfers between devices: 9.95 us -> 23.4 us
  starting transfers between devices: 10.4 us -> 16.2 us
  local copies, waits for them, and re-layouts: 4.83 us -> 0.75 us
  other arithmetic: 3.46 us -> 0.16 us
  Pallas kernels: 19.5 us -> 18 us
    all_to_all x1 -> x0, blocking collectives: 20.2 us -> none  [on_device_line(): parts = lax.all_to_all(summed.astype(BF), 'space', 1, 1, tiled=True)]
    ppermute x7 -> x11, waiting for transfers between devices: 7.27 us -> 17.9 us  [swap(): lax.ppermute(block, axis, [(i, i ^ bits) for i in range(lax.axis_size(axi...]
    ppermute x7 -> x11, starting transfers between devices: 4.2 us -> 9.9 us  [swap(): lax.ppermute(block, axis, [(i, i ^ bits) for i in range(lax.axis_size(axi...]
    pallas_call x1, Pallas kernels: 19.5 us -> 16.2 us  [backward_call(): pl.pallas_call(body, out_shape=[jax.ShapeDtypeStruct((voxels, channels),...]
    ppermute x2, waiting for transfers between devices: 2.68 us -> 5.44 us  [from_behind(): return lax.ppermute(block, axis, route)]
    slice x2 -> x0, local copies, waits for them, and re-layouts: 2.07 us -> none  [the longest x1 1.04 us: on_device_line(): feature_box[:, :, TE - HALO:]]
    pallas_call x0 -> x1, Pallas kernels: none -> 1.81 us  [sides_call(): pl.pallas_call(sides_kernel, out_shape=[side, side, jax.ShapeDtypeStruct(...]
    dynamic_slice x2 -> x0, local copies, waits for them, and re-layouts: 1.26 us -> none  [for_depth(): return lax.dynamic_index_in_dim(by_owner, owner, 2, keepdims=False)]
  transfers between devices with their start and end apart: 9 -> 13, of which waited for: 5 -> 7; matrix products, arithmetic and copies ran while one was open for 4% -> 0% of each run, Pallas kernels for 0% -> 0%
where the time goes in v3:
time: 59.3 us; the launch traced here: 59.2 us
  waiting for transfers between devices  23.4 us (39%)
  Pallas kernels  18 us (30%)
  starting transfers between devices  16.2 us (27%)
  local copies, waits for them, and re-layouts  0.75 us (1%)
  between operations  0.72 us (1%)
    ppermute x11, waiting for transfers between devices, swap(): lax.ppermute(block, axis, [(i, i ^ bits) for i in range(lax.axis_size(axi...  17.9 us
    pallas_call x1, Pallas kernels, backward_call(): pl.pallas_call(body, out_shape=[jax.ShapeDtypeStruct((voxels, channels),...  16.2 us
    ppermute x11, starting transfers between devices, swap(): lax.ppermute(block, axis, [(i, i ^ bits) for i in range(lax.axis_size(axi...  9.9 us
    ppermute x2, starting transfers between devices, from_behind(): return lax.ppermute(block, axis, route)  6.28 us
    ppermute x2, waiting for transfers between devices, from_behind(): return lax.ppermute(block, axis, route)  5.44 us
    pallas_call x1, Pallas kernels, sides_call(): pl.pallas_call(sides_kernel, out_shape=[side, side, jax.ShapeDtypeStruct(...  1.81 us
  transfers between devices with their start and end apart: 13, of which 7 were waited for; matrix products, arithmetic and copies ran while one was open for 0% of the time, Pallas kernels for 0%

profile of v3, /device:TPU:0, one launch (start us, length us, event | category | flops | bytes accessed | tf_op | source)
XLA Modules:
  0.0 59.2 jit_solution(4166474231552484203)
XLA Ops:
  0.6 1.8 %pack_sides.1 = (bf16[400,128]{1,0:T(8,128)(2,1)}, bf16[400,128]{1,0:T(8,128)(2,1)}, bf16[1040,128]{1,0:T(8,128)(2,1)}) custom-call(s32[1,4]{1,0:T(1,128)} %tile.1, s32[1,4]{1,0:T(1,128)} %used.1, bf16[512,128]{1,0:T(8,128)(2,1)} %bitcast.24, bf16[512,128]{1,0:T(8,128)(2,1)} %bitcast.25), custom_call_target="tpu_custom_call" | custom-call | tf_op jit(solution)/shard_map/pack_sides/pallas_call | solution.py:274
  2.4 0.0 copy-start
  2.4 5.0 %collective-permute-start.3 = (bf16[400,128]{1,0:T(8,128)(2,1)}, bf16[400,128]{1,0:T(8,128)(2,1)S(1)}, u32[]{:S(2)}, u32[]{:S(2)}) collective-permute-start(bf16[400,128]{1,0:T(8,128)(2,1)} %get-tuple-element.10), channel_id=1, source_target_pairs={{0,4},{4,8},{8,12},{12,16},{16,20},{20,24},{24,28},{1,5},{5,9},{9,... | collective-permute-start | bytes 307208 | tf_op jit(solution)/shard_map/ppermute | solution.py:19
  7.5 1.6 %collective-permute-start.1 = (bf16[1040,128]{1,0:T(8,128)(2,1)}, bf16[1040,128]{1,0:T(8,128)(2,1)S(1)}, u32[]{:S(2)}, u32[]{:S(2)}) collective-permute-start(bf16[1040,128]{1,0:T(8,128)(2,1)} %get-tuple-element.9.refs_1_), channel_id=1, source_target_pairs={{0,2},{1,3},{2,0},{3,1},{4,6},{5,7},{6,4},{7,5},{8,10},{9,11},{10,... | collective-permute-start | bytes 798728 | tf_op jit(solution)/shard_map/ppermute | solution.py:487
  9.0 1.3 %collective-permute-start.4 = (bf16[400,128]{1,0:T(8,128)(2,1)}, bf16[400,128]{1,0:T(8,128)(2,1)S(1)}, u32[]{:S(2)}, u32[]{:S(2)}) collective-permute-start(bf16[400,128]{1,0:T(8,128)(2,1)} %get-tuple-element.11), channel_id=1, source_target_pairs={{4,0},{8,4},{12,8},{16,12},{20,16},{24,20},{28,24},{5,1},{9,5},{13... | collective-permute-start | bytes 307208 | tf_op jit(solution)/shard_map/ppermute | solution.py:19
  10.3 0.0 collective-permute-done.3
  10.3 5.4 %collective-permute-done.4 = bf16[400,128]{1,0:T(8,128)(2,1)S(1)} collective-permute-done((bf16[400,128]{1,0:T(8,128)(2,1)}, bf16[400,128]{1,0:T(8,128)(2,1)S(1)}, u32[]{:S(2)}, u32[]{:S(2)}) %collective-permute-start.4) | collective-permute-done | bytes 102432 | tf_op jit(solution)/shard_map/ppermute | solution.py:19
  15.8 0.6 %collective-permute-start.6 = (bf16[800,128]{1,0:T(8,128)(2,1)S(1)}, bf16[800,128]{1,0:T(8,128)(2,1)S(1)}, u32[]{:S(2)}, u32[]{:S(2)}) collective-permute-start(bf16[800,128]{1,0:T(8,128)(2,1)S(1)} %constant_dynamic-update-slice_fusion.refs_5_), channel_id=1, source_target_pairs={{0,2},{1,3},{2,0},{3,1},{4,6},{5,7},{6,4},{7,5},{8,10},{9,11},{10,... | collective-permute-start | bytes 614408 | tf_op jit(solution)/shard_map/ppermute | solution.py:487
  16.4 0.0 copy-done
  16.4 0.0 collective-permute-start
  16.4 0.0 collective-permute-done.1.refs_3_
  16.4 0.5 collective-permute-start.2
  16.9 0.1 collective-permute-start.5
  17.0 4.6 %collective-permute-done.6.refs_7_ = bf16[800,128]{1,0:T(8,128)(2,1)S(1)} collective-permute-done((bf16[800,128]{1,0:T(8,128)(2,1)S(1)}, bf16[800,128]{1,0:T(8,128)(2,1)S(1)}, u32[]{:S(2)}, u32[]{:S(2)}) %collective-permute-start.6) | collective-permute-done | bytes 204832 | tf_op jit(solution)/shard_map/ppermute | solution.py:487
  21.6 0.0 collective-permute-start.7
  21.6 0.0 collective-permute-done.refs_2_
  21.6 0.0 collective-permute-done.5.refs_6_
  21.6 1.4 %collective-permute-done.7.refs_8_ = bf16[800,128]{1,0:T(8,128)(2,1)S(1)} collective-permute-done((bf16[800,128]{1,0:T(8,128)(2,1)S(1)}, bf16[800,128]{1,0:T(8,128)(2,1)S(1)}, u32[]{:S(2)}, u32[]{:S(2)}) %collective-permute-start.7) | collective-permute-done | bytes 204832 | tf_op jit(solution)/shard_map/ppermute | solution.py:487
  23.1 0.0 collective-permute-done.2.refs_4_
  23.1 16.2 %tile_backward.1 = (bf16[512,128]{1,0:T(8,128)(2,1)}, bf16[2,4,2,112,128]{4,3,2,1,0:T(8,128)(2,1)S(1)}, bf16[2,4,2,112,128]{4,3,2,1,0:T(8,128)(2,1)S(1)}) custom-call(s32[1]{0:T(128)} %bitcast.refs_0_, bf16[1040,128]{1,0:T(8,128)(2,1)S(1)} %copy-done, bf16[1040,128]{1,0:T(8,128)(2,1)S(1)} %collective-permute-done.refs_2_, ...), custom_call_target="tpu_custom_call" | custom-call | tf_op jit(solution)/shard_map/tile_backward/pallas_call | solution.py:470
  39.2 0.2 collective-permute-start.8
  39.5 1.7 %collective-permute-done.8 = bf16[2,4,2,112,128]{4,3,2,1,0:T(8,128)(2,1)S(1)} collective-permute-done((bf16[2,4,2,112,128]{4,3,2,1,0:T(8,128)(2,1)S(1)}, bf16[2,4,2,112,128]{4,3,2,1,0:T(8,128)(2,1)S(1)}, u32[]{:S(2)}, u32[]{:S(2)}) %collective-permute-start.8) | collective-permute-done | bytes 458784 | tf_op jit(solution)/shard_map/ppermute | solution.py:487
  41.1 0.1 convert_add_fusion
  41.3 2.5 %collective-permute-start.9 = (bf16[4,2,112,128]{3,2,1,0:T(8,128)(2,1)S(1)}, bf16[4,2,112,128]{3,2,1,0:T(8,128)(2,1)S(1)}, u32[]{:S(2)}, u32[]{:S(2)}) collective-permute-start(bf16[4,2,112,128]{3,2,1,0:T(8,128)(2,1)S(1)} %fusion), channel_id=1, source_target_pairs={{0,4},{4,0},{8,12},{12,8},{16,20},{20,16},{24,28},{28,24},{1,5},{5... | collective-permute-start | bytes 688136 | tf_op jit(solution)/shard_map/ppermute | solution.py:487
  43.8 5.9 %collective-permute-done.9 = bf16[4,2,112,128]{3,2,1,0:T(8,128)(2,1)S(1)} collective-permute-done((bf16[4,2,112,128]{3,2,1,0:T(8,128)(2,1)S(1)}, bf16[4,2,112,128]{3,2,1,0:T(8,128)(2,1)S(1)}, u32[]{:S(2)}, u32[]{:S(2)}) %collective-permute-start.9) | collective-permute-done | bytes 229408 | tf_op jit(solution)/shard_map/ppermute | solution.py:487
  49.8 3.0 %collective-permute-start.12 = (bf16[2,112,128]{2,1,0:T(8,128)(2,1)S(1)}, bf16[2,112,128]{2,1,0:T(8,128)(2,1)S(1)}, u32[]{:S(2)}, u32[]{:S(2)}) collective-permute-start(bf16[2,112,128]{2,1,0:T(8,128)(2,1)S(1)} %get-tuple-element.16), channel_id=1, source_target_pairs={{0,24},{4,28},{8,16},{12,20},{16,8},{20,12},{24,0},{28,4},{1,25},{... | collective-permute-start | bytes 172040 | tf_op jit(solution)/shard_map/ppermute | solution.py:487
  52.8 0.5 collective-permute-start.11
  53.3 0.9 %collective-permute-start.10 = (bf16[2,112,128]{2,1,0:T(8,128)(2,1)S(1)}, bf16[2,112,128]{2,1,0:T(8,128)(2,1)S(1)}, u32[]{:S(2)}, u32[]{:S(2)}) collective-permute-start(bf16[2,112,128]{2,1,0:T(8,128)(2,1)S(1)} %get-tuple-element.15), channel_id=1, source_target_pairs={{0,8},{4,12},{8,0},{12,4},{16,24},{20,28},{24,16},{28,20},{1,9},{5... | collective-permute-start | bytes 172040 | tf_op jit(solution)/shard_map/ppermute | solution.py:487
  54.2 2.0 %collective-permute-done.12 = bf16[2,112,128]{2,1,0:T(8,128)(2,1)S(1)} collective-permute-done((bf16[2,112,128]{2,1,0:T(8,128)(2,1)S(1)}, bf16[2,112,128]{2,1,0:T(8,128)(2,1)S(1)}, u32[]{:S(2)}, u32[]{:S(2)}) %collective-permute-start.12) | collective-permute-done | bytes 57376 | tf_op jit(solution)/shard_map/ppermute | solution.py:487
  56.3 2.2 %collective-permute-done.11 = bf16[2,112,128]{2,1,0:T(8,128)(2,1)S(1)} collective-permute-done((bf16[2,112,128]{2,1,0:T(8,128)(2,1)S(1)}, bf16[2,112,128]{2,1,0:T(8,128)(2,1)S(1)}, u32[]{:S(2)}, u32[]{:S(2)}) %collective-permute-start.11) | collective-permute-done | bytes 57376 | tf_op jit(solution)/shard_map/ppermute | solution.py:487
  58.5 0.0 collective-permute-done.10
  58.5 0.6 %slice_bitcast_fusion = (f32[13824]{0:T(1024)}, f32[13824]{0:T(1024)}) fusion(f32[2,112,128]{2,1,0:T(8,128)S(1)} %fusion.2), kind=kLoop, calls=%fused_computation.13 | loop fusion | bytes 221184 | tf_op jit(solution)/shard_map/reshape;squeeze | solution.py:518
  (6 shorter events, 0.2 us)
Async XLA Ops:
  2.4 13.9 %copy-start = (bf16[1040,128]{1,0:T(8,128)(2,1)S(1)}, bf16[1040,128]{1,0:T(8,128)(2,1)}, u32[]{:S(2)}) copy-start(bf16[1040,128]{1,0:T(8,128)(2,1)} %get-tuple-element.9.refs_1_) | copy-start | bytes 798724
  2.4 7.9 %collective-permute-start.3 = (bf16[400,128]{1,0:T(8,128)(2,1)}, bf16[400,128]{1,0:T(8,128)(2,1)S(1)}, u32[]{:S(2)}, u32[]{:S(2)}) collective-permute-start(bf16[400,128]{1,0:T(8,128)(2,1)} %get-tuple-element.10), channel_id=1, source_target_pairs={{0,4},{4,8},{8,12},{12,16},{16,20},{20,24},{24,28},{1,5},{5,9},{9,... | collective-permute-start | bytes 307208 | tf_op jit(solution)/shard_map/ppermute | solution.py:19
  7.5 8.9 %collective-permute-start.1 = (bf16[1040,128]{1,0:T(8,128)(2,1)}, bf16[1040,128]{1,0:T(8,128)(2,1)S(1)}, u32[]{:S(2)}, u32[]{:S(2)}) collective-permute-start(bf16[1040,128]{1,0:T(8,128)(2,1)} %get-tuple-element.9.refs_1_), channel_id=1, source_target_pairs={{0,2},{1,3},{2,0},{3,1},{4,6},{5,7},{6,4},{7,5},{8,10},{9,11},{10,... | collective-permute-start | bytes 798728 | tf_op jit(solution)/shard_map/ppermute | solution.py:487
  9.0 6.8 %collective-permute-start.4 = (bf16[400,128]{1,0:T(8,128)(2,1)}, bf16[400,128]{1,0:T(8,128)(2,1)S(1)}, u32[]{:S(2)}, u32[]{:S(2)}) collective-permute-start(bf16[400,128]{1,0:T(8,128)(2,1)} %get-tuple-element.11), channel_id=1, source_target_pairs={{4,0},{8,4},{12,8},{16,12},{20,16},{24,20},{28,24},{5,1},{9,5},{13... | collective-permute-start | bytes 307208 | tf_op jit(solution)/shard_map/ppermute | solution.py:19
  15.8 5.8 %collective-permute-start.6 = (bf16[800,128]{1,0:T(8,128)(2,1)S(1)}, bf16[800,128]{1,0:T(8,128)(2,1)S(1)}, u32[]{:S(2)}, u32[]{:S(2)}) collective-permute-start(bf16[800,128]{1,0:T(8,128)(2,1)S(1)} %constant_dynamic-update-slice_fusion.refs_5_), channel_id=1, source_target_pairs={{0,2},{1,3},{2,0},{3,1},{4,6},{5,7},{6,4},{7,5},{8,10},{9,11},{10,... | collective-permute-start | bytes 614408 | tf_op jit(solution)/shard_map/ppermute | solution.py:487
  16.4 5.2 %collective-permute-start = (bf16[1040,128]{1,0:T(8,128)(2,1)S(1)}, bf16[1040,128]{1,0:T(8,128)(2,1)S(1)}, u32[]{:S(2)}, u32[]{:S(2)}) collective-permute-start(bf16[1040,128]{1,0:T(8,128)(2,1)S(1)} %copy-done), channel_id=1, source_target_pairs={{0,1},{1,0},{2,3},{3,2},{4,5},{5,4},{6,7},{7,6},{8,9},{9,8},{10,11... | collective-permute-start | bytes 798728 | tf_op jit(solution)/shard_map/ppermute | solution.py:487
  16.4 6.7 %collective-permute-start.2 = (bf16[1040,128]{1,0:T(8,128)(2,1)S(1)}, bf16[1040,128]{1,0:T(8,128)(2,1)S(1)}, u32[]{:S(2)}, u32[]{:S(2)}) collective-permute-start(bf16[1040,128]{1,0:T(8,128)(2,1)S(1)} %collective-permute-done.1.refs_3_), channel_id=1, source_target_pairs={{0,1},{1,0},{2,3},{3,2},{4,5},{5,4},{6,7},{7,6},{8,9},{9,8},{10,11... | collective-permute-start | bytes 798728 | tf_op jit(solution)/shard_map/ppermute | solution.py:487
  16.9 4.7 %collective-permute-start.5 = (bf16[800,128]{1,0:T(8,128)(2,1)S(1)}, bf16[800,128]{1,0:T(8,128)(2,1)S(1)}, u32[]{:S(2)}, u32[]{:S(2)}) collective-permute-start(bf16[800,128]{1,0:T(8,128)(2,1)S(1)} %constant_dynamic-update-slice_fusion.refs_5_), channel_id=1, source_target_pairs={{0,1},{1,0},{2,3},{3,2},{4,5},{5,4},{6,7},{7,6},{8,9},{9,8},{10,11... | collective-permute-start | bytes 614408 | tf_op jit(solution)/shard_map/ppermute | solution.py:487
  21.6 1.5 %collective-permute-start.7 = (bf16[800,128]{1,0:T(8,128)(2,1)S(1)}, bf16[800,128]{1,0:T(8,128)(2,1)S(1)}, u32[]{:S(2)}, u32[]{:S(2)}) collective-permute-start(bf16[800,128]{1,0:T(8,128)(2,1)S(1)} %collective-permute-done.6.refs_7_), channel_id=1, source_target_pairs={{0,1},{1,0},{2,3},{3,2},{4,5},{5,4},{6,7},{7,6},{8,9},{9,8},{10,11... | collective-permute-start | bytes 614408 | tf_op jit(solution)/shard_map/ppermute | solution.py:487
  39.2 1.9 %collective-permute-start.8 = (bf16[2,4,2,112,128]{4,3,2,1,0:T(8,128)(2,1)S(1)}, bf16[2,4,2,112,128]{4,3,2,1,0:T(8,128)(2,1)S(1)}, u32[]{:S(2)}, u32[]{:S(2)}) collective-permute-start(bf16[2,4,2,112,128]{4,3,2,1,0:T(8,128)(2,1)S(1)} %get-tuple-element.14), channel_id=1, source_target_pairs={{0,1},{1,0},{2,3},{3,2},{4,5},{5,4},{6,7},{7,6},{8,9},{9,8},{10,11... | collective-permute-start | bytes 1376264 | tf_op jit(solution)/shard_map/ppermute | solution.py:487
  41.3 8.4 %collective-permute-start.9 = (bf16[4,2,112,128]{3,2,1,0:T(8,128)(2,1)S(1)}, bf16[4,2,112,128]{3,2,1,0:T(8,128)(2,1)S(1)}, u32[]{:S(2)}, u32[]{:S(2)}) collective-permute-start(bf16[4,2,112,128]{3,2,1,0:T(8,128)(2,1)S(1)} %fusion), channel_id=1, source_target_pairs={{0,4},{4,0},{8,12},{12,8},{16,20},{20,16},{24,28},{28,24},{1,5},{5... | collective-permute-start | bytes 688136 | tf_op jit(solution)/shard_map/ppermute | solution.py:487
  49.8 6.5 %collective-permute-start.12 = (bf16[2,112,128]{2,1,0:T(8,128)(2,1)S(1)}, bf16[2,112,128]{2,1,0:T(8,128)(2,1)S(1)}, u32[]{:S(2)}, u32[]{:S(2)}) collective-permute-start(bf16[2,112,128]{2,1,0:T(8,128)(2,1)S(1)} %get-tuple-element.16), channel_id=1, source_target_pairs={{0,24},{4,28},{8,16},{12,20},{16,8},{20,12},{24,0},{28,4},{1,25},{... | collective-permute-start | bytes 172040 | tf_op jit(solution)/shard_map/ppermute | solution.py:487
  52.8 5.8 %collective-permute-start.11 = (bf16[2,112,128]{2,1,0:T(8,128)(2,1)S(1)}, bf16[2,112,128]{2,1,0:T(8,128)(2,1)S(1)}, u32[]{:S(2)}, u32[]{:S(2)}) collective-permute-start(bf16[2,112,128]{2,1,0:T(8,128)(2,1)S(1)} %get-tuple-element.17), channel_id=1, source_target_pairs={{0,16},{4,20},{8,24},{12,28},{16,0},{20,4},{24,8},{28,12},{1,17},{... | collective-permute-start | bytes 172040 | tf_op jit(solution)/shard_map/ppermute | solution.py:487
  53.3 5.2 %collective-permute-start.10 = (bf16[2,112,128]{2,1,0:T(8,128)(2,1)S(1)}, bf16[2,112,128]{2,1,0:T(8,128)(2,1)S(1)}, u32[]{:S(2)}, u32[]{:S(2)}) collective-permute-start(bf16[2,112,128]{2,1,0:T(8,128)(2,1)S(1)} %get-tuple-element.15), channel_id=1, source_target_pairs={{0,8},{4,12},{8,0},{12,4},{16,24},{20,28},{24,16},{28,20},{1,9},{5... | collective-permute-start | bytes 172040 | tf_op jit(solution)/shard_map/ppermute | solution.py:487

commit v4 on v3

--- a/solution.py
+++ b/solution.py
@@ -153,6 +153,7 @@
 
 
 HALO = 4
+NEAR = 4
 VMEM_LIMIT = 51 * 1024 * 1024
 BF = jnp.bfloat16
 F32 = jnp.float32
@@ -247,11 +248,9 @@
     return face, thin, face + thin + 16
 
 
-def sides_kernel(tile, used, feature_rows, upstream_rows, to_above, to_below, own, lifted):
-    voxels, channels = feature_rows.shape
+def sides_kernel(tile, used, feature_rows, upstream_rows, to_above, to_below, own_table, lifted):
+    channels = feature_rows.shape[1]
     face = side_sizes()[0]
-    own[0:voxels] = feature_rows[...]
-    own[voxels : 2 * voxels] = upstream_rows[...]
     for rows, width, offset in ((feature_rows, HALO, 0), (upstream_rows, 2, face)):
         lifted[...] = rows[...].astype(F32).reshape(lifted.shape)
         count = TE * TE * width
@@ -262,7 +261,7 @@
     for slot in range(tile.shape[1]):
         code = jnp.where(used[0, slot] == 1, tile[0, slot] + 1, 0)
         table = jnp.where(place == slot, code.astype(F32), table)
-    for out in (to_above, to_below, own):
+    for out in (to_above, to_below, own_table):
         out[out.shape[0] - 16 :] = table.astype(BF)
 
 
@@ -273,7 +272,7 @@
     side = jax.ShapeDtypeStruct((side_sizes()[2], channels), BF)
     return pl.pallas_call(
         sides_kernel,
-        out_shape=[side, side, jax.ShapeDtypeStruct((2 * voxels + 16, channels), BF)],
+        out_shape=[side, side, jax.ShapeDtypeStruct((16, channels), BF)],
         in_specs=[smem, smem, vmem, vmem],
         out_specs=[vmem] * 3,
         scratch_shapes=[pltpu.VMEM((TE * TE, TE, channels), F32)],
@@ -282,27 +281,26 @@
 
 
 def backward_kernel(block_count, tiles, depth_ref, *refs):
-    own, rims = refs[:block_count], refs[block_count : 2 * block_count]
-    far_kernels = refs[2 * block_count : 2 * block_count + 2]
-    input_grad, kept, given = refs[2 * block_count + 2 : 2 * block_count + 5]
-    rest = list(refs[2 * block_count + 5 :])
+    own, up, below, above = (list(refs[at * block_count : (at + 1) * block_count]) for at in range(4))
+    own_table, far_first, far_second, input_grad, kept, given = refs[4 * block_count : 4 * block_count + 6]
+    rest = list(refs[4 * block_count + 6 :])
     channels = own[0].shape[-1]
 
     def take():
         return rest.pop(0)
 
-    volume, upstream, mask, lifted, result, grad_rows, first_kernel, second_kernel, near_own, sems = (
-        take() for _ in range(10)
+    volume, upstream, mask, lifted, result, grad_rows, first_kernel, second_kernel, near_own, near_up, sems = (
+        take() for _ in range(11)
     )
     fetches = [
         pltpu.make_async_copy(far, near, sems.at[at])
         for at, (far, near) in enumerate(
-            ((own[0], near_own), (far_kernels[0], first_kernel), (far_kernels[1], second_kernel))
+            ((own[0], near_own), (up[0], near_up), (far_first, first_kernel), (far_second, second_kernel))
         )
     ]
     for fetch in fetches:
         fetch.start()
-    own = (near_own,) + own[1:]
+    own[0], up[0] = near_own, near_up
     regions = []
     for number in range(tiles):
         halo = HALO - number
@@ -321,23 +319,25 @@
     volume[...] = jnp.zeros_like(volume)
     upstream[...] = jnp.zeros_like(upstream)
     mask[...] = jnp.zeros_like(mask)
-    face, thin, side_rows = side_sizes()
+    face, thin, _ = side_sizes()
 
     def table_at(block, first):
         table = block[first : first + 16].astype(F32)
         place = lax.broadcasted_iota(jnp.int32, table.shape, 0)
         return [jnp.max(jnp.where(place == slot, table, 0.0)).astype(jnp.int32) for slot in slots]
 
+    held = table_at(own_table, 0)
+    codes = table_at(below[0], face + thin)
+    place_slots(codes, below, 0, 0, HALO, lifted, volume, mask, 0)
+    place_slots(codes, below, face, HALO - 2, 2, lifted, upstream, None, 0)
+    codes = table_at(above[0], face + thin)
+    place_slots(codes, above, 0, HALO + TE, HALO, lifted, volume, mask, 2)
+    place_slots(codes, above, face, HALO + TE, 2, lifted, upstream, None, 2)
+
     fetches[0].wait()
-    held = table_at(own[0], 2 * voxels)
     place_slots(held, own, 0, HALO, TE, lifted, volume, mask, 1)
-    place_slots(held, own, voxels, HALO, TE, lifted, upstream, None, 1)
-    codes = table_at(rims[0], face + thin)
-    place_slots(codes, rims, 0, 0, HALO, lifted, volume, mask, 0)
-    place_slots(codes, rims, face, HALO - 2, 2, lifted, upstream, None, 0)
-    codes = table_at(rims[0], side_rows + face + thin)
-    place_slots(codes, rims, side_rows, HALO + TE, HALO, lifted, volume, mask, 2)
-    place_slots(codes, rims, side_rows + face, HALO + TE, 2, lifted, upstream, None, 2)
+    fetches[1].wait()
+    place_slots(held, up, 0, HALO, TE, lifted, upstream, None, 1)
 
     starts = []
     alive = []
@@ -400,21 +400,21 @@
                     lane = (y_tap * 3 + x_tap) * channels
                     row = (z_tap * 9 + x_tap * 3 + y_tap) * channels
                     grad_rows[row : row + channels] = product[:, lane : lane + channels].T
-        y_parts, z_parts, _, padded, _ = kept.shape
-        share = 27 * channels // (y_parts * z_parts * block_count)
-        for y_at in range(y_parts):
-            for z_at in range(z_parts):
-                column = (z_at * y_parts + y_at) * block_count
+        near_parts, far_parts, _, padded, _ = kept.shape
+        share = 27 * channels // (near_parts * far_parts * block_count)
+        for near_at in range(near_parts):
+            for far_at in range(far_parts):
+                column = (far_at * near_parts + near_at) * block_count
                 for out, owner in ((kept, me), (given, me ^ 1)):
                     rows = grad_rows[pl.ds((column + owner) * share, padded)]
-                    out[y_at, z_at, at] = rows.astype(BF)
+                    out[near_at, far_at, at] = rows.astype(BF)
 
     grad_rows[27 * channels :] = jnp.zeros_like(grad_rows[27 * channels :])
-    fetches[1].wait()
+    fetches[2].wait()
     for number in range(tiles):
         convolve_region(regions[number][0], first_kernel, False, result)
         finish_layer(number, 1, "act")
-    fetches[2].wait()
+    fetches[3].wait()
     for number in range(tiles):
         convolve_region(regions[number][1], second_kernel, False, result)
         finish_layer(number, 2, "delta_two")
@@ -430,10 +430,10 @@
             value = value.reshape(TE, TE, channels)
             for z_at in range(TE):
                 lifted[pl.ds(z_at * TE * TE + 2 * pair + parity, TE, stride=TE)] = value[z_at]
-    input_grad[...] = lifted[...].astype(BF)
-
-
-def backward_call(own, rims, kernels, depth_at, columns, positions, tiles):
+    input_grad[...] = lifted[0:voxels].astype(BF)
+
+
+def backward_call(own, up, below, above, own_table, kernels, depth_at, columns, positions, tiles):
     channels = own[0].shape[-1]
     voxels = TE * TE * TE
     planes = positions * TE + 2 * HALO
@@ -444,13 +444,14 @@
         pltpu.VMEM((planes, span, TE, channels), F32),
         pltpu.VMEM((planes, span, TE, channels), F32),
         pltpu.VMEM((3, planes, TE, channels), F32),
-        pltpu.VMEM((voxels, channels), F32),
+        pltpu.VMEM((voxels + 16, channels), F32),
         pltpu.VMEM((inner, inner, 2 * TE, 2 * channels), F32),
         pltpu.VMEM((27 * channels + 16, channels), F32),
         pltpu.VMEM((27, channels, channels), BF),
         pltpu.VMEM((27, channels, channels), BF),
-        pltpu.VMEM(own[0].shape, BF),
-        pltpu.SemaphoreType.DMA((3,)),
+        pltpu.VMEM((voxels, channels), BF),
+        pltpu.VMEM((voxels, channels), BF),
+        pltpu.SemaphoreType.DMA((4,)),
     ]
     for number in range(tiles):
         for layer in range(4):
@@ -466,16 +467,16 @@
     def body(*refs):
         backward_kernel(len(own), tiles, *refs)
 
-    share = jax.ShapeDtypeStruct((2, columns // 2, 2, padded, channels), BF)
+    share = jax.ShapeDtypeStruct((NEAR, columns // NEAR, 2, padded, channels), BF)
     return pl.pallas_call(
         body,
         out_shape=[jax.ShapeDtypeStruct((voxels, channels), BF), share, share],
-        in_specs=[smem, hbm] + [vmem] * (2 * len(own) - 1) + [hbm, hbm],
+        in_specs=[smem] + ([hbm] + [vmem] * (len(own) - 1)) * 2 + [vmem] * (len(below) + len(above) + 1) + [hbm, hbm],
         out_specs=[vmem] * 3,
         scratch_shapes=scratch,
         compiler_params=pltpu.CompilerParams(vmem_limit_bytes=VMEM_LIMIT),
         name="tile_backward",
-    )(depth_at.reshape(1), *own, *rims, *kernels)
+    )(depth_at.reshape(1), *own, *up, *below, *above, own_table, *kernels)
 
 
 def on_device_line(features, cotangent, first_kernel, second_kernel, slot_tile, slot_used):
@@ -486,18 +487,22 @@
     def swap(block, axis, bits):
         return lax.ppermute(block, axis, [(i, i ^ bits) for i in range(lax.axis_size(axis))])
 
-    to_above, to_below, own = sides_call(slot_tile, slot_used, features[0, 0], cotangent[0, 0])
-    own_far = swap(own, "depth", 2)
+    own, up = features[0, 0], cotangent[0, 0]
+    own_far, up_far = swap(own, "depth", 2), swap(up, "depth", 2)
+    to_above, to_below, own_table = sides_call(slot_tile, slot_used, own, up)
+    to_below, own_far = lax.optimization_barrier((to_below, own_far))
     below, above = from_behind(to_above, "space", 1), from_behind(to_below, "space", -1)
-    rim = jnp.concatenate([below, above], axis=0)
-    rim_far = swap(rim, "depth", 2)
+    below_far, above_far = swap(below, "depth", 2), swap(above, "depth", 2)
 
     def with_sibling(near, far):
         return [near, swap(near, "depth", 1), far, swap(far, "depth", 1)]
 
     input_grad, kept, given = backward_call(
         with_sibling(own, own_far),
-        with_sibling(rim, rim_far),
+        with_sibling(up, up_far),
+        with_sibling(below, below_far),
+        with_sibling(above, above_far),
+        own_table,
         (first_kernel, second_kernel),
         depth_at,
         space_size,
@@ -509,12 +514,14 @@
     def part(block, at):
         return lax.dynamic_index_in_dim(block, at, 0, keepdims=False)
 
-    y_at, z_at = space_at % 2, space_at // 2
+    near_at, far_at = space_at % NEAR, space_at // NEAR
     column_sum = kept.astype(F32) + swap(given, "depth", 1).astype(F32)
-    line = part(column_sum, y_at) + swap(part(column_sum, 1 - y_at).astype(BF), "space", 1).astype(F32)
-    total = part(line, z_at)
-    for step in range(1, space_size // 2):
-        total = total + swap(part(line, z_at ^ step).astype(BF), "space", 2 * step).astype(F32)
+    group = part(column_sum, near_at)
+    for step in range(1, NEAR):
+        group = group + swap(part(column_sum, near_at ^ step).astype(BF), "space", step).astype(F32)
+    total = part(group, far_at)
+    for step in range(1, space_size // NEAR):
+        total = total + swap(part(group, far_at ^ step).astype(BF), "space", NEAR * step).astype(F32)
     first_share, second_share = (total[at, :share].reshape(-1) for at in range(2))
     return (input_grad.reshape(features.shape), first_share, second_share)
 

time: 59.3 us -> 56.7 us (0.956)
  waiting for transfers between devices: 23.4 us -> 16.6 us
  starting transfers between devices: 16.2 us -> 19.6 us
  Pallas kernels: 18 us -> 18.6 us
    ppermute x11 -> x17, waiting for transfers between devices: 17.9 us -> 13.2 us  [swap(): lax.ppermute(block, axis, [(i, i ^ bits) for i in range(lax.axis_size(axi...]
    ppermute x11 -> x17, starting transfers between devices: 9.9 us -> 14.5 us  [swap(): lax.ppermute(block, axis, [(i, i ^ bits) for i in range(lax.axis_size(axi...]
    ppermute x2, waiting for transfers between devices: 5.44 us -> 3.38 us  [from_behind(): return lax.ppermute(block, axis, route)]
    ppermute x2, starting transfers between devices: 6.28 us -> 5.12 us  [from_behind(): return lax.ppermute(block, axis, route)]
    pallas_call x1, Pallas kernels: 16.2 us -> 16.9 us  [backward_call(): pl.pallas_call(body, out_shape=[jax.ShapeDtypeStruct((voxels, channels),...]
  transfers between devices with their start and end apart: 13 -> 19, of which waited for: 7 -> 9; matrix products, arithmetic and copies ran while one was open for 0% -> 0% of each run, Pallas kernels for 0% -> 3%
where the time goes in v4:
time: 56.7 us; the launch traced here: 56.5 us
  starting transfers between devices  19.6 us (35%)
  Pallas kernels  18.6 us (33%)
  waiting for transfers between devices  16.6 us (29%)
  between operations  0.76 us (1%)
  local copies, waits for them, and re-layouts  0.73 us (1%)
    pallas_call x1, Pallas kernels, backward_call(): pl.pallas_call(body, out_shape=[jax.ShapeDtypeStruct((voxels, channels),...  16.9 us
    ppermute x17, starting transfers between devices, swap(): lax.ppermute(block, axis, [(i, i ^ bits) for i in range(lax.axis_size(axi...  14.5 us
    ppermute x17, waiting for transfers between devices, swap(): lax.ppermute(block, axis, [(i, i ^ bits) for i in range(lax.axis_size(axi...  13.2 us
    ppermute x2, starting transfers between devices, from_behind(): return lax.ppermute(block, axis, route)  5.12 us
    ppermute x2, waiting for transfers between devices, from_behind(): return lax.ppermute(block, axis, route)  3.38 us
    pallas_call x1, Pallas kernels, sides_call(): pl.pallas_call(sides_kernel, out_shape=[side, side, jax.ShapeDtypeStruct(...  1.75 us
  transfers between devices with their start and end apart: 19, of which 9 were waited for; matrix products, arithmetic and copies ran while one was open for 0% of the time, Pallas kernels for 3%

profile of v4, /device:TPU:0, one launch (start us, length us, event | category | flops | bytes accessed | tf_op | source)
XLA Modules:
  0.0 56.5 jit_solution(16125305416453272175)
XLA Ops:
  0.6 3.0 %collective-permute-start.1 = (bf16[512,128]{1,0:T(8,128)(2,1)}, bf16[512,128]{1,0:T(8,128)(2,1)S(1)}, u32[]{:S(2)}, u32[]{:S(2)}) collective-permute-start(bf16[512,128]{1,0:T(8,128)(2,1)} %bitcast.24), channel_id=1, source_target_pairs={{0,2},{1,3},{2,0},{3,1},{4,6},{5,7},{6,4},{7,5},{8,10},{9,11},{10,... | collective-permute-start | bytes 393224 | tf_op jit(solution)/shard_map/ppermute | solution.py:488
  3.6 0.0 copy-start
  3.6 0.1 collective-permute-start.4
  3.7 1.8 %pack_sides.1 = (bf16[400,128]{1,0:T(8,128)(2,1)}, bf16[400,128]{1,0:T(8,128)(2,1)}, bf16[16,128]{1,0:T(8,128)(2,1)}) custom-call(s32[1,4]{1,0:T(1,128)} %tile.1, s32[1,4]{1,0:T(1,128)} %used.1, bf16[512,128]{1,0:T(8,128)(2,1)} %bitcast.25, bf16[512,128]{1,0:T(8,128)(2,1)} %bitcast.29), custom_call_target="tpu_custom_call" | custom-call | tf_op jit(solution)/shard_map/pack_sides/pallas_call | solution.py:273
  5.5 3.8 %collective-permute-start.6 = (bf16[400,128]{1,0:T(8,128)(2,1)}, bf16[400,128]{1,0:T(8,128)(2,1)S(1)}, u32[]{:S(2)}, u32[]{:S(2)}) collective-permute-start(bf16[400,128]{1,0:T(8,128)(2,1)} %get-tuple-element.13), channel_id=1, source_target_pairs={{0,4},{4,8},{8,12},{12,16},{16,20},{20,24},{24,28},{1,5},{5,9},{9,... | collective-permute-start | bytes 307208 | tf_op jit(solution)/shard_map/ppermute | solution.py:19
  9.3 0.0 collective-permute-done.1.refs_3_
  9.3 1.3 %collective-permute-start.10 = (bf16[400,128]{1,0:T(8,128)(2,1)}, bf16[400,128]{1,0:T(8,128)(2,1)S(1)}, u32[]{:S(2)}, u32[]{:S(2)}) collective-permute-start(bf16[400,128]{1,0:T(8,128)(2,1)} %get-tuple-element.14), channel_id=1, source_target_pairs={{4,0},{8,4},{12,8},{16,12},{20,16},{24,20},{28,24},{5,1},{9,5},{13... | collective-permute-start | bytes 307208 | tf_op jit(solution)/shard_map/ppermute | solution.py:19
  10.6 0.0 copy-done
  10.6 0.1 collective-permute-start
  10.7 0.0 copy-done.1
  10.7 0.5 collective-permute-start.3
  11.2 0.6 %collective-permute-done.6.refs_9_ = bf16[400,128]{1,0:T(8,128)(2,1)S(1)} collective-permute-done((bf16[400,128]{1,0:T(8,128)(2,1)}, bf16[400,128]{1,0:T(8,128)(2,1)S(1)}, u32[]{:S(2)}, u32[]{:S(2)}) %collective-permute-start.6) | collective-permute-done | bytes 102432 | tf_op jit(solution)/shard_map/ppermute | solution.py:19
  11.9 1.5 %collective-permute-start.8 = (bf16[400,128]{1,0:T(8,128)(2,1)S(1)}, bf16[400,128]{1,0:T(8,128)(2,1)S(1)}, u32[]{:S(2)}, u32[]{:S(2)}) collective-permute-start(bf16[400,128]{1,0:T(8,128)(2,1)S(1)} %collective-permute-done.6.refs_9_), channel_id=1, source_target_pairs={{0,2},{1,3},{2,0},{3,1},{4,6},{5,7},{6,4},{7,5},{8,10},{9,11},{10,... | collective-permute-start | bytes 307208 | tf_op jit(solution)/shard_map/ppermute | solution.py:488
  13.4 0.0 collective-permute-done.4.refs_7_
  13.4 0.0 collective-permute-start.7
  13.4 2.7 %collective-permute-done.10.refs_13_ = bf16[400,128]{1,0:T(8,128)(2,1)S(1)} collective-permute-done((bf16[400,128]{1,0:T(8,128)(2,1)}, bf16[400,128]{1,0:T(8,128)(2,1)S(1)}, u32[]{:S(2)}, u32[]{:S(2)}) %collective-permute-start.10) | collective-permute-done | bytes 102432 | tf_op jit(solution)/shard_map/ppermute | solution.py:19
  16.1 1.5 %collective-permute-start.12 = (bf16[400,128]{1,0:T(8,128)(2,1)S(1)}, bf16[400,128]{1,0:T(8,128)(2,1)S(1)}, u32[]{:S(2)}, u32[]{:S(2)}) collective-permute-start(bf16[400,128]{1,0:T(8,128)(2,1)S(1)} %collective-permute-done.10.refs_13_), channel_id=1, source_target_pairs={{0,2},{1,3},{2,0},{3,1},{4,6},{5,7},{6,4},{7,5},{8,10},{9,11},{10,... | collective-permute-start | bytes 307208 | tf_op jit(solution)/shard_map/ppermute | solution.py:488
  17.6 0.0 collective-permute-done.refs_2_
  17.6 0.0 collective-permute-start.2
  17.6 0.0 collective-permute-done.3.refs_6_
  17.6 0.5 collective-permute-start.5
  18.1 0.0 collective-permute-done.8.refs_11_
  18.1 0.1 collective-permute-start.9
  18.2 0.0 collective-permute-done.7.refs_10_
  18.2 0.4 collective-permute-start.11
  18.6 2.1 %collective-permute-done.12.refs_15_ = bf16[400,128]{1,0:T(8,128)(2,1)S(1)} collective-permute-done((bf16[400,128]{1,0:T(8,128)(2,1)S(1)}, bf16[400,128]{1,0:T(8,128)(2,1)S(1)}, u32[]{:S(2)}, u32[]{:S(2)}) %collective-permute-start.12) | collective-permute-done | bytes 102432 | tf_op jit(solution)/shard_map/ppermute | solution.py:488
  20.8 0.0 collective-permute-start.13
  20.8 0.0 collective-permute-done.2.refs_4_
  20.8 0.0 collective-permute-done.5.refs_8_
  20.8 0.0 collective-permute-done.9.refs_12_
  20.8 0.0 collective-permute-done.11.refs_14_
  20.8 1.3 %collective-permute-done.13.refs_16_ = bf16[400,128]{1,0:T(8,128)(2,1)S(1)} collective-permute-done((bf16[400,128]{1,0:T(8,128)(2,1)S(1)}, bf16[400,128]{1,0:T(8,128)(2,1)S(1)}, u32[]{:S(2)}, u32[]{:S(2)}) %collective-permute-start.13) | collective-permute-done | bytes 102432 | tf_op jit(solution)/shard_map/ppermute | solution.py:488
  22.1 0.0 copy-done.2
  22.1 16.9 %tile_backward.1 = (bf16[512,128]{1,0:T(8,128)(2,1)}, bf16[4,2,2,112,128]{4,3,2,1,0:T(8,128)(2,1)S(1)}, bf16[4,2,2,112,128]{4,3,2,1,0:T(8,128)(2,1)S(1)}) custom-call(s32[1]{0:T(128)} %bitcast.refs_0_, bf16[512,128]{1,0:T(8,128)(2,1)S(1)} %bitcast.27, bf16[512,128]{1,0:T(8,128)(2,1)S(1)} %collective-permute-done.refs_2_, ...), custom_call_target="tpu_custom_call" | custom-call | tf_op jit(solution)/shard_map/tile_backward/pallas_call | solution.py:471
  38.9 0.2 collective-permute-start.14
  39.1 1.7 %collective-permute-done.14 = bf16[4,2,2,112,128]{4,3,2,1,0:T(8,128)(2,1)S(1)} collective-permute-done((bf16[4,2,2,112,128]{4,3,2,1,0:T(8,128)(2,1)S(1)}, bf16[4,2,2,112,128]{4,3,2,1,0:T(8,128)(2,1)S(1)}, u32[]{:S(2)}, u32[]{:S(2)}) %collective-permute-start.14) | collective-permute-done | bytes 458784 | tf_op jit(solution)/shard_map/ppermute | solution.py:488
  40.8 0.1 convert_add_fusion
  40.9 0.1 fusion.2
  41.0 2.4 %collective-permute-start.15 = (bf16[2,2,112,128]{3,2,1,0:T(8,128)(2,1)S(1)}, bf16[2,2,112,128]{3,2,1,0:T(8,128)(2,1)S(1)}, u32[]{:S(2)}, u32[]{:S(2)}) collective-permute-start(bf16[2,2,112,128]{3,2,1,0:T(8,128)(2,1)S(1)} %get-tuple-element.19), channel_id=1, source_target_pairs={{0,4},{4,0},{8,12},{12,8},{16,20},{20,16},{24,28},{28,24},{1,5},{5... | collective-permute-start | bytes 344072 | tf_op jit(solution)/shard_map/ppermute | solution.py:488
  43.4 1.5 %collective-permute-start.16 = (bf16[2,2,112,128]{3,2,1,0:T(8,128)(2,1)S(1)}, bf16[2,2,112,128]{3,2,1,0:T(8,128)(2,1)S(1)}, u32[]{:S(2)}, u32[]{:S(2)}) collective-permute-start(bf16[2,2,112,128]{3,2,1,0:T(8,128)(2,1)S(1)} %get-tuple-element.21), channel_id=1, source_target_pairs={{0,8},{4,12},{8,0},{12,4},{16,24},{20,28},{24,16},{28,20},{1,9},{5... | collective-permute-start | bytes 344072 | tf_op jit(solution)/shard_map/ppermute | solution.py:488
  44.9 0.0 collective-permute-start.17
  44.9 1.9 %collective-permute-done.15 = bf16[2,2,112,128]{3,2,1,0:T(8,128)(2,1)S(1)} collective-permute-done((bf16[2,2,112,128]{3,2,1,0:T(8,128)(2,1)S(1)}, bf16[2,2,112,128]{3,2,1,0:T(8,128)(2,1)S(1)}, u32[]{:S(2)}, u32[]{:S(2)}) %collective-permute-start.15) | collective-permute-done | bytes 114720 | tf_op jit(solution)/shard_map/ppermute | solution.py:488
  46.8 2.6 %collective-permute-done.16 = bf16[2,2,112,128]{3,2,1,0:T(8,128)(2,1)S(1)} collective-permute-done((bf16[2,2,112,128]{3,2,1,0:T(8,128)(2,1)S(1)}, bf16[2,2,112,128]{3,2,1,0:T(8,128)(2,1)S(1)}, u32[]{:S(2)}, u32[]{:S(2)}) %collective-permute-start.16) | collective-permute-done | bytes 114720 | tf_op jit(solution)/shard_map/ppermute | solution.py:488
  49.4 1.2 %collective-permute-done.17 = bf16[2,2,112,128]{3,2,1,0:T(8,128)(2,1)S(1)} collective-permute-done((bf16[2,2,112,128]{3,2,1,0:T(8,128)(2,1)S(1)}, bf16[2,2,112,128]{3,2,1,0:T(8,128)(2,1)S(1)}, u32[]{:S(2)}, u32[]{:S(2)}) %collective-permute-start.17) | collective-permute-done | bytes 114720 | tf_op jit(solution)/shard_map/ppermute | solution.py:488
  50.6 0.1 fusion.1
  50.7 2.7 %collective-permute-start.18 = (bf16[2,112,128]{2,1,0:T(8,128)(2,1)S(1)}, bf16[2,112,128]{2,1,0:T(8,128)(2,1)S(1)}, u32[]{:S(2)}, u32[]{:S(2)}) collective-permute-start(bf16[2,112,128]{2,1,0:T(8,128)(2,1)S(1)} %fusion.5), channel_id=1, source_target_pairs={{0,16},{4,20},{8,24},{12,28},{16,0},{20,4},{24,8},{28,12},{1,17},{... | collective-permute-start | bytes 172040 | tf_op jit(solution)/shard_map/ppermute | solution.py:488
  53.4 2.4 %collective-permute-done.18 = bf16[2,112,128]{2,1,0:T(8,128)(2,1)S(1)} collective-permute-done((bf16[2,112,128]{2,1,0:T(8,128)(2,1)S(1)}, bf16[2,112,128]{2,1,0:T(8,128)(2,1)S(1)}, u32[]{:S(2)}, u32[]{:S(2)}) %collective-permute-start.18) | collective-permute-done | bytes 57376 | tf_op jit(solution)/shard_map/ppermute | solution.py:488
  55.8 0.6 %slice_bitcast_fusion = (f32[13824]{0:T(1024)}, f32[13824]{0:T(1024)}) fusion(f32[2,112,128]{2,1,0:T(8,128)S(1)} %bitcast_add_fusion.1), kind=kLoop, calls=%fused_computation.13 | loop fusion | bytes 221184 | tf_op jit(solution)/shard_map/reshape;squeeze | solution.py:525
  (4 shorter events, 0.0 us)
Async XLA Ops:
  0.6 8.7 %collective-permute-start.1 = (bf16[512,128]{1,0:T(8,128)(2,1)}, bf16[512,128]{1,0:T(8,128)(2,1)S(1)}, u32[]{:S(2)}, u32[]{:S(2)}) collective-permute-start(bf16[512,128]{1,0:T(8,128)(2,1)} %bitcast.24), channel_id=1, source_target_pairs={{0,2},{1,3},{2,0},{3,1},{4,6},{5,7},{6,4},{7,5},{8,10},{9,11},{10,... | collective-permute-start | bytes 393224 | tf_op jit(solution)/shard_map/ppermute | solution.py:488
  3.6 7.0 %copy-start = (bf16[1,1,512,128]{3,2,1,0:T(8,128)(2,1)S(1)}, bf16[1,1,512,128]{3,2,1,0:T(8,128)(2,1)}, u32[]{:S(2)}) copy-start(bf16[1,1,512,128]{3,2,1,0:T(8,128)(2,1)} %param.6) | copy-start | bytes 393220
  3.6 7.1 %copy-start.1 = (bf16[1,1,512,128]{3,2,1,0:T(8,128)(2,1)S(1)}, bf16[1,1,512,128]{3,2,1,0:T(8,128)(2,1)}, u32[]{:S(2)}) copy-start(bf16[1,1,512,128]{3,2,1,0:T(8,128)(2,1)} %param.7) | copy-start | bytes 393220
  3.6 9.7 %collective-permute-start.4 = (bf16[512,128]{1,0:T(8,128)(2,1)}, bf16[512,128]{1,0:T(8,128)(2,1)S(1)}, u32[]{:S(2)}, u32[]{:S(2)}) collective-permute-start(bf16[512,128]{1,0:T(8,128)(2,1)} %bitcast.28), channel_id=1, source_target_pairs={{0,2},{1,3},{2,0},{3,1},{4,6},{5,7},{6,4},{7,5},{8,10},{9,11},{10,... | collective-permute-start | bytes 393224 | tf_op jit(solution)/shard_map/ppermute | solution.py:488
  5.5 6.4 %collective-permute-start.6 = (bf16[400,128]{1,0:T(8,128)(2,1)}, bf16[400,128]{1,0:T(8,128)(2,1)S(1)}, u32[]{:S(2)}, u32[]{:S(2)}) collective-permute-start(bf16[400,128]{1,0:T(8,128)(2,1)} %get-tuple-element.13), channel_id=1, source_target_pairs={{0,4},{4,8},{8,12},{12,16},{16,20},{20,24},{24,28},{1,5},{5,9},{9,... | collective-permute-start | bytes 307208 | tf_op jit(solution)/shard_map/ppermute | solution.py:19
  9.3 6.8 %collective-permute-start.10 = (bf16[400,128]{1,0:T(8,128)(2,1)}, bf16[400,128]{1,0:T(8,128)(2,1)S(1)}, u32[]{:S(2)}, u32[]{:S(2)}) collective-permute-start(bf16[400,128]{1,0:T(8,128)(2,1)} %get-tuple-element.14), channel_id=1, source_target_pairs={{4,0},{8,4},{12,8},{16,12},{20,16},{24,20},{28,24},{5,1},{9,5},{13... | collective-permute-start | bytes 307208 | tf_op jit(solution)/shard_map/ppermute | solution.py:19
  10.6 6.9 %collective-permute-start = (bf16[512,128]{1,0:T(8,128)(2,1)S(1)}, bf16[512,128]{1,0:T(8,128)(2,1)S(1)}, u32[]{:S(2)}, u32[]{:S(2)}) collective-permute-start(bf16[512,128]{1,0:T(8,128)(2,1)S(1)} %bitcast.26), channel_id=1, source_target_pairs={{0,1},{1,0},{2,3},{3,2},{4,5},{5,4},{6,7},{7,6},{8,9},{9,8},{10,11... | collective-permute-start | bytes 393224 | tf_op jit(solution)/shard_map/ppermute | solution.py:488
  10.7 6.9 %collective-permute-start.3 = (bf16[512,128]{1,0:T(8,128)(2,1)S(1)}, bf16[512,128]{1,0:T(8,128)(2,1)S(1)}, u32[]{:S(2)}, u32[]{:S(2)}) collective-permute-start(bf16[512,128]{1,0:T(8,128)(2,1)S(1)} %bitcast.30), channel_id=1, source_target_pairs={{0,1},{1,0},{2,3},{3,2},{4,5},{5,4},{6,7},{7,6},{8,9},{9,8},{10,11... | collective-permute-start | bytes 393224 | tf_op jit(solution)/shard_map/ppermute | solution.py:488
  11.9 6.2 %collective-permute-start.8 = (bf16[400,128]{1,0:T(8,128)(2,1)S(1)}, bf16[400,128]{1,0:T(8,128)(2,1)S(1)}, u32[]{:S(2)}, u32[]{:S(2)}) collective-permute-start(bf16[400,128]{1,0:T(8,128)(2,1)S(1)} %collective-permute-done.6.refs_9_), channel_id=1, source_target_pairs={{0,2},{1,3},{2,0},{3,1},{4,6},{5,7},{6,4},{7,5},{8,10},{9,11},{10,... | collective-permute-start | bytes 307208 | tf_op jit(solution)/shard_map/ppermute | solution.py:488
  13.4 4.8 %collective-permute-start.7 = (bf16[400,128]{1,0:T(8,128)(2,1)S(1)}, bf16[400,128]{1,0:T(8,128)(2,1)S(1)}, u32[]{:S(2)}, u32[]{:S(2)}) collective-permute-start(bf16[400,128]{1,0:T(8,128)(2,1)S(1)} %collective-permute-done.6.refs_9_), channel_id=1, source_target_pairs={{0,1},{1,0},{2,3},{3,2},{4,5},{5,4},{6,7},{7,6},{8,9},{9,8},{10,11... | collective-permute-start | bytes 307208 | tf_op jit(solution)/shard_map/ppermute | solution.py:488
  16.1 4.7 %collective-permute-start.12 = (bf16[400,128]{1,0:T(8,128)(2,1)S(1)}, bf16[400,128]{1,0:T(8,128)(2,1)S(1)}, u32[]{:S(2)}, u32[]{:S(2)}) collective-permute-start(bf16[400,128]{1,0:T(8,128)(2,1)S(1)} %collective-permute-done.10.refs_13_), channel_id=1, source_target_pairs={{0,2},{1,3},{2,0},{3,1},{4,6},{5,7},{6,4},{7,5},{8,10},{9,11},{10,... | collective-permute-start | bytes 307208 | tf_op jit(solution)/shard_map/ppermute | solution.py:488
  17.6 3.2 %collective-permute-start.2 = (bf16[512,128]{1,0:T(8,128)(2,1)S(1)}, bf16[512,128]{1,0:T(8,128)(2,1)S(1)}, u32[]{:S(2)}, u32[]{:S(2)}) collective-permute-start(bf16[512,128]{1,0:T(8,128)(2,1)S(1)} %collective-permute-done.1.refs_3_), channel_id=1, source_target_pairs={{0,1},{1,0},{2,3},{3,2},{4,5},{5,4},{6,7},{7,6},{8,9},{9,8},{10,11... | collective-permute-start | bytes 393224 | tf_op jit(solution)/shard_map/ppermute | solution.py:488
  17.6 3.2 %collective-permute-start.5 = (bf16[512,128]{1,0:T(8,128)(2,1)S(1)}, bf16[512,128]{1,0:T(8,128)(2,1)S(1)}, u32[]{:S(2)}, u32[]{:S(2)}) collective-permute-start(bf16[512,128]{1,0:T(8,128)(2,1)S(1)} %collective-permute-done.4.refs_7_), channel_id=1, source_target_pairs={{0,1},{1,0},{2,3},{3,2},{4,5},{5,4},{6,7},{7,6},{8,9},{9,8},{10,11... | collective-permute-start | bytes 393224 | tf_op jit(solution)/shard_map/ppermute | solution.py:488
  18.1 2.7 %collective-permute-start.9 = (bf16[400,128]{1,0:T(8,128)(2,1)S(1)}, bf16[400,128]{1,0:T(8,128)(2,1)S(1)}, u32[]{:S(2)}, u32[]{:S(2)}) collective-permute-start(bf16[400,128]{1,0:T(8,128)(2,1)S(1)} %collective-permute-done.8.refs_11_), channel_id=1, source_target_pairs={{0,1},{1,0},{2,3},{3,2},{4,5},{5,4},{6,7},{7,6},{8,9},{9,8},{10,11... | collective-permute-start | bytes 307208 | tf_op jit(solution)/shard_map/ppermute | solution.py:488
  18.2 2.6 %collective-permute-start.11 = (bf16[400,128]{1,0:T(8,128)(2,1)S(1)}, bf16[400,128]{1,0:T(8,128)(2,1)S(1)}, u32[]{:S(2)}, u32[]{:S(2)}) collective-permute-start(bf16[400,128]{1,0:T(8,128)(2,1)S(1)} %collective-permute-done.10.refs_13_), channel_id=1, source_target_pairs={{0,1},{1,0},{2,3},{3,2},{4,5},{5,4},{6,7},{7,6},{8,9},{9,8},{10,11... | collective-permute-start | bytes 307208 | tf_op jit(solution)/shard_map/ppermute | solution.py:488
  20.8 1.3 %collective-permute-start.13 = (bf16[400,128]{1,0:T(8,128)(2,1)S(1)}, bf16[400,128]{1,0:T(8,128)(2,1)S(1)}, u32[]{:S(2)}, u32[]{:S(2)}) collective-permute-start(bf16[400,128]{1,0:T(8,128)(2,1)S(1)} %collective-permute-done.12.refs_15_), channel_id=1, source_target_pairs={{0,1},{1,0},{2,3},{3,2},{4,5},{5,4},{6,7},{7,6},{8,9},{9,8},{10,11... | collective-permute-start | bytes 307208 | tf_op jit(solution)/shard_map/ppermute | solution.py:488
  20.8 1.3 %copy-start.2 = (bf16[16,128]{1,0:T(8,128)(2,1)S(1)}, bf16[16,128]{1,0:T(8,128)(2,1)}, u32[]{:S(2)}) copy-start(bf16[16,128]{1,0:T(8,128)(2,1)} %get-tuple-element.15.refs_17_) | copy-start | bytes 12292
  38.9 1.9 %collective-permute-start.14 = (bf16[4,2,2,112,128]{4,3,2,1,0:T(8,128)(2,1)S(1)}, bf16[4,2,2,112,128]{4,3,2,1,0:T(8,128)(2,1)S(1)}, u32[]{:S(2)}, u32[]{:S(2)}) collective-permute-start(bf16[4,2,2,112,128]{4,3,2,1,0:T(8,128)(2,1)S(1)} %get-tuple-element.18), channel_id=1, source_target_pairs={{0,1},{1,0},{2,3},{3,2},{4,5},{5,4},{6,7},{7,6},{8,9},{9,8},{10,11... | collective-permute-start | bytes 1376264 | tf_op jit(solution)/shard_map/ppermute | solution.py:488
  41.0 5.8 %collective-permute-start.15 = (bf16[2,2,112,128]{3,2,1,0:T(8,128)(2,1)S(1)}, bf16[2,2,112,128]{3,2,1,0:T(8,128)(2,1)S(1)}, u32[]{:S(2)}, u32[]{:S(2)}) collective-permute-start(bf16[2,2,112,128]{3,2,1,0:T(8,128)(2,1)S(1)} %get-tuple-element.19), channel_id=1, source_target_pairs={{0,4},{4,0},{8,12},{12,8},{16,20},{20,16},{24,28},{28,24},{1,5},{5... | collective-permute-start | bytes 344072 | tf_op jit(solution)/shard_map/ppermute | solution.py:488
  43.4 6.0 %collective-permute-start.16 = (bf16[2,2,112,128]{3,2,1,0:T(8,128)(2,1)S(1)}, bf16[2,2,112,128]{3,2,1,0:T(8,128)(2,1)S(1)}, u32[]{:S(2)}, u32[]{:S(2)}) collective-permute-start(bf16[2,2,112,128]{3,2,1,0:T(8,128)(2,1)S(1)} %get-tuple-element.21), channel_id=1, source_target_pairs={{0,8},{4,12},{8,0},{12,4},{16,24},{20,28},{24,16},{28,20},{1,9},{5... | collective-permute-start | bytes 344072 | tf_op jit(solution)/shard_map/ppermute | solution.py:488
  44.9 5.7 %collective-permute-start.17 = (bf16[2,2,112,128]{3,2,1,0:T(8,128)(2,1)S(1)}, bf16[2,2,112,128]{3,2,1,0:T(8,128)(2,1)S(1)}, u32[]{:S(2)}, u32[]{:S(2)}) collective-permute-start(bf16[2,2,112,128]{3,2,1,0:T(8,128)(2,1)S(1)} %get-tuple-element.20), channel_id=1, source_target_pairs={{0,12},{4,8},{8,4},{12,0},{16,28},{20,24},{24,20},{28,16},{1,13},{... | collective-permute-start | bytes 344072 | tf_op jit(solution)/shard_map/ppermute | solution.py:488
  50.7 5.1 %collective-permute-start.18 = (bf16[2,112,128]{2,1,0:T(8,128)(2,1)S(1)}, bf16[2,112,128]{2,1,0:T(8,128)(2,1)S(1)}, u32[]{:S(2)}, u32[]{:S(2)}) collective-permute-start(bf16[2,112,128]{2,1,0:T(8,128)(2,1)S(1)} %fusion.5), channel_id=1, source_target_pairs={{0,16},{4,20},{8,24},{12,28},{16,0},{20,4},{24,8},{28,12},{1,17},{... | collective-permute-start | bytes 172040 | tf_op jit(solution)/shard_map/ppermute | solution.py:488

commit v5 on v4

--- a/solution.py
+++ b/solution.py
@@ -154,6 +154,7 @@
 
 HALO = 4
 NEAR = 4
+INPUT_VMEM = 16 * 1024 * 1024
 VMEM_LIMIT = 51 * 1024 * 1024
 BF = jnp.bfloat16
 F32 = jnp.float32
@@ -280,9 +281,15 @@
     )(slot_tile, slot_used, feature_rows, upstream_rows)
 
 
+def table_at(block, first, slots):
+    table = block[first : first + 16].astype(F32)
+    place = lax.broadcasted_iota(jnp.int32, table.shape, 0)
+    return [jnp.max(jnp.where(place == slot, table, 0.0)).astype(jnp.int32) for slot in slots]
+
+
 def backward_kernel(block_count, tiles, depth_ref, *refs):
     own, up, below, above = (list(refs[at * block_count : (at + 1) * block_count]) for at in range(4))
-    own_table, far_first, far_second, input_grad, kept, given = refs[4 * block_count : 4 * block_count + 6]
+    own_table, far_first, far_second, last, kept, given = refs[4 * block_count : 4 * block_count + 6]
     rest = list(refs[4 * block_count + 6 :])
     channels = own[0].shape[-1]
 
@@ -321,16 +328,11 @@
     mask[...] = jnp.zeros_like(mask)
     face, thin, _ = side_sizes()
 
-    def table_at(block, first):
-        table = block[first : first + 16].astype(F32)
-        place = lax.broadcasted_iota(jnp.int32, table.shape, 0)
-        return [jnp.max(jnp.where(place == slot, table, 0.0)).astype(jnp.int32) for slot in slots]
-
-    held = table_at(own_table, 0)
-    codes = table_at(below[0], face + thin)
+    held = table_at(own_table, 0, slots)
+    codes = table_at(below[0], face + thin, slots)
     place_slots(codes, below, 0, 0, HALO, lifted, volume, mask, 0)
     place_slots(codes, below, face, HALO - 2, 2, lifted, upstream, None, 0)
-    codes = table_at(above[0], face + thin)
+    codes = table_at(above[0], face + thin, slots)
     place_slots(codes, above, 0, HALO + TE, HALO, lifted, volume, mask, 2)
     place_slots(codes, above, face, HALO + TE, 2, lifted, upstream, None, 2)
 
@@ -422,15 +424,61 @@
     for number in range(tiles):
         convolve_region(regions[number][2], second_kernel, True, result)
         finish_layer(number, 3, "delta_one")
+    last[...] = regions[0][3].even[:, :, :, :, channels : 2 * channels]
     kernel_gradient(0, 0, 3)
-    convolve_region(regions[0][3], first_kernel, True, result)
+
+
+def input_kernel(depth_ref, own_table, last, far_first, input_grad, even, odd, lifted, result, first_kernel, sem):
+    fetch = pltpu.make_async_copy(far_first, first_kernel, sem.at[0])
+    fetch.start()
+    (held,) = table_at(own_table, 0, [depth_ref[0]])
+    alive = (held > 0).astype(F32)
+    channels = input_grad.shape[-1]
+    region = Region(even, odd, TE + 2, TE + 2)
+    for pair in range(region.y_size // 2):
+        for parity in range(2):
+            column = last[:, pair, parity].astype(F32)
+            region.store_row(pair, parity, column.reshape(region.z_size, TE, channels))
+    fetch.wait()
+    convolve_region(region, first_kernel, True, result)
     for pair in range(TE // 2):
         for parity in range(2):
-            value = result[0 : TE // 2, pair, :, parity * channels : (parity + 1) * channels] * alive[0]
+            value = result[:, pair, :, parity * channels : (parity + 1) * channels] * alive
             value = value.reshape(TE, TE, channels)
             for z_at in range(TE):
                 lifted[pl.ds(z_at * TE * TE + 2 * pair + parity, TE, stride=TE)] = value[z_at]
-    input_grad[...] = lifted[0:voxels].astype(BF)
+    input_grad[...] = lifted[0 : input_grad.shape[0]].astype(BF)
+
+
+def input_call(depth_at, own_table, last, first_kernel):
+    channels = first_kernel.shape[-1]
+    voxels = TE * TE * TE
+    vmem = pl.BlockSpec(memory_space=pltpu.VMEM)
+    return pl.pallas_call(
+        input_kernel,
+        out_shape=jax.ShapeDtypeStruct((voxels, channels), BF),
+        in_specs=[
+            pl.BlockSpec(memory_space=pltpu.SMEM),
+            vmem,
+            vmem,
+            pl.BlockSpec(memory_space=pltpu.HBM),
+        ],
+        out_specs=vmem,
+        scratch_shapes=region_shapes(TE + 2, TE + 2, TE, channels, True)
+        + [
+            pltpu.VMEM((voxels + 16, channels), F32),
+            pltpu.VMEM((TE // 2, TE // 2, 2 * TE, 2 * channels), F32),
+            pltpu.VMEM((27, channels, channels), BF),
+            pltpu.SemaphoreType.DMA((1,)),
+        ],
+        compiler_params=pltpu.CompilerParams(vmem_limit_bytes=INPUT_VMEM),
+        cost_estimate=pl.CostEstimate(
+            flops=2 * 36 * voxels * channels * channels,
+            bytes_accessed=2 * 27 * channels * channels + 8 * voxels * channels,
+            transcendentals=0,
+        ),
+        name="input_gradient",
+    )(depth_at.reshape(1), own_table, last, first_kernel)
 
 
 def backward_call(own, up, below, above, own_table, kernels, depth_at, columns, positions, tiles):
@@ -467,14 +515,24 @@
     def body(*refs):
         backward_kernel(len(own), tiles, *refs)
 
+    last = TE + 2
     share = jax.ShapeDtypeStruct((NEAR, columns // NEAR, 2, padded, channels), BF)
     return pl.pallas_call(
         body,
-        out_shape=[jax.ShapeDtypeStruct((voxels, channels), BF), share, share],
+        out_shape=[
+            jax.ShapeDtypeStruct((last // 2, last // 2, 2, 2 * TE, channels), BF),
+            share,
+            share,
+        ],
         in_specs=[smem] + ([hbm] + [vmem] * (len(own) - 1)) * 2 + [vmem] * (len(below) + len(above) + 1) + [hbm, hbm],
         out_specs=[vmem] * 3,
         scratch_shapes=scratch,
         compiler_params=pltpu.CompilerParams(vmem_limit_bytes=VMEM_LIMIT),
+        cost_estimate=pl.CostEstimate(
+            flops=40 * 27 * voxels * channels * channels,
+            bytes_accessed=100 * voxels * channels,
+            transcendentals=4 * voxels * channels,
+        ),
         name="tile_backward",
     )(depth_at.reshape(1), *own, *up, *below, *above, own_table, *kernels)
 
@@ -497,7 +555,7 @@
     def with_sibling(near, far):
         return [near, swap(near, "depth", 1), far, swap(far, "depth", 1)]
 
-    input_grad, kept, given = backward_call(
+    last, kept, given = backward_call(
         with_sibling(own, own_far),
         with_sibling(up, up_far),
         with_sibling(below, below_far),
@@ -509,6 +567,7 @@
         slot_tile.shape[1],
         2,
     )
+    input_grad = input_call(depth_at, own_table, last, first_kernel)
     share = 27 * channels // (depth_size * space_size)
 
     def part(block, at):

time: 56.7 us -> 55.1 us (0.972)
  waiting for transfers between devices: 16.6 us -> 15.2 us
    ppermute x17, waiting for transfers between devices: 13.2 us -> 11.8 us  [swap(): lax.ppermute(block, axis, [(i, i ^ bits) for i in range(lax.axis_size(axi...]
    pallas_call x1 -> x2, Pallas kernels: 16.9 us -> 16.8 us  [the longest x1 14.9 us: backward_call(): pl.pallas_call(body, out_shape=[jax.ShapeDtypeStruct((last // 2, last //...]
  transfers between devices with their start and end apart: 19 -> 19, of which waited for: 9 -> 9; matrix products, arithmetic and copies ran while one was open for 0% -> 0% of each run, Pallas kernels for 3% -> 7%
where the time goes in v5:
time: 55.1 us; the launch traced here: 54.9 us
  starting transfers between devices  19.5 us (35%)
  Pallas kernels  18.5 us (34%)
  waiting for transfers between devices  15.2 us (28%)
  between operations  0.78 us (1%)
  local copies, waits for them, and re-layouts  0.74 us (1%)
    pallas_call x1, Pallas kernels, backward_call(): pl.pallas_call(body, out_shape=[jax.ShapeDtypeStruct((last // 2, last //...  14.9 us
    ppermute x17, starting transfers between devices, swap(): lax.ppermute(block, axis, [(i, i ^ bits) for i in range(lax.axis_size(axi...  14.4 us
    ppermute x17, waiting for transfers between devices, swap(): lax.ppermute(block, axis, [(i, i ^ bits) for i in range(lax.axis_size(axi...  11.8 us
    ppermute x2, starting transfers between devices, from_behind(): return lax.ppermute(block, axis, route)  5.12 us
    ppermute x2, waiting for transfers between devices, from_behind(): return lax.ppermute(block, axis, route)  3.38 us
    pallas_call x1, Pallas kernels, input_call(): pl.pallas_call(input_kernel, out_shape=jax.ShapeDtypeStruct((voxels, chan...  1.84 us
    pallas_call x1, Pallas kernels, sides_call(): pl.pallas_call(sides_kernel, out_shape=[side, side, jax.ShapeDtypeStruct(...  1.75 us
  transfers between devices with their start and end apart: 19, of which 9 were waited for; matrix products, arithmetic and copies ran while one was open for 0% of the time, Pallas kernels for 7%

profile of v5, /device:TPU:0, one launch (start us, length us, event | category | flops | bytes accessed | tf_op | source)
XLA Modules:
  0.0 54.9 jit_solution(15177167350128490359)
XLA Ops:
  0.6 3.0 %collective-permute-start.1 = (bf16[512,128]{1,0:T(8,128)(2,1)}, bf16[512,128]{1,0:T(8,128)(2,1)S(1)}, u32[]{:S(2)}, u32[]{:S(2)}) collective-permute-start(bf16[512,128]{1,0:T(8,128)(2,1)} %bitcast.24), channel_id=1, source_target_pairs={{0,2},{1,3},{2,0},{3,1},{4,6},{5,7},{6,4},{7,5},{8,10},{9,11},{10,... | collective-permute-start | bytes 393224 | tf_op jit(solution)/shard_map/ppermute | solution.py:546
  3.6 0.1 collective-permute-start.4
  3.7 1.8 %pack_sides.1 = (bf16[400,128]{1,0:T(8,128)(2,1)}, bf16[400,128]{1,0:T(8,128)(2,1)}, bf16[16,128]{1,0:T(8,128)(2,1)}) custom-call(s32[1,4]{1,0:T(1,128)} %tile.1, s32[1,4]{1,0:T(1,128)} %used.1, bf16[512,128]{1,0:T(8,128)(2,1)} %bitcast.25, bf16[512,128]{1,0:T(8,128)(2,1)} %bitcast.29), custom_call_target="tpu_custom_call" | custom-call | tf_op jit(solution)/shard_map/pack_sides/pallas_call | solution.py:274
  5.5 3.8 %collective-permute-start.6 = (bf16[400,128]{1,0:T(8,128)(2,1)}, bf16[400,128]{1,0:T(8,128)(2,1)S(1)}, u32[]{:S(2)}, u32[]{:S(2)}) collective-permute-start(bf16[400,128]{1,0:T(8,128)(2,1)} %get-tuple-element.14), channel_id=1, source_target_pairs={{0,4},{4,8},{8,12},{12,16},{16,20},{20,24},{24,28},{1,5},{5,9},{9,... | collective-permute-start | bytes 307208 | tf_op jit(solution)/shard_map/ppermute | solution.py:19
  9.3 0.0 collective-permute-done.1.refs_3_
  9.3 1.3 %collective-permute-start.10 = (bf16[400,128]{1,0:T(8,128)(2,1)}, bf16[400,128]{1,0:T(8,128)(2,1)S(1)}, u32[]{:S(2)}, u32[]{:S(2)}) collective-permute-start(bf16[400,128]{1,0:T(8,128)(2,1)} %get-tuple-element.15), channel_id=1, source_target_pairs={{4,0},{8,4},{12,8},{16,12},{20,16},{24,20},{28,24},{5,1},{9,5},{13... | collective-permute-start | bytes 307208 | tf_op jit(solution)/shard_map/ppermute | solution.py:19
  10.6 0.0 copy-done
  10.6 0.1 collective-permute-start
  10.7 0.5 collective-permute-start.3
  11.2 0.6 %collective-permute-done.6.refs_9_ = bf16[400,128]{1,0:T(8,128)(2,1)S(1)} collective-permute-done((bf16[400,128]{1,0:T(8,128)(2,1)}, bf16[400,128]{1,0:T(8,128)(2,1)S(1)}, u32[]{:S(2)}, u32[]{:S(2)}) %collective-permute-start.6) | collective-permute-done | bytes 102432 | tf_op jit(solution)/shard_map/ppermute | solution.py:19
  11.9 1.5 %collective-permute-start.8 = (bf16[400,128]{1,0:T(8,128)(2,1)S(1)}, bf16[400,128]{1,0:T(8,128)(2,1)S(1)}, u32[]{:S(2)}, u32[]{:S(2)}) collective-permute-start(bf16[400,128]{1,0:T(8,128)(2,1)S(1)} %collective-permute-done.6.refs_9_), channel_id=1, source_target_pairs={{0,2},{1,3},{2,0},{3,1},{4,6},{5,7},{6,4},{7,5},{8,10},{9,11},{10,... | collective-permute-start | bytes 307208 | tf_op jit(solution)/shard_map/ppermute | solution.py:546
  13.4 0.0 collective-permute-done.4.refs_7_
  13.4 0.0 collective-permute-start.7
  13.4 2.7 %collective-permute-done.10.refs_13_ = bf16[400,128]{1,0:T(8,128)(2,1)S(1)} collective-permute-done((bf16[400,128]{1,0:T(8,128)(2,1)}, bf16[400,128]{1,0:T(8,128)(2,1)S(1)}, u32[]{:S(2)}, u32[]{:S(2)}) %collective-permute-start.10) | collective-permute-done | bytes 102432 | tf_op jit(solution)/shard_map/ppermute | solution.py:19
  16.1 1.5 %collective-permute-start.12 = (bf16[400,128]{1,0:T(8,128)(2,1)S(1)}, bf16[400,128]{1,0:T(8,128)(2,1)S(1)}, u32[]{:S(2)}, u32[]{:S(2)}) collective-permute-start(bf16[400,128]{1,0:T(8,128)(2,1)S(1)} %collective-permute-done.10.refs_13_), channel_id=1, source_target_pairs={{0,2},{1,3},{2,0},{3,1},{4,6},{5,7},{6,4},{7,5},{8,10},{9,11},{10,... | collective-permute-start | bytes 307208 | tf_op jit(solution)/shard_map/ppermute | solution.py:546
  17.6 0.0 collective-permute-done.refs_2_
  17.6 0.0 collective-permute-start.2
  17.6 0.0 collective-permute-done.3.refs_6_
  17.6 0.5 collective-permute-start.5
  18.1 0.0 collective-permute-done.8.refs_11_
  18.1 0.1 collective-permute-start.9
  18.2 0.0 collective-permute-done.7.refs_10_
  18.2 0.4 collective-permute-start.11
  18.6 2.1 %collective-permute-done.12.refs_15_ = bf16[400,128]{1,0:T(8,128)(2,1)S(1)} collective-permute-done((bf16[400,128]{1,0:T(8,128)(2,1)S(1)}, bf16[400,128]{1,0:T(8,128)(2,1)S(1)}, u32[]{:S(2)}, u32[]{:S(2)}) %collective-permute-start.12) | collective-permute-done | bytes 102432 | tf_op jit(solution)/shard_map/ppermute | solution.py:546
  20.8 0.0 collective-permute-start.13
  20.8 0.0 collective-permute-done.2.refs_4_
  20.8 0.0 collective-permute-done.5.refs_8_
  20.8 0.0 collective-permute-done.9.refs_12_
  20.8 0.0 collective-permute-done.11.refs_14_
  20.8 1.3 %collective-permute-done.13.refs_16_ = bf16[400,128]{1,0:T(8,128)(2,1)S(1)} collective-permute-done((bf16[400,128]{1,0:T(8,128)(2,1)S(1)}, bf16[400,128]{1,0:T(8,128)(2,1)S(1)}, u32[]{:S(2)}, u32[]{:S(2)}) %collective-permute-start.13) | collective-permute-done | bytes 102432 | tf_op jit(solution)/shard_map/ppermute | solution.py:546
  22.1 14.9 %tile_backward.1 = (bf16[5,5,2,16,128]{4,3,2,1,0:T(8,128)(2,1)S(1)}, bf16[4,2,2,112,128]{4,3,2,1,0:T(8,128)(2,1)S(1)}, bf16[4,2,2,112,128]{4,3,2,1,0:T(8,128)(2,1)S(1)}) custom-call(s32[1]{0:T(128)} %bitcast.refs_0_.depth_ref, bf16[512,128]{1,0:T(8,128)(2,1)S(1)} %bitcast.27, bf16[512,128]{1,0:T(8,128)(2,1)S(1)} %collective-permute-done.refs_2_, ...), custom_call_target="tpu_custom_call" | custom-call | flops 9059696640 | bytes 6553600 | tf_op jit(solution)/shard_map/tile_backward/pallas_call | solution.py:520
  37.0 0.2 collective-permute-start.14
  37.2 1.7 %collective-permute-done.14 = bf16[4,2,2,112,128]{4,3,2,1,0:T(8,128)(2,1)S(1)} collective-permute-done((bf16[4,2,2,112,128]{4,3,2,1,0:T(8,128)(2,1)S(1)}, bf16[4,2,2,112,128]{4,3,2,1,0:T(8,128)(2,1)S(1)}, u32[]{:S(2)}, u32[]{:S(2)}) %collective-permute-start.14) | collective-permute-done | bytes 458784 | tf_op jit(solution)/shard_map/ppermute | solution.py:546
  38.9 0.1 convert_add_fusion
  39.0 0.0 copy-start.2
  39.0 0.1 fusion.2
  39.1 2.8 %collective-permute-start.15 = (bf16[2,2,112,128]{3,2,1,0:T(8,128)(2,1)S(1)}, bf16[2,2,112,128]{3,2,1,0:T(8,128)(2,1)S(1)}, u32[]{:S(2)}, u32[]{:S(2)}) collective-permute-start(bf16[2,2,112,128]{3,2,1,0:T(8,128)(2,1)S(1)} %get-tuple-element.19), channel_id=1, source_target_pairs={{0,4},{4,0},{8,12},{12,8},{16,20},{20,16},{24,28},{28,24},{1,5},{5... | collective-permute-start | bytes 344072 | tf_op jit(solution)/shard_map/ppermute | solution.py:546
  41.8 1.4 %collective-permute-start.16 = (bf16[2,2,112,128]{3,2,1,0:T(8,128)(2,1)S(1)}, bf16[2,2,112,128]{3,2,1,0:T(8,128)(2,1)S(1)}, u32[]{:S(2)}, u32[]{:S(2)}) collective-permute-start(bf16[2,2,112,128]{3,2,1,0:T(8,128)(2,1)S(1)} %get-tuple-element.21), channel_id=1, source_target_pairs={{0,8},{4,12},{8,0},{12,4},{16,24},{20,28},{24,16},{28,20},{1,9},{5... | collective-permute-start | bytes 344072 | tf_op jit(solution)/shard_map/ppermute | solution.py:546
  43.3 0.1 collective-permute-start.17
  43.4 1.9 %collective-permute-done.15 = bf16[2,2,112,128]{3,2,1,0:T(8,128)(2,1)S(1)} collective-permute-done((bf16[2,2,112,128]{3,2,1,0:T(8,128)(2,1)S(1)}, bf16[2,2,112,128]{3,2,1,0:T(8,128)(2,1)S(1)}, u32[]{:S(2)}, u32[]{:S(2)}) %collective-permute-start.15) | collective-permute-done | bytes 114720 | tf_op jit(solution)/shard_map/ppermute | solution.py:546
  45.3 2.6 %collective-permute-done.16 = bf16[2,2,112,128]{3,2,1,0:T(8,128)(2,1)S(1)} collective-permute-done((bf16[2,2,112,128]{3,2,1,0:T(8,128)(2,1)S(1)}, bf16[2,2,112,128]{3,2,1,0:T(8,128)(2,1)S(1)}, u32[]{:S(2)}, u32[]{:S(2)}) %collective-permute-start.16) | collective-permute-done | bytes 114720 | tf_op jit(solution)/shard_map/ppermute | solution.py:546
  47.9 1.1 %collective-permute-done.17 = bf16[2,2,112,128]{3,2,1,0:T(8,128)(2,1)S(1)} collective-permute-done((bf16[2,2,112,128]{3,2,1,0:T(8,128)(2,1)S(1)}, bf16[2,2,112,128]{3,2,1,0:T(8,128)(2,1)S(1)}, u32[]{:S(2)}, u32[]{:S(2)}) %collective-permute-start.17) | collective-permute-done | bytes 114720 | tf_op jit(solution)/shard_map/ppermute | solution.py:546
  49.0 0.1 fusion.1
  49.1 2.2 %collective-permute-start.18 = (bf16[2,112,128]{2,1,0:T(8,128)(2,1)S(1)}, bf16[2,112,128]{2,1,0:T(8,128)(2,1)S(1)}, u32[]{:S(2)}, u32[]{:S(2)}) collective-permute-start(bf16[2,112,128]{2,1,0:T(8,128)(2,1)S(1)} %fusion.5), channel_id=1, source_target_pairs={{0,16},{4,20},{8,24},{12,28},{16,0},{20,4},{24,8},{28,12},{1,17},{... | collective-permute-start | bytes 172040 | tf_op jit(solution)/shard_map/ppermute | solution.py:546
  51.3 0.0 copy-done.2
  51.3 1.8 %input_gradient.1 = bf16[512,128]{1,0:T(8,128)(2,1)} custom-call(s32[1]{0:T(128)} %bitcast.refs_0_.depth_ref, bf16[16,128]{1,0:T(8,128)(2,1)S(1)} %copy-done.3, bf16[5,5,2,16,128]{4,3,2,1,0:T(8,128)(2,1)S(1)} %get-tuple-element.16.last, bf16[27,128,128]{2,1,0:T(8,128)(2,1)S(1)} %copy-done.2), custom_call_target="tpu_custom_call" | custom-call | flops 603979776 | bytes 1409024 | tf_op jit(solution)/shard_map/input_gradient/pallas_call | solution.py:457
  53.1 1.1 %collective-permute-done.18 = bf16[2,112,128]{2,1,0:T(8,128)(2,1)S(1)} collective-permute-done((bf16[2,112,128]{2,1,0:T(8,128)(2,1)S(1)}, bf16[2,112,128]{2,1,0:T(8,128)(2,1)S(1)}, u32[]{:S(2)}, u32[]{:S(2)}) %collective-permute-start.18) | collective-permute-done | bytes 57376 | tf_op jit(solution)/shard_map/ppermute | solution.py:546
  54.2 0.6 %slice_bitcast_fusion = (f32[13824]{0:T(1024)}, f32[13824]{0:T(1024)}) fusion(f32[2,112,128]{2,1,0:T(8,128)S(1)} %bitcast_add_fusion.1), kind=kLoop, calls=%fused_computation.13 | loop fusion | bytes 221184 | tf_op jit(solution)/shard_map/reshape;squeeze | solution.py:584
  (7 shorter events, 0.0 us)
Async XLA Ops:
  0.6 8.7 %collective-permute-start.1 = (bf16[512,128]{1,0:T(8,128)(2,1)}, bf16[512,128]{1,0:T(8,128)(2,1)S(1)}, u32[]{:S(2)}, u32[]{:S(2)}) collective-permute-start(bf16[512,128]{1,0:T(8,128)(2,1)} %bitcast.24), channel_id=1, source_target_pairs={{0,2},{1,3},{2,0},{3,1},{4,6},{5,7},{6,4},{7,5},{8,10},{9,11},{10,... | collective-permute-start | bytes 393224 | tf_op jit(solution)/shard_map/ppermute | solution.py:546
  3.6 7.0 %copy-start = (bf16[1,1,512,128]{3,2,1,0:T(8,128)(2,1)S(1)}, bf16[1,1,512,128]{3,2,1,0:T(8,128)(2,1)}, u32[]{:S(2)}) copy-start(bf16[1,1,512,128]{3,2,1,0:T(8,128)(2,1)} %param.6) | copy-start | bytes 393220
  3.6 7.1 %copy-start.1 = (bf16[1,1,512,128]{3,2,1,0:T(8,128)(2,1)S(1)}, bf16[1,1,512,128]{3,2,1,0:T(8,128)(2,1)}, u32[]{:S(2)}) copy-start(bf16[1,1,512,128]{3,2,1,0:T(8,128)(2,1)} %param.7) | copy-start | bytes 393220
  3.6 9.7 %collective-permute-start.4 = (bf16[512,128]{1,0:T(8,128)(2,1)}, bf16[512,128]{1,0:T(8,128)(2,1)S(1)}, u32[]{:S(2)}, u32[]{:S(2)}) collective-permute-start(bf16[512,128]{1,0:T(8,128)(2,1)} %bitcast.28), channel_id=1, source_target_pairs={{0,2},{1,3},{2,0},{3,1},{4,6},{5,7},{6,4},{7,5},{8,10},{9,11},{10,... | collective-permute-start | bytes 393224 | tf_op jit(solution)/shard_map/ppermute | solution.py:546
  5.5 6.4 %collective-permute-start.6 = (bf16[400,128]{1,0:T(8,128)(2,1)}, bf16[400,128]{1,0:T(8,128)(2,1)S(1)}, u32[]{:S(2)}, u32[]{:S(2)}) collective-permute-start(bf16[400,128]{1,0:T(8,128)(2,1)} %get-tuple-element.14), channel_id=1, source_target_pairs={{0,4},{4,8},{8,12},{12,16},{16,20},{20,24},{24,28},{1,5},{5,9},{9,... | collective-permute-start | bytes 307208 | tf_op jit(solution)/shard_map/ppermute | solution.py:19
  9.3 6.8 %collective-permute-start.10 = (bf16[400,128]{1,0:T(8,128)(2,1)}, bf16[400,128]{1,0:T(8,128)(2,1)S(1)}, u32[]{:S(2)}, u32[]{:S(2)}) collective-permute-start(bf16[400,128]{1,0:T(8,128)(2,1)} %get-tuple-element.15), channel_id=1, source_target_pairs={{4,0},{8,4},{12,8},{16,12},{20,16},{24,20},{28,24},{5,1},{9,5},{13... | collective-permute-start | bytes 307208 | tf_op jit(solution)/shard_map/ppermute | solution.py:19
  10.6 6.9 %collective-permute-start = (bf16[512,128]{1,0:T(8,128)(2,1)S(1)}, bf16[512,128]{1,0:T(8,128)(2,1)S(1)}, u32[]{:S(2)}, u32[]{:S(2)}) collective-permute-start(bf16[512,128]{1,0:T(8,128)(2,1)S(1)} %bitcast.26), channel_id=1, source_target_pairs={{0,1},{1,0},{2,3},{3,2},{4,5},{5,4},{6,7},{7,6},{8,9},{9,8},{10,11... | collective-permute-start | bytes 393224 | tf_op jit(solution)/shard_map/ppermute | solution.py:546
  10.7 6.9 %collective-permute-start.3 = (bf16[512,128]{1,0:T(8,128)(2,1)S(1)}, bf16[512,128]{1,0:T(8,128)(2,1)S(1)}, u32[]{:S(2)}, u32[]{:S(2)}) collective-permute-start(bf16[512,128]{1,0:T(8,128)(2,1)S(1)} %bitcast.30), channel_id=1, source_target_pairs={{0,1},{1,0},{2,3},{3,2},{4,5},{5,4},{6,7},{7,6},{8,9},{9,8},{10,11... | collective-permute-start | bytes 393224 | tf_op jit(solution)/shard_map/ppermute | solution.py:546
  11.9 6.2 %collective-permute-start.8 = (bf16[400,128]{1,0:T(8,128)(2,1)S(1)}, bf16[400,128]{1,0:T(8,128)(2,1)S(1)}, u32[]{:S(2)}, u32[]{:S(2)}) collective-permute-start(bf16[400,128]{1,0:T(8,128)(2,1)S(1)} %collective-permute-done.6.refs_9_), channel_id=1, source_target_pairs={{0,2},{1,3},{2,0},{3,1},{4,6},{5,7},{6,4},{7,5},{8,10},{9,11},{10,... | collective-permute-start | bytes 307208 | tf_op jit(solution)/shard_map/ppermute | solution.py:546
  13.4 4.8 %collective-permute-start.7 = (bf16[400,128]{1,0:T(8,128)(2,1)S(1)}, bf16[400,128]{1,0:T(8,128)(2,1)S(1)}, u32[]{:S(2)}, u32[]{:S(2)}) collective-permute-start(bf16[400,128]{1,0:T(8,128)(2,1)S(1)} %collective-permute-done.6.refs_9_), channel_id=1, source_target_pairs={{0,1},{1,0},{2,3},{3,2},{4,5},{5,4},{6,7},{7,6},{8,9},{9,8},{10,11... | collective-permute-start | bytes 307208 | tf_op jit(solution)/shard_map/ppermute | solution.py:546
  16.1 4.7 %collective-permute-start.12 = (bf16[400,128]{1,0:T(8,128)(2,1)S(1)}, bf16[400,128]{1,0:T(8,128)(2,1)S(1)}, u32[]{:S(2)}, u32[]{:S(2)}) collective-permute-start(bf16[400,128]{1,0:T(8,128)(2,1)S(1)} %collective-permute-done.10.refs_13_), channel_id=1, source_target_pairs={{0,2},{1,3},{2,0},{3,1},{4,6},{5,7},{6,4},{7,5},{8,10},{9,11},{10,... | collective-permute-start | bytes 307208 | tf_op jit(solution)/shard_map/ppermute | solution.py:546
  17.6 3.2 %collective-permute-start.2 = (bf16[512,128]{1,0:T(8,128)(2,1)S(1)}, bf16[512,128]{1,0:T(8,128)(2,1)S(1)}, u32[]{:S(2)}, u32[]{:S(2)}) collective-permute-start(bf16[512,128]{1,0:T(8,128)(2,1)S(1)} %collective-permute-done.1.refs_3_), channel_id=1, source_target_pairs={{0,1},{1,0},{2,3},{3,2},{4,5},{5,4},{6,7},{7,6},{8,9},{9,8},{10,11... | collective-permute-start | bytes 393224 | tf_op jit(solution)/shard_map/ppermute | solution.py:546
  17.6 3.2 %collective-permute-start.5 = (bf16[512,128]{1,0:T(8,128)(2,1)S(1)}, bf16[512,128]{1,0:T(8,128)(2,1)S(1)}, u32[]{:S(2)}, u32[]{:S(2)}) collective-permute-start(bf16[512,128]{1,0:T(8,128)(2,1)S(1)} %collective-permute-done.4.refs_7_), channel_id=1, source_target_pairs={{0,1},{1,0},{2,3},{3,2},{4,5},{5,4},{6,7},{7,6},{8,9},{9,8},{10,11... | collective-permute-start | bytes 393224 | tf_op jit(solution)/shard_map/ppermute | solution.py:546
  18.1 2.7 %collective-permute-start.9 = (bf16[400,128]{1,0:T(8,128)(2,1)S(1)}, bf16[400,128]{1,0:T(8,128)(2,1)S(1)}, u32[]{:S(2)}, u32[]{:S(2)}) collective-permute-start(bf16[400,128]{1,0:T(8,128)(2,1)S(1)} %collective-permute-done.8.refs_11_), channel_id=1, source_target_pairs={{0,1},{1,0},{2,3},{3,2},{4,5},{5,4},{6,7},{7,6},{8,9},{9,8},{10,11... | collective-permute-start | bytes 307208 | tf_op jit(solution)/shard_map/ppermute | solution.py:546
  18.2 2.6 %collective-permute-start.11 = (bf16[400,128]{1,0:T(8,128)(2,1)S(1)}, bf16[400,128]{1,0:T(8,128)(2,1)S(1)}, u32[]{:S(2)}, u32[]{:S(2)}) collective-permute-start(bf16[400,128]{1,0:T(8,128)(2,1)S(1)} %collective-permute-done.10.refs_13_), channel_id=1, source_target_pairs={{0,1},{1,0},{2,3},{3,2},{4,5},{5,4},{6,7},{7,6},{8,9},{9,8},{10,11... | collective-permute-start | bytes 307208 | tf_op jit(solution)/shard_map/ppermute | solution.py:546
  20.8 1.3 %collective-permute-start.13 = (bf16[400,128]{1,0:T(8,128)(2,1)S(1)}, bf16[400,128]{1,0:T(8,128)(2,1)S(1)}, u32[]{:S(2)}, u32[]{:S(2)}) collective-permute-start(bf16[400,128]{1,0:T(8,128)(2,1)S(1)} %collective-permute-done.12.refs_15_), channel_id=1, source_target_pairs={{0,1},{1,0},{2,3},{3,2},{4,5},{5,4},{6,7},{7,6},{8,9},{9,8},{10,11... | collective-permute-start | bytes 307208 | tf_op jit(solution)/shard_map/ppermute | solution.py:546
  20.8 1.3 %copy-start.3 = (bf16[16,128]{1,0:T(8,128)(2,1)S(1)}, bf16[16,128]{1,0:T(8,128)(2,1)}, u32[]{:S(2)}) copy-start(bf16[16,128]{1,0:T(8,128)(2,1)} %get-tuple-element.11.refs_17_.own_table) | copy-start | bytes 12292
  37.0 1.9 %collective-permute-start.14 = (bf16[4,2,2,112,128]{4,3,2,1,0:T(8,128)(2,1)S(1)}, bf16[4,2,2,112,128]{4,3,2,1,0:T(8,128)(2,1)S(1)}, u32[]{:S(2)}, u32[]{:S(2)}) collective-permute-start(bf16[4,2,2,112,128]{4,3,2,1,0:T(8,128)(2,1)S(1)} %get-tuple-element.18), channel_id=1, source_target_pairs={{0,1},{1,0},{2,3},{3,2},{4,5},{5,4},{6,7},{7,6},{8,9},{9,8},{10,11... | collective-permute-start | bytes 1376264 | tf_op jit(solution)/shard_map/ppermute | solution.py:546
  39.0 12.3 %copy-start.2 = (bf16[27,128,128]{2,1,0:T(8,128)(2,1)S(1)}, bf16[27,128,128]{2,1,0:T(8,128)(2,1)}, u32[]{:S(2)}) copy-start(bf16[27,128,128]{2,1,0:T(8,128)(2,1)} %far_first.1) | copy-start | bytes 2654212
  39.1 6.2 %collective-permute-start.15 = (bf16[2,2,112,128]{3,2,1,0:T(8,128)(2,1)S(1)}, bf16[2,2,112,128]{3,2,1,0:T(8,128)(2,1)S(1)}, u32[]{:S(2)}, u32[]{:S(2)}) collective-permute-start(bf16[2,2,112,128]{3,2,1,0:T(8,128)(2,1)S(1)} %get-tuple-element.19), channel_id=1, source_target_pairs={{0,4},{4,0},{8,12},{12,8},{16,20},{20,16},{24,28},{28,24},{1,5},{5... | collective-permute-start | bytes 344072 | tf_op jit(solution)/shard_map/ppermute | solution.py:546
  41.8 6.0 %collective-permute-start.16 = (bf16[2,2,112,128]{3,2,1,0:T(8,128)(2,1)S(1)}, bf16[2,2,112,128]{3,2,1,0:T(8,128)(2,1)S(1)}, u32[]{:S(2)}, u32[]{:S(2)}) collective-permute-start(bf16[2,2,112,128]{3,2,1,0:T(8,128)(2,1)S(1)} %get-tuple-element.21), channel_id=1, source_target_pairs={{0,8},{4,12},{8,0},{12,4},{16,24},{20,28},{24,16},{28,20},{1,9},{5... | collective-permute-start | bytes 344072 | tf_op jit(solution)/shard_map/ppermute | solution.py:546
  43.3 5.7 %collective-permute-start.17 = (bf16[2,2,112,128]{3,2,1,0:T(8,128)(2,1)S(1)}, bf16[2,2,112,128]{3,2,1,0:T(8,128)(2,1)S(1)}, u32[]{:S(2)}, u32[]{:S(2)}) collective-permute-start(bf16[2,2,112,128]{3,2,1,0:T(8,128)(2,1)S(1)} %get-tuple-element.20), channel_id=1, source_target_pairs={{0,12},{4,8},{8,4},{12,0},{16,28},{20,24},{24,20},{28,16},{1,13},{... | collective-permute-start | bytes 344072 | tf_op jit(solution)/shard_map/ppermute | solution.py:546
  49.1 5.1 %collective-permute-start.18 = (bf16[2,112,128]{2,1,0:T(8,128)(2,1)S(1)}, bf16[2,112,128]{2,1,0:T(8,128)(2,1)S(1)}, u32[]{:S(2)}, u32[]{:S(2)}) collective-permute-start(bf16[2,112,128]{2,1,0:T(8,128)(2,1)S(1)} %fusion.5), channel_id=1, source_target_pairs={{0,16},{4,20},{8,24},{12,28},{16,0},{20,4},{24,8},{28,12},{1,17},{... | collective-permute-start | bytes 172040 | tf_op jit(solution)/shard_map/ppermute | solution.py:546

commit v6 on v5

--- a/solution.py
+++ b/solution.py
@@ -249,24 +249,26 @@
     return face, thin, face + thin + 16
 
 
-def sides_kernel(tile, used, feature_rows, upstream_rows, to_above, to_below, own_table, lifted):
+def sides_kernel(tile, used, odd, feature_rows, upstream_rows, to_pair, to_cross, own_table, lifted):
     channels = feature_rows.shape[1]
     face = side_sizes()[0]
     for rows, width, offset in ((feature_rows, HALO, 0), (upstream_rows, 2, face)):
         lifted[...] = rows[...].astype(F32).reshape(lifted.shape)
         count = TE * TE * width
-        to_above[offset : offset + count] = lifted[:, TE - width :].reshape(count, channels).astype(BF)
-        to_below[offset : offset + count] = lifted[:, :width].reshape(count, channels).astype(BF)
+        high = lifted[:, TE - width :].reshape(count, channels)
+        low = lifted[:, :width].reshape(count, channels)
+        to_pair[offset : offset + count] = jnp.where(odd[0] == 1, low, high).astype(BF)
+        to_cross[offset : offset + count] = jnp.where(odd[0] == 1, high, low).astype(BF)
     place = lax.broadcasted_iota(jnp.int32, (16, channels), 0)
     table = jnp.zeros((16, channels), F32)
     for slot in range(tile.shape[1]):
         code = jnp.where(used[0, slot] == 1, tile[0, slot] + 1, 0)
         table = jnp.where(place == slot, code.astype(F32), table)
-    for out in (to_above, to_below, own_table):
+    for out in (to_pair, to_cross, own_table):
         out[out.shape[0] - 16 :] = table.astype(BF)
 
 
-def sides_call(slot_tile, slot_used, feature_rows, upstream_rows):
+def sides_call(slot_tile, slot_used, odd, feature_rows, upstream_rows):
     voxels, channels = feature_rows.shape
     smem = pl.BlockSpec(memory_space=pltpu.SMEM)
     vmem = pl.BlockSpec(memory_space=pltpu.VMEM)
@@ -274,11 +276,11 @@
     return pl.pallas_call(
         sides_kernel,
         out_shape=[side, side, jax.ShapeDtypeStruct((16, channels), BF)],
-        in_specs=[smem, smem, vmem, vmem],
+        in_specs=[smem, smem, smem, vmem, vmem],
         out_specs=[vmem] * 3,
         scratch_shapes=[pltpu.VMEM((TE * TE, TE, channels), F32)],
         name="pack_sides",
-    )(slot_tile, slot_used, feature_rows, upstream_rows)
+    )(slot_tile, slot_used, odd, feature_rows, upstream_rows)
 
 
 def table_at(block, first, slots):
@@ -287,8 +289,8 @@
     return [jnp.max(jnp.where(place == slot, table, 0.0)).astype(jnp.int32) for slot in slots]
 
 
-def backward_kernel(block_count, tiles, depth_ref, *refs):
-    own, up, below, above = (list(refs[at * block_count : (at + 1) * block_count]) for at in range(4))
+def backward_kernel(block_count, tiles, depth_ref, odd_ref, *refs):
+    own, up, pair, cross = (list(refs[at * block_count : (at + 1) * block_count]) for at in range(4))
     own_table, far_first, far_second, last, kept, given = refs[4 * block_count : 4 * block_count + 6]
     rest = list(refs[4 * block_count + 6 :])
     channels = own[0].shape[-1]
@@ -329,13 +331,14 @@
     face, thin, _ = side_sizes()
 
     held = table_at(own_table, 0, slots)
-    codes = table_at(below[0], face + thin, slots)
-    place_slots(codes, below, 0, 0, HALO, lifted, volume, mask, 0)
-    place_slots(codes, below, face, HALO - 2, 2, lifted, upstream, None, 0)
-    codes = table_at(above[0], face + thin, slots)
-    place_slots(codes, above, 0, HALO + TE, HALO, lifted, volume, mask, 2)
-    place_slots(codes, above, face, HALO + TE, 2, lifted, upstream, None, 2)
-
+    odd = odd_ref[0]
+    for blocks, low in ((pair, odd), (cross, 1 - odd)):
+        codes = table_at(blocks[0], face + thin, slots)
+        side = 2 * (1 - low)
+        y_feature = (1 - low) * (HALO + TE)
+        y_upstream = (1 - low) * (TE + 2) + HALO - 2
+        place_slots(codes, blocks, 0, y_feature, HALO, lifted, volume, mask, side)
+        place_slots(codes, blocks, face, y_upstream, 2, lifted, upstream, None, side)
     fetches[0].wait()
     place_slots(held, own, 0, HALO, TE, lifted, volume, mask, 1)
     fetches[1].wait()
@@ -481,7 +484,7 @@
     )(depth_at.reshape(1), own_table, last, first_kernel)
 
 
-def backward_call(own, up, below, above, own_table, kernels, depth_at, columns, positions, tiles):
+def backward_call(own, up, pair, cross, own_table, kernels, depth_at, odd, columns, positions, tiles):
     channels = own[0].shape[-1]
     voxels = TE * TE * TE
     planes = positions * TE + 2 * HALO
@@ -524,7 +527,7 @@
             share,
             share,
         ],
-        in_specs=[smem] + ([hbm] + [vmem] * (len(own) - 1)) * 2 + [vmem] * (len(below) + len(above) + 1) + [hbm, hbm],
+        in_specs=[smem, smem] + ([hbm] + [vmem] * (len(own) - 1)) * 2 + [vmem] * (len(pair) + len(cross) + 1) + [hbm, hbm],
         out_specs=[vmem] * 3,
         scratch_shapes=scratch,
         compiler_params=pltpu.CompilerParams(vmem_limit_bytes=VMEM_LIMIT),
@@ -534,7 +537,7 @@
             transcendentals=4 * voxels * channels,
         ),
         name="tile_backward",
-    )(depth_at.reshape(1), *own, *up, *below, *above, own_table, *kernels)
+    )(depth_at.reshape(1), odd, *own, *up, *pair, *cross, own_table, *kernels)
 
 
 def on_device_line(features, cotangent, first_kernel, second_kernel, slot_tile, slot_used):
@@ -547,10 +550,12 @@
 
     own, up = features[0, 0], cotangent[0, 0]
     own_far, up_far = swap(own, "depth", 2), swap(up, "depth", 2)
-    to_above, to_below, own_table = sides_call(slot_tile, slot_used, own, up)
-    to_below, own_far = lax.optimization_barrier((to_below, own_far))
-    below, above = from_behind(to_above, "space", 1), from_behind(to_below, "space", -1)
-    below_far, above_far = swap(below, "depth", 2), swap(above, "depth", 2)
+    odd = (space_at % 2).reshape(1)
+    to_pair, to_cross, own_table = sides_call(slot_tile, slot_used, odd, own, up)
+    to_pair, own_far = lax.optimization_barrier((to_pair, own_far))
+    crossing = [(i, i + 1 if i % 2 else i - 1) for i in range(1, space_size - 1)]
+    cross, pair = lax.ppermute(to_cross, "space", crossing), swap(to_pair, "space", 1)
+    cross_far, pair_far = swap(cross, "depth", 2), swap(pair, "depth", 2)
 
     def with_sibling(near, far):
         return [near, swap(near, "depth", 1), far, swap(far, "depth", 1)]
@@ -558,11 +563,12 @@
     last, kept, given = backward_call(
         with_sibling(own, own_far),
         with_sibling(up, up_far),
-        with_sibling(below, below_far),
-        with_sibling(above, above_far),
+        with_sibling(pair, pair_far),
+        with_sibling(cross, cross_far),
         own_table,
         (first_kernel, second_kernel),
         depth_at,
+        odd,
         space_size,
         slot_tile.shape[1],
         2,

time: 55.1 us -> 54 us (0.980)
  starting transfers between devices: 19.5 us -> 18.8 us
  waiting for transfers between devices: 15.2 us -> 14.6 us
    ppermute x2 -> x1, starting transfers between devices: 5.12 us -> 0.66 us  [on_device_line(): lax.ppermute(to_cross, 'space', crossing)]
    ppermute x17 -> x18, starting transfers between devices: 14.4 us -> 18.2 us  [swap(): lax.ppermute(block, axis, [(i, i ^ bits) for i in range(lax.axis_size(axi...]
    ppermute x2 -> x1, waiting for transfers between devices: 3.38 us -> 0.01 us  [on_device_line(): lax.ppermute(to_cross, 'space', crossing)]
    ppermute x17 -> x18, waiting for transfers between devices: 11.8 us -> 14.6 us  [swap(): lax.ppermute(block, axis, [(i, i ^ bits) for i in range(lax.axis_size(axi...]
  transfers between devices with their start and end apart: 19 -> 19, of which waited for: 9 -> 10; matrix products, arithmetic and copies ran while one was open for 0% -> 0% of each run, Pallas kernels for 7% -> 7%
where the time goes in v6:
time: 54 us; the launch traced here: 53.9 us
  starting transfers between devices  18.8 us (35%)
  Pallas kernels  18.7 us (35%)
  waiting for transfers between devices  14.6 us (27%)
  local copies, waits for them, and re-layouts  0.74 us (1%)
  between operations  0.74 us (1%)
    ppermute x18, starting transfers between devices, swap(): lax.ppermute(block, axis, [(i, i ^ bits) for i in range(lax.axis_size(axi...  18.2 us
    pallas_call x1, Pallas kernels, backward_call(): pl.pallas_call(body, out_shape=[jax.ShapeDtypeStruct((last // 2, last //...  15 us
    ppermute x18, waiting for transfers between devices, swap(): lax.ppermute(block, axis, [(i, i ^ bits) for i in range(lax.axis_size(axi...  14.6 us
    pallas_call x1, Pallas kernels, sides_call(): pl.pallas_call(sides_kernel, out_shape=[side, side, jax.ShapeDtypeStruct(...  1.88 us
    pallas_call x1, Pallas kernels, input_call(): pl.pallas_call(input_kernel, out_shape=jax.ShapeDtypeStruct((voxels, chan...  1.84 us
  transfers between devices with their start and end apart: 19, of which 10 were waited for; matrix products, arithmetic and copies ran while one was open for 0% of the time, Pallas kernels for 7%

profile of v6, /device:TPU:0, one launch (start us, length us, event | category | flops | bytes accessed | tf_op | source)
XLA Modules:
  0.0 53.9 jit_solution(16101634092145492485)
XLA Ops:
  0.6 3.0 %collective-permute-start.1 = (bf16[512,128]{1,0:T(8,128)(2,1)}, bf16[512,128]{1,0:T(8,128)(2,1)S(1)}, u32[]{:S(2)}, u32[]{:S(2)}) collective-permute-start(bf16[512,128]{1,0:T(8,128)(2,1)} %bitcast.25), channel_id=1, source_target_pairs={{0,2},{1,3},{2,0},{3,1},{4,6},{5,7},{6,4},{7,5},{8,10},{9,11},{10,... | collective-permute-start | bytes 393224 | tf_op jit(solution)/shard_map/ppermute | solution.py:549
  3.6 0.1 collective-permute-start.4
  3.7 1.9 %pack_sides.1 = (bf16[400,128]{1,0:T(8,128)(2,1)}, bf16[400,128]{1,0:T(8,128)(2,1)}, bf16[16,128]{1,0:T(8,128)(2,1)}) custom-call(s32[1,4]{1,0:T(1,128)} %tile.1, s32[1,4]{1,0:T(1,128)} %used.1, s32[1]{0:T(128)} %bitcast.1.odd.refs_1_, bf16[512,128]{1,0:T(8,128)(2,1)} %bitcast.26, bf16[512,128]{1,0:T(8,128)(2,1)} %bitcast.30), custom_call_target="tpu_custom_call" | custom-call | tf_op jit(solution)/shard_map/pack_sides/pallas_call | solution.py:276
  5.6 0.7 %collective-permute-start.10 = (bf16[400,128]{1,0:T(8,128)(2,1)}, bf16[400,128]{1,0:T(8,128)(2,1)S(1)}, u32[]{:S(2)}, u32[]{:S(2)}) collective-permute-start(bf16[400,128]{1,0:T(8,128)(2,1)} %get-tuple-element.15), channel_id=1, source_target_pairs={{4,8},{8,4},{12,16},{16,12},{20,24},{24,20},{5,9},{9,5},{13,17},{1... | collective-permute-start | bytes 307208 | tf_op jit(solution)/shard_map/ppermute | solution.py:557
  6.3 1.9 %collective-permute-done.1.refs_4_ = bf16[512,128]{1,0:T(8,128)(2,1)S(1)} collective-permute-done((bf16[512,128]{1,0:T(8,128)(2,1)}, bf16[512,128]{1,0:T(8,128)(2,1)S(1)}, u32[]{:S(2)}, u32[]{:S(2)}) %collective-permute-start.1) | collective-permute-done | bytes 131104 | tf_op jit(solution)/shard_map/ppermute | solution.py:549
  8.2 2.9 %collective-permute-start.6 = (bf16[400,128]{1,0:T(8,128)(2,1)}, bf16[400,128]{1,0:T(8,128)(2,1)S(1)}, u32[]{:S(2)}, u32[]{:S(2)}) collective-permute-start(bf16[400,128]{1,0:T(8,128)(2,1)} %get-tuple-element.14), channel_id=1, source_target_pairs={{0,4},{4,0},{8,12},{12,8},{16,20},{20,16},{24,28},{28,24},{1,5},{5... | collective-permute-start | bytes 307208 | tf_op jit(solution)/shard_map/ppermute | solution.py:549
  11.1 0.0 copy-done
  11.1 0.0 collective-permute-start
  11.1 0.5 collective-permute-start.3
  11.6 0.0 collective-permute-done.10.refs_14_
  11.6 1.5 %collective-permute-start.12 = (bf16[400,128]{1,0:T(8,128)(2,1)S(1)}, bf16[400,128]{1,0:T(8,128)(2,1)S(1)}, u32[]{:S(2)}, u32[]{:S(2)}) collective-permute-start(bf16[400,128]{1,0:T(8,128)(2,1)S(1)} %collective-permute-done.10.refs_14_), channel_id=1, source_target_pairs={{0,2},{1,3},{2,0},{3,1},{4,6},{5,7},{6,4},{7,5},{8,10},{9,11},{10,... | collective-permute-start | bytes 307208 | tf_op jit(solution)/shard_map/ppermute | solution.py:549
  13.1 0.0 collective-permute-done.4.refs_8_
  13.1 0.0 collective-permute-start.11
  13.1 1.3 %collective-permute-done.6.refs_10_ = bf16[400,128]{1,0:T(8,128)(2,1)S(1)} collective-permute-done((bf16[400,128]{1,0:T(8,128)(2,1)}, bf16[400,128]{1,0:T(8,128)(2,1)S(1)}, u32[]{:S(2)}, u32[]{:S(2)}) %collective-permute-start.6) | collective-permute-done | bytes 102432 | tf_op jit(solution)/shard_map/ppermute | solution.py:549
  14.4 1.5 %collective-permute-start.8 = (bf16[400,128]{1,0:T(8,128)(2,1)S(1)}, bf16[400,128]{1,0:T(8,128)(2,1)S(1)}, u32[]{:S(2)}, u32[]{:S(2)}) collective-permute-start(bf16[400,128]{1,0:T(8,128)(2,1)S(1)} %collective-permute-done.6.refs_10_), channel_id=1, source_target_pairs={{0,2},{1,3},{2,0},{3,1},{4,6},{5,7},{6,4},{7,5},{8,10},{9,11},{10,... | collective-permute-start | bytes 307208 | tf_op jit(solution)/shard_map/ppermute | solution.py:549
  15.9 0.0 collective-permute-done.refs_3_
  15.9 0.0 collective-permute-start.2
  15.9 0.0 collective-permute-done.3.refs_7_
  16.0 0.5 collective-permute-start.5
  16.5 0.2 collective-permute-done.12.refs_16_
  16.7 0.0 collective-permute-start.13
  16.7 0.0 collective-permute-done.11.refs_15_
  16.7 0.5 collective-permute-start.7
  17.2 1.9 %collective-permute-done.8.refs_12_ = bf16[400,128]{1,0:T(8,128)(2,1)S(1)} collective-permute-done((bf16[400,128]{1,0:T(8,128)(2,1)S(1)}, bf16[400,128]{1,0:T(8,128)(2,1)S(1)}, u32[]{:S(2)}, u32[]{:S(2)}) %collective-permute-start.8) | collective-permute-done | bytes 102432 | tf_op jit(solution)/shard_map/ppermute | solution.py:549
  19.1 0.0 collective-permute-start.9
  19.1 0.0 collective-permute-done.2.refs_5_
  19.1 0.0 collective-permute-done.5.refs_9_
  19.1 0.0 collective-permute-done.13.refs_17_
  19.1 0.0 collective-permute-done.7.refs_11_
  19.1 1.3 %collective-permute-done.9.refs_13_ = bf16[400,128]{1,0:T(8,128)(2,1)S(1)} collective-permute-done((bf16[400,128]{1,0:T(8,128)(2,1)S(1)}, bf16[400,128]{1,0:T(8,128)(2,1)S(1)}, u32[]{:S(2)}, u32[]{:S(2)}) %collective-permute-start.9) | collective-permute-done | bytes 102432 | tf_op jit(solution)/shard_map/ppermute | solution.py:549
  20.4 15.0 %tile_backward.1 = (bf16[5,5,2,16,128]{4,3,2,1,0:T(8,128)(2,1)S(1)}, bf16[4,2,2,112,128]{4,3,2,1,0:T(8,128)(2,1)S(1)}, bf16[4,2,2,112,128]{4,3,2,1,0:T(8,128)(2,1)S(1)}) custom-call(s32[1]{0:T(128)} %bitcast.refs_0_.depth_ref, s32[1]{0:T(128)} %bitcast.1.odd.refs_1_, bf16[512,128]{1,0:T(8,128)(2,1)S(1)} %bitcast.28, ...), custom_call_target="tpu_custom_call" | custom-call | flops 9059696640 | bytes 6553600 | tf_op jit(solution)/shard_map/tile_backward/pallas_call | solution.py:523
  35.4 0.2 collective-permute-start.14
  35.6 1.7 %collective-permute-done.14 = bf16[4,2,2,112,128]{4,3,2,1,0:T(8,128)(2,1)S(1)} collective-permute-done((bf16[4,2,2,112,128]{4,3,2,1,0:T(8,128)(2,1)S(1)}, bf16[4,2,2,112,128]{4,3,2,1,0:T(8,128)(2,1)S(1)}, u32[]{:S(2)}, u32[]{:S(2)}) %collective-permute-start.14) | collective-permute-done | bytes 458784 | tf_op jit(solution)/shard_map/ppermute | solution.py:549
  37.3 0.1 convert_add_fusion
  37.4 0.0 copy-start.2
  37.4 0.1 fusion.2
  37.5 3.3 %collective-permute-start.15 = (bf16[2,2,112,128]{3,2,1,0:T(8,128)(2,1)S(1)}, bf16[2,2,112,128]{3,2,1,0:T(8,128)(2,1)S(1)}, u32[]{:S(2)}, u32[]{:S(2)}) collective-permute-start(bf16[2,2,112,128]{3,2,1,0:T(8,128)(2,1)S(1)} %get-tuple-element.19), channel_id=1, source_target_pairs={{0,4},{4,0},{8,12},{12,8},{16,20},{20,16},{24,28},{28,24},{1,5},{5... | collective-permute-start | bytes 344072 | tf_op jit(solution)/shard_map/ppermute | solution.py:549
  40.7 1.5 %collective-permute-start.16 = (bf16[2,2,112,128]{3,2,1,0:T(8,128)(2,1)S(1)}, bf16[2,2,112,128]{3,2,1,0:T(8,128)(2,1)S(1)}, u32[]{:S(2)}, u32[]{:S(2)}) collective-permute-start(bf16[2,2,112,128]{3,2,1,0:T(8,128)(2,1)S(1)} %get-tuple-element.21), channel_id=1, source_target_pairs={{0,8},{4,12},{8,0},{12,4},{16,24},{20,28},{24,16},{28,20},{1,9},{5... | collective-permute-start | bytes 344072 | tf_op jit(solution)/shard_map/ppermute | solution.py:549
  42.3 0.1 collective-permute-start.17
  42.3 1.8 %collective-permute-done.15 = bf16[2,2,112,128]{3,2,1,0:T(8,128)(2,1)S(1)} collective-permute-done((bf16[2,2,112,128]{3,2,1,0:T(8,128)(2,1)S(1)}, bf16[2,2,112,128]{3,2,1,0:T(8,128)(2,1)S(1)}, u32[]{:S(2)}, u32[]{:S(2)}) %collective-permute-start.15) | collective-permute-done | bytes 114720 | tf_op jit(solution)/shard_map/ppermute | solution.py:549
  44.2 2.6 %collective-permute-done.16 = bf16[2,2,112,128]{3,2,1,0:T(8,128)(2,1)S(1)} collective-permute-done((bf16[2,2,112,128]{3,2,1,0:T(8,128)(2,1)S(1)}, bf16[2,2,112,128]{3,2,1,0:T(8,128)(2,1)S(1)}, u32[]{:S(2)}, u32[]{:S(2)}) %collective-permute-start.16) | collective-permute-done | bytes 114720 | tf_op jit(solution)/shard_map/ppermute | solution.py:549
  46.8 1.2 %collective-permute-done.17 = bf16[2,2,112,128]{3,2,1,0:T(8,128)(2,1)S(1)} collective-permute-done((bf16[2,2,112,128]{3,2,1,0:T(8,128)(2,1)S(1)}, bf16[2,2,112,128]{3,2,1,0:T(8,128)(2,1)S(1)}, u32[]{:S(2)}, u32[]{:S(2)}) %collective-permute-start.17) | collective-permute-done | bytes 114720 | tf_op jit(solution)/shard_map/ppermute | solution.py:549
  48.0 0.1 fusion.1
  48.0 2.6 %collective-permute-start.18 = (bf16[2,112,128]{2,1,0:T(8,128)(2,1)S(1)}, bf16[2,112,128]{2,1,0:T(8,128)(2,1)S(1)}, u32[]{:S(2)}, u32[]{:S(2)}) collective-permute-start(bf16[2,112,128]{2,1,0:T(8,128)(2,1)S(1)} %fusion.5), channel_id=1, source_target_pairs={{0,16},{4,20},{8,24},{12,28},{16,0},{20,4},{24,8},{28,12},{1,17},{... | collective-permute-start | bytes 172040 | tf_op jit(solution)/shard_map/ppermute | solution.py:549
  50.7 0.0 copy-done.2
  50.7 1.8 %input_gradient.1 = bf16[512,128]{1,0:T(8,128)(2,1)} custom-call(s32[1]{0:T(128)} %bitcast.refs_0_.depth_ref, bf16[16,128]{1,0:T(8,128)(2,1)S(1)} %copy-done.3, bf16[5,5,2,16,128]{4,3,2,1,0:T(8,128)(2,1)S(1)} %get-tuple-element.16.last, bf16[27,128,128]{2,1,0:T(8,128)(2,1)S(1)} %copy-done.2), custom_call_target="tpu_custom_call" | custom-call | flops 603979776 | bytes 1409024 | tf_op jit(solution)/shard_map/input_gradient/pallas_call | solution.py:460
  52.5 0.7 %collective-permute-done.18 = bf16[2,112,128]{2,1,0:T(8,128)(2,1)S(1)} collective-permute-done((bf16[2,112,128]{2,1,0:T(8,128)(2,1)S(1)}, bf16[2,112,128]{2,1,0:T(8,128)(2,1)S(1)}, u32[]{:S(2)}, u32[]{:S(2)}) %collective-permute-start.18) | collective-permute-done | bytes 57376 | tf_op jit(solution)/shard_map/ppermute | solution.py:549
  53.2 0.6 %slice_bitcast_fusion = (f32[13824]{0:T(1024)}, f32[13824]{0:T(1024)}) fusion(f32[2,112,128]{2,1,0:T(8,128)S(1)} %bitcast_add_fusion.1), kind=kLoop, calls=%fused_computation.13 | loop fusion | bytes 221184 | tf_op jit(solution)/shard_map/reshape;squeeze | solution.py:590
  (7 shorter events, 0.0 us)
Async XLA Ops:
  0.6 7.5 %collective-permute-start.1 = (bf16[512,128]{1,0:T(8,128)(2,1)}, bf16[512,128]{1,0:T(8,128)(2,1)S(1)}, u32[]{:S(2)}, u32[]{:S(2)}) collective-permute-start(bf16[512,128]{1,0:T(8,128)(2,1)} %bitcast.25), channel_id=1, source_target_pairs={{0,2},{1,3},{2,0},{3,1},{4,6},{5,7},{6,4},{7,5},{8,10},{9,11},{10,... | collective-permute-start | bytes 393224 | tf_op jit(solution)/shard_map/ppermute | solution.py:549
  3.6 9.5 %collective-permute-start.4 = (bf16[512,128]{1,0:T(8,128)(2,1)}, bf16[512,128]{1,0:T(8,128)(2,1)S(1)}, u32[]{:S(2)}, u32[]{:S(2)}) collective-permute-start(bf16[512,128]{1,0:T(8,128)(2,1)} %bitcast.29), channel_id=1, source_target_pairs={{0,2},{1,3},{2,0},{3,1},{4,6},{5,7},{6,4},{7,5},{8,10},{9,11},{10,... | collective-permute-start | bytes 393224 | tf_op jit(solution)/shard_map/ppermute | solution.py:549
  3.7 7.4 %copy-start = (bf16[1,1,512,128]{3,2,1,0:T(8,128)(2,1)S(1)}, bf16[1,1,512,128]{3,2,1,0:T(8,128)(2,1)}, u32[]{:S(2)}) copy-start(bf16[1,1,512,128]{3,2,1,0:T(8,128)(2,1)} %param.6) | copy-start | bytes 393220
  3.7 7.4 %copy-start.1 = (bf16[1,1,512,128]{3,2,1,0:T(8,128)(2,1)S(1)}, bf16[1,1,512,128]{3,2,1,0:T(8,128)(2,1)}, u32[]{:S(2)}) copy-start(bf16[1,1,512,128]{3,2,1,0:T(8,128)(2,1)} %param.7) | copy-start | bytes 393220
  5.6 6.0 %collective-permute-start.10 = (bf16[400,128]{1,0:T(8,128)(2,1)}, bf16[400,128]{1,0:T(8,128)(2,1)S(1)}, u32[]{:S(2)}, u32[]{:S(2)}) collective-permute-start(bf16[400,128]{1,0:T(8,128)(2,1)} %get-tuple-element.15), channel_id=1, source_target_pairs={{4,8},{8,4},{12,16},{16,12},{20,24},{24,20},{5,9},{9,5},{13,17},{1... | collective-permute-start | bytes 307208 | tf_op jit(solution)/shard_map/ppermute | solution.py:557
  8.2 12.2 %copy-start.3 = (bf16[16,128]{1,0:T(8,128)(2,1)S(1)}, bf16[16,128]{1,0:T(8,128)(2,1)}, u32[]{:S(2)}) copy-start(bf16[16,128]{1,0:T(8,128)(2,1)} %get-tuple-element.11.refs_18_.own_table) | copy-start | bytes 12292
  8.2 6.3 %collective-permute-start.6 = (bf16[400,128]{1,0:T(8,128)(2,1)}, bf16[400,128]{1,0:T(8,128)(2,1)S(1)}, u32[]{:S(2)}, u32[]{:S(2)}) collective-permute-start(bf16[400,128]{1,0:T(8,128)(2,1)} %get-tuple-element.14), channel_id=1, source_target_pairs={{0,4},{4,0},{8,12},{12,8},{16,20},{20,16},{24,28},{28,24},{1,5},{5... | collective-permute-start | bytes 307208 | tf_op jit(solution)/shard_map/ppermute | solution.py:549
  11.1 4.9 %collective-permute-start = (bf16[512,128]{1,0:T(8,128)(2,1)S(1)}, bf16[512,128]{1,0:T(8,128)(2,1)S(1)}, u32[]{:S(2)}, u32[]{:S(2)}) collective-permute-start(bf16[512,128]{1,0:T(8,128)(2,1)S(1)} %bitcast.27), channel_id=1, source_target_pairs={{0,1},{1,0},{2,3},{3,2},{4,5},{5,4},{6,7},{7,6},{8,9},{9,8},{10,11... | collective-permute-start | bytes 393224 | tf_op jit(solution)/shard_map/ppermute | solution.py:549
  11.1 4.8 %collective-permute-start.3 = (bf16[512,128]{1,0:T(8,128)(2,1)S(1)}, bf16[512,128]{1,0:T(8,128)(2,1)S(1)}, u32[]{:S(2)}, u32[]{:S(2)}) collective-permute-start(bf16[512,128]{1,0:T(8,128)(2,1)S(1)} %bitcast.31), channel_id=1, source_target_pairs={{0,1},{1,0},{2,3},{3,2},{4,5},{5,4},{6,7},{7,6},{8,9},{9,8},{10,11... | collective-permute-start | bytes 393224 | tf_op jit(solution)/shard_map/ppermute | solution.py:549
  11.6 5.1 %collective-permute-start.12 = (bf16[400,128]{1,0:T(8,128)(2,1)S(1)}, bf16[400,128]{1,0:T(8,128)(2,1)S(1)}, u32[]{:S(2)}, u32[]{:S(2)}) collective-permute-start(bf16[400,128]{1,0:T(8,128)(2,1)S(1)} %collective-permute-done.10.refs_14_), channel_id=1, source_target_pairs={{0,2},{1,3},{2,0},{3,1},{4,6},{5,7},{6,4},{7,5},{8,10},{9,11},{10,... | collective-permute-start | bytes 307208 | tf_op jit(solution)/shard_map/ppermute | solution.py:549
  13.1 3.6 %collective-permute-start.11 = (bf16[400,128]{1,0:T(8,128)(2,1)S(1)}, bf16[400,128]{1,0:T(8,128)(2,1)S(1)}, u32[]{:S(2)}, u32[]{:S(2)}) collective-permute-start(bf16[400,128]{1,0:T(8,128)(2,1)S(1)} %collective-permute-done.10.refs_14_), channel_id=1, source_target_pairs={{0,1},{1,0},{2,3},{3,2},{4,5},{5,4},{6,7},{7,6},{8,9},{9,8},{10,11... | collective-permute-start | bytes 307208 | tf_op jit(solution)/shard_map/ppermute | solution.py:549
  14.4 4.7 %collective-permute-start.8 = (bf16[400,128]{1,0:T(8,128)(2,1)S(1)}, bf16[400,128]{1,0:T(8,128)(2,1)S(1)}, u32[]{:S(2)}, u32[]{:S(2)}) collective-permute-start(bf16[400,128]{1,0:T(8,128)(2,1)S(1)} %collective-permute-done.6.refs_10_), channel_id=1, source_target_pairs={{0,2},{1,3},{2,0},{3,1},{4,6},{5,7},{6,4},{7,5},{8,10},{9,11},{10,... | collective-permute-start | bytes 307208 | tf_op jit(solution)/shard_map/ppermute | solution.py:549
  15.9 3.2 %collective-permute-start.2 = (bf16[512,128]{1,0:T(8,128)(2,1)S(1)}, bf16[512,128]{1,0:T(8,128)(2,1)S(1)}, u32[]{:S(2)}, u32[]{:S(2)}) collective-permute-start(bf16[512,128]{1,0:T(8,128)(2,1)S(1)} %collective-permute-done.1.refs_4_), channel_id=1, source_target_pairs={{0,1},{1,0},{2,3},{3,2},{4,5},{5,4},{6,7},{7,6},{8,9},{9,8},{10,11... | collective-permute-start | bytes 393224 | tf_op jit(solution)/shard_map/ppermute | solution.py:549
  16.0 3.2 %collective-permute-start.5 = (bf16[512,128]{1,0:T(8,128)(2,1)S(1)}, bf16[512,128]{1,0:T(8,128)(2,1)S(1)}, u32[]{:S(2)}, u32[]{:S(2)}) collective-permute-start(bf16[512,128]{1,0:T(8,128)(2,1)S(1)} %collective-permute-done.4.refs_8_), channel_id=1, source_target_pairs={{0,1},{1,0},{2,3},{3,2},{4,5},{5,4},{6,7},{7,6},{8,9},{9,8},{10,11... | collective-permute-start | bytes 393224 | tf_op jit(solution)/shard_map/ppermute | solution.py:549
  16.7 2.5 %collective-permute-start.13 = (bf16[400,128]{1,0:T(8,128)(2,1)S(1)}, bf16[400,128]{1,0:T(8,128)(2,1)S(1)}, u32[]{:S(2)}, u32[]{:S(2)}) collective-permute-start(bf16[400,128]{1,0:T(8,128)(2,1)S(1)} %collective-permute-done.12.refs_16_), channel_id=1, source_target_pairs={{0,1},{1,0},{2,3},{3,2},{4,5},{5,4},{6,7},{7,6},{8,9},{9,8},{10,11... | collective-permute-start | bytes 307208 | tf_op jit(solution)/shard_map/ppermute | solution.py:549
  16.7 2.5 %collective-permute-start.7 = (bf16[400,128]{1,0:T(8,128)(2,1)S(1)}, bf16[400,128]{1,0:T(8,128)(2,1)S(1)}, u32[]{:S(2)}, u32[]{:S(2)}) collective-permute-start(bf16[400,128]{1,0:T(8,128)(2,1)S(1)} %collective-permute-done.6.refs_10_), channel_id=1, source_target_pairs={{0,1},{1,0},{2,3},{3,2},{4,5},{5,4},{6,7},{7,6},{8,9},{9,8},{10,11... | collective-permute-start | bytes 307208 | tf_op jit(solution)/shard_map/ppermute | solution.py:549
  19.1 1.3 %collective-permute-start.9 = (bf16[400,128]{1,0:T(8,128)(2,1)S(1)}, bf16[400,128]{1,0:T(8,128)(2,1)S(1)}, u32[]{:S(2)}, u32[]{:S(2)}) collective-permute-start(bf16[400,128]{1,0:T(8,128)(2,1)S(1)} %collective-permute-done.8.refs_12_), channel_id=1, source_target_pairs={{0,1},{1,0},{2,3},{3,2},{4,5},{5,4},{6,7},{7,6},{8,9},{9,8},{10,11... | collective-permute-start | bytes 307208 | tf_op jit(solution)/shard_map/ppermute | solution.py:549
  35.4 1.9 %collective-permute-start.14 = (bf16[4,2,2,112,128]{4,3,2,1,0:T(8,128)(2,1)S(1)}, bf16[4,2,2,112,128]{4,3,2,1,0:T(8,128)(2,1)S(1)}, u32[]{:S(2)}, u32[]{:S(2)}) collective-permute-start(bf16[4,2,2,112,128]{4,3,2,1,0:T(8,128)(2,1)S(1)} %get-tuple-element.18), channel_id=1, source_target_pairs={{0,1},{1,0},{2,3},{3,2},{4,5},{5,4},{6,7},{7,6},{8,9},{9,8},{10,11... | collective-permute-start | bytes 1376264 | tf_op jit(solution)/shard_map/ppermute | solution.py:549
  37.4 13.3 %copy-start.2 = (bf16[27,128,128]{2,1,0:T(8,128)(2,1)S(1)}, bf16[27,128,128]{2,1,0:T(8,128)(2,1)}, u32[]{:S(2)}) copy-start(bf16[27,128,128]{2,1,0:T(8,128)(2,1)} %far_first.1) | copy-start | bytes 2654212
  37.5 6.7 %collective-permute-start.15 = (bf16[2,2,112,128]{3,2,1,0:T(8,128)(2,1)S(1)}, bf16[2,2,112,128]{3,2,1,0:T(8,128)(2,1)S(1)}, u32[]{:S(2)}, u32[]{:S(2)}) collective-permute-start(bf16[2,2,112,128]{3,2,1,0:T(8,128)(2,1)S(1)} %get-tuple-element.19), channel_id=1, source_target_pairs={{0,4},{4,0},{8,12},{12,8},{16,20},{20,16},{24,28},{28,24},{1,5},{5... | collective-permute-start | bytes 344072 | tf_op jit(solution)/shard_map/ppermute | solution.py:549
  40.7 6.0 %collective-permute-start.16 = (bf16[2,2,112,128]{3,2,1,0:T(8,128)(2,1)S(1)}, bf16[2,2,112,128]{3,2,1,0:T(8,128)(2,1)S(1)}, u32[]{:S(2)}, u32[]{:S(2)}) collective-permute-start(bf16[2,2,112,128]{3,2,1,0:T(8,128)(2,1)S(1)} %get-tuple-element.21), channel_id=1, source_target_pairs={{0,8},{4,12},{8,0},{12,4},{16,24},{20,28},{24,16},{28,20},{1,9},{5... | collective-permute-start | bytes 344072 | tf_op jit(solution)/shard_map/ppermute | solution.py:549
  42.3 5.7 %collective-permute-start.17 = (bf16[2,2,112,128]{3,2,1,0:T(8,128)(2,1)S(1)}, bf16[2,2,112,128]{3,2,1,0:T(8,128)(2,1)S(1)}, u32[]{:S(2)}, u32[]{:S(2)}) collective-permute-start(bf16[2,2,112,128]{3,2,1,0:T(8,128)(2,1)S(1)} %get-tuple-element.20), channel_id=1, source_target_pairs={{0,12},{4,8},{8,4},{12,0},{16,28},{20,24},{24,20},{28,16},{1,13},{... | collective-permute-start | bytes 344072 | tf_op jit(solution)/shard_map/ppermute | solution.py:549
  48.0 5.1 %collective-permute-start.18 = (bf16[2,112,128]{2,1,0:T(8,128)(2,1)S(1)}, bf16[2,112,128]{2,1,0:T(8,128)(2,1)S(1)}, u32[]{:S(2)}, u32[]{:S(2)}) collective-permute-start(bf16[2,112,128]{2,1,0:T(8,128)(2,1)S(1)} %fusion.5), channel_id=1, source_target_pairs={{0,16},{4,20},{8,24},{12,28},{16,0},{20,4},{24,8},{28,12},{1,17},{... | collective-permute-start | bytes 172040 | tf_op jit(solution)/shard_map/ppermute | solution.py:549

commit v7 on v6

--- a/solution.py
+++ b/solution.py
@@ -229,19 +229,17 @@
 
 
 def place_slots(codes, blocks, offset, y_first, y_count, lifted, volume, mask, side):
-    for code, block in zip(codes, blocks):
-
-        @pl.when(code > 0)
-        def _():
-            z_first = HALO + (code - 1) * TE
-            rows = TE * TE * y_count
-            lifted[0:rows] = block[offset : offset + rows].astype(F32)
-            for z_at in range(TE):
-                for y_at in range(y_count):
-                    row = z_at * TE * y_count + y_at
-                    volume[z_first + z_at, y_first + y_at] = lifted[pl.ds(row, TE, stride=y_count)]
-            if mask is not None:
-                mask[side, pl.ds(z_first, TE)] = jnp.ones((TE,) + mask.shape[2:], F32)
+    spare = volume.shape[0] - TE
+    for at, (code, block) in enumerate(zip(codes, blocks)):
+        z_first = jnp.where(code > 0, HALO + (code - 1) * TE, spare)
+        rows = TE * TE * y_count
+        lifted[at, 0:rows] = block[offset : offset + rows].astype(F32)
+        for z_at in range(TE):
+            for y_at in range(y_count):
+                row = z_at * TE * y_count + y_at
+                volume[z_first + z_at, y_first + y_at] = lifted[at, pl.ds(row, TE, stride=y_count)]
+        if mask is not None:
+            mask[side, pl.ds(z_first, TE)] = jnp.ones((TE,) + mask.shape[2:], F32)
 
 
 def side_sizes():
@@ -255,10 +253,10 @@
     for rows, width, offset in ((feature_rows, HALO, 0), (upstream_rows, 2, face)):
         lifted[...] = rows[...].astype(F32).reshape(lifted.shape)
         count = TE * TE * width
-        high = lifted[:, TE - width :].reshape(count, channels)
-        low = lifted[:, :width].reshape(count, channels)
-        to_pair[offset : offset + count] = jnp.where(odd[0] == 1, low, high).astype(BF)
-        to_cross[offset : offset + count] = jnp.where(odd[0] == 1, high, low).astype(BF)
+        up_first = odd[0] * (TE - width)
+        low_first = (1 - odd[0]) * (TE - width)
+        to_cross[offset : offset + count] = lifted[:, pl.ds(up_first, width)].reshape(count, channels).astype(BF)
+        to_pair[offset : offset + count] = lifted[:, pl.ds(low_first, width)].reshape(count, channels).astype(BF)
     place = lax.broadcasted_iota(jnp.int32, (16, channels), 0)
     table = jnp.zeros((16, channels), F32)
     for slot in range(tile.shape[1]):
@@ -487,7 +485,7 @@
 def backward_call(own, up, pair, cross, own_table, kernels, depth_at, odd, columns, positions, tiles):
     channels = own[0].shape[-1]
     voxels = TE * TE * TE
-    planes = positions * TE + 2 * HALO
+    planes = positions * TE + 2 * HALO + TE
     span = TE + 2 * HALO
     inner = span // 2 - 1
     padded = -(-(27 * channels // (columns * len(own))) // 16) * 16
@@ -495,7 +493,7 @@
         pltpu.VMEM((planes, span, TE, channels), F32),
         pltpu.VMEM((planes, span, TE, channels), F32),
         pltpu.VMEM((3, planes, TE, channels), F32),
-        pltpu.VMEM((voxels + 16, channels), F32),
+        pltpu.VMEM((len(own), voxels + 16, channels), F32),
         pltpu.VMEM((inner, inner, 2 * TE, 2 * channels), F32),
         pltpu.VMEM((27 * channels + 16, channels), F32),
         pltpu.VMEM((27, channels, channels), BF),

time: 54 us -> 53.8 us (level)
  no operation moved by 1% of the time
where the time goes in v7:
time: 53.8 us; the launch traced here: 53.7 us
  starting transfers between devices  18.7 us (35%)
  Pallas kernels  18.6 us (35%)
  waiting for transfers between devices  14.7 us (27%)
  local copies, waits for them, and re-layouts  0.74 us (1%)
  between operations  0.74 us (1%)
    ppermute x18, starting transfers between devices, swap(): lax.ppermute(block, axis, [(i, i ^ bits) for i in range(lax.axis_size(axi...  18.1 us
    pallas_call x1, Pallas kernels, backward_call(): pl.pallas_call(body, out_shape=[jax.ShapeDtypeStruct((last // 2, last //...  14.9 us
    ppermute x18, waiting for transfers between devices, swap(): lax.ppermute(block, axis, [(i, i ^ bits) for i in range(lax.axis_size(axi...  14.7 us
    pallas_call x1, Pallas kernels, input_call(): pl.pallas_call(input_kernel, out_shape=jax.ShapeDtypeStruct((voxels, chan...  1.84 us
    pallas_call x1, Pallas kernels, sides_call(): pl.pallas_call(sides_kernel, out_shape=[side, side, jax.ShapeDtypeStruct(...  1.81 us
  transfers between devices with their start and end apart: 19, of which 10 were waited for; matrix products, arithmetic and copies ran while one was open for 0% of the time, Pallas kernels for 7%

profile of v7, /device:TPU:0, one launch (start us, length us, event | category | flops | bytes accessed | tf_op | source)
XLA Modules:
  0.0 53.7 jit_solution(10710755316101590567)
XLA Ops:
  0.6 3.0 %collective-permute-start.1 = (bf16[512,128]{1,0:T(8,128)(2,1)}, bf16[512,128]{1,0:T(8,128)(2,1)S(1)}, u32[]{:S(2)}, u32[]{:S(2)}) collective-permute-start(bf16[512,128]{1,0:T(8,128)(2,1)} %bitcast.25), channel_id=1, source_target_pairs={{0,2},{1,3},{2,0},{3,1},{4,6},{5,7},{6,4},{7,5},{8,10},{9,11},{10,... | collective-permute-start | bytes 393224 | tf_op jit(solution)/shard_map/ppermute | solution.py:547
  3.6 0.1 collective-permute-start.4
  3.7 1.8 %pack_sides.1 = (bf16[400,128]{1,0:T(8,128)(2,1)}, bf16[400,128]{1,0:T(8,128)(2,1)}, bf16[16,128]{1,0:T(8,128)(2,1)}) custom-call(s32[1,4]{1,0:T(1,128)} %tile.1, s32[1,4]{1,0:T(1,128)} %used.1, s32[1]{0:T(128)} %bitcast.1.odd.refs_1_, bf16[512,128]{1,0:T(8,128)(2,1)} %bitcast.26, bf16[512,128]{1,0:T(8,128)(2,1)} %bitcast.30), custom_call_target="tpu_custom_call" | custom-call | tf_op jit(solution)/shard_map/pack_sides/pallas_call | solution.py:274
  5.5 0.7 %collective-permute-start.10 = (bf16[400,128]{1,0:T(8,128)(2,1)}, bf16[400,128]{1,0:T(8,128)(2,1)S(1)}, u32[]{:S(2)}, u32[]{:S(2)}) collective-permute-start(bf16[400,128]{1,0:T(8,128)(2,1)} %get-tuple-element.15), channel_id=1, source_target_pairs={{4,8},{8,4},{12,16},{16,12},{20,24},{24,20},{5,9},{9,5},{13,17},{1... | collective-permute-start | bytes 307208 | tf_op jit(solution)/shard_map/ppermute | solution.py:555
  6.2 2.0 %collective-permute-done.1.refs_4_ = bf16[512,128]{1,0:T(8,128)(2,1)S(1)} collective-permute-done((bf16[512,128]{1,0:T(8,128)(2,1)}, bf16[512,128]{1,0:T(8,128)(2,1)S(1)}, u32[]{:S(2)}, u32[]{:S(2)}) %collective-permute-start.1) | collective-permute-done | bytes 131104 | tf_op jit(solution)/shard_map/ppermute | solution.py:547
  8.2 2.8 %collective-permute-start.6 = (bf16[400,128]{1,0:T(8,128)(2,1)}, bf16[400,128]{1,0:T(8,128)(2,1)S(1)}, u32[]{:S(2)}, u32[]{:S(2)}) collective-permute-start(bf16[400,128]{1,0:T(8,128)(2,1)} %get-tuple-element.14), channel_id=1, source_target_pairs={{0,4},{4,0},{8,12},{12,8},{16,20},{20,16},{24,28},{28,24},{1,5},{5... | collective-permute-start | bytes 307208 | tf_op jit(solution)/shard_map/ppermute | solution.py:547
  11.0 0.0 copy-done
  11.0 0.0 collective-permute-start
  11.0 0.0 copy-done.1
  11.0 0.5 collective-permute-start.3
  11.5 0.0 collective-permute-done.10.refs_14_
  11.5 1.5 %collective-permute-start.12 = (bf16[400,128]{1,0:T(8,128)(2,1)S(1)}, bf16[400,128]{1,0:T(8,128)(2,1)S(1)}, u32[]{:S(2)}, u32[]{:S(2)}) collective-permute-start(bf16[400,128]{1,0:T(8,128)(2,1)S(1)} %collective-permute-done.10.refs_14_), channel_id=1, source_target_pairs={{0,2},{1,3},{2,0},{3,1},{4,6},{5,7},{6,4},{7,5},{8,10},{9,11},{10,... | collective-permute-start | bytes 307208 | tf_op jit(solution)/shard_map/ppermute | solution.py:547
  13.0 0.0 collective-permute-done.4.refs_8_
  13.0 0.0 collective-permute-start.11
  13.0 1.3 %collective-permute-done.6.refs_10_ = bf16[400,128]{1,0:T(8,128)(2,1)S(1)} collective-permute-done((bf16[400,128]{1,0:T(8,128)(2,1)}, bf16[400,128]{1,0:T(8,128)(2,1)S(1)}, u32[]{:S(2)}, u32[]{:S(2)}) %collective-permute-start.6) | collective-permute-done | bytes 102432 | tf_op jit(solution)/shard_map/ppermute | solution.py:547
  14.4 1.5 %collective-permute-start.8 = (bf16[400,128]{1,0:T(8,128)(2,1)S(1)}, bf16[400,128]{1,0:T(8,128)(2,1)S(1)}, u32[]{:S(2)}, u32[]{:S(2)}) collective-permute-start(bf16[400,128]{1,0:T(8,128)(2,1)S(1)} %collective-permute-done.6.refs_10_), channel_id=1, source_target_pairs={{0,2},{1,3},{2,0},{3,1},{4,6},{5,7},{6,4},{7,5},{8,10},{9,11},{10,... | collective-permute-start | bytes 307208 | tf_op jit(solution)/shard_map/ppermute | solution.py:547
  15.9 0.0 collective-permute-done.refs_3_
  15.9 0.0 collective-permute-start.2
  15.9 0.0 collective-permute-done.3.refs_7_
  15.9 0.5 collective-permute-start.5
  16.4 0.2 collective-permute-done.12.refs_16_
  16.6 0.0 collective-permute-start.13
  16.6 0.0 collective-permute-done.11.refs_15_
  16.6 0.5 collective-permute-start.7
  17.1 1.9 %collective-permute-done.8.refs_12_ = bf16[400,128]{1,0:T(8,128)(2,1)S(1)} collective-permute-done((bf16[400,128]{1,0:T(8,128)(2,1)S(1)}, bf16[400,128]{1,0:T(8,128)(2,1)S(1)}, u32[]{:S(2)}, u32[]{:S(2)}) %collective-permute-start.8) | collective-permute-done | bytes 102432 | tf_op jit(solution)/shard_map/ppermute | solution.py:547
  19.0 0.0 collective-permute-start.9
  19.0 0.0 collective-permute-done.2.refs_5_
  19.0 0.0 collective-permute-done.5.refs_9_
  19.1 0.0 collective-permute-done.13.refs_17_
  19.1 0.0 collective-permute-done.7.refs_11_
  19.1 1.3 %collective-permute-done.9.refs_13_ = bf16[400,128]{1,0:T(8,128)(2,1)S(1)} collective-permute-done((bf16[400,128]{1,0:T(8,128)(2,1)S(1)}, bf16[400,128]{1,0:T(8,128)(2,1)S(1)}, u32[]{:S(2)}, u32[]{:S(2)}) %collective-permute-start.9) | collective-permute-done | bytes 102432 | tf_op jit(solution)/shard_map/ppermute | solution.py:547
  20.3 14.9 %tile_backward.1 = (bf16[5,5,2,16,128]{4,3,2,1,0:T(8,128)(2,1)S(1)}, bf16[4,2,2,112,128]{4,3,2,1,0:T(8,128)(2,1)S(1)}, bf16[4,2,2,112,128]{4,3,2,1,0:T(8,128)(2,1)S(1)}) custom-call(s32[1]{0:T(128)} %bitcast.refs_0_.depth_ref, s32[1]{0:T(128)} %bitcast.1.odd.refs_1_, bf16[512,128]{1,0:T(8,128)(2,1)S(1)} %bitcast.28, ...), custom_call_target="tpu_custom_call" | custom-call | flops 9059696640 | bytes 6553600 | tf_op jit(solution)/shard_map/tile_backward/pallas_call | solution.py:521
  35.3 0.2 collective-permute-start.14
  35.5 1.7 %collective-permute-done.14 = bf16[4,2,2,112,128]{4,3,2,1,0:T(8,128)(2,1)S(1)} collective-permute-done((bf16[4,2,2,112,128]{4,3,2,1,0:T(8,128)(2,1)S(1)}, bf16[4,2,2,112,128]{4,3,2,1,0:T(8,128)(2,1)S(1)}, u32[]{:S(2)}, u32[]{:S(2)}) %collective-permute-start.14) | collective-permute-done | bytes 458784 | tf_op jit(solution)/shard_map/ppermute | solution.py:547
  37.2 0.1 convert_add_fusion
  37.3 0.0 copy-start.2
  37.3 0.1 fusion.2
  37.4 3.1 %collective-permute-start.15 = (bf16[2,2,112,128]{3,2,1,0:T(8,128)(2,1)S(1)}, bf16[2,2,112,128]{3,2,1,0:T(8,128)(2,1)S(1)}, u32[]{:S(2)}, u32[]{:S(2)}) collective-permute-start(bf16[2,2,112,128]{3,2,1,0:T(8,128)(2,1)S(1)} %get-tuple-element.19), channel_id=1, source_target_pairs={{0,4},{4,0},{8,12},{12,8},{16,20},{20,16},{24,28},{28,24},{1,5},{5... | collective-permute-start | bytes 344072 | tf_op jit(solution)/shard_map/ppermute | solution.py:547
  40.5 1.6 %collective-permute-start.16 = (bf16[2,2,112,128]{3,2,1,0:T(8,128)(2,1)S(1)}, bf16[2,2,112,128]{3,2,1,0:T(8,128)(2,1)S(1)}, u32[]{:S(2)}, u32[]{:S(2)}) collective-permute-start(bf16[2,2,112,128]{3,2,1,0:T(8,128)(2,1)S(1)} %get-tuple-element.21), channel_id=1, source_target_pairs={{0,8},{4,12},{8,0},{12,4},{16,24},{20,28},{24,16},{28,20},{1,9},{5... | collective-permute-start | bytes 344072 | tf_op jit(solution)/shard_map/ppermute | solution.py:547
  42.1 0.0 collective-permute-start.17
  42.1 1.9 %collective-permute-done.15 = bf16[2,2,112,128]{3,2,1,0:T(8,128)(2,1)S(1)} collective-permute-done((bf16[2,2,112,128]{3,2,1,0:T(8,128)(2,1)S(1)}, bf16[2,2,112,128]{3,2,1,0:T(8,128)(2,1)S(1)}, u32[]{:S(2)}, u32[]{:S(2)}) %collective-permute-start.15) | collective-permute-done | bytes 114720 | tf_op jit(solution)/shard_map/ppermute | solution.py:547
  44.0 2.6 %collective-permute-done.16 = bf16[2,2,112,128]{3,2,1,0:T(8,128)(2,1)S(1)} collective-permute-done((bf16[2,2,112,128]{3,2,1,0:T(8,128)(2,1)S(1)}, bf16[2,2,112,128]{3,2,1,0:T(8,128)(2,1)S(1)}, u32[]{:S(2)}, u32[]{:S(2)}) %collective-permute-start.16) | collective-permute-done | bytes 114720 | tf_op jit(solution)/shard_map/ppermute | solution.py:547
  46.5 1.2 %collective-permute-done.17 = bf16[2,2,112,128]{3,2,1,0:T(8,128)(2,1)S(1)} collective-permute-done((bf16[2,2,112,128]{3,2,1,0:T(8,128)(2,1)S(1)}, bf16[2,2,112,128]{3,2,1,0:T(8,128)(2,1)S(1)}, u32[]{:S(2)}, u32[]{:S(2)}) %collective-permute-start.17) | collective-permute-done | bytes 114720 | tf_op jit(solution)/shard_map/ppermute | solution.py:547
  47.8 0.1 fusion.1
  47.9 2.7 %collective-permute-start.18 = (bf16[2,112,128]{2,1,0:T(8,128)(2,1)S(1)}, bf16[2,112,128]{2,1,0:T(8,128)(2,1)S(1)}, u32[]{:S(2)}, u32[]{:S(2)}) collective-permute-start(bf16[2,112,128]{2,1,0:T(8,128)(2,1)S(1)} %fusion.5), channel_id=1, source_target_pairs={{0,16},{4,20},{8,24},{12,28},{16,0},{20,4},{24,8},{28,12},{1,17},{... | collective-permute-start | bytes 172040 | tf_op jit(solution)/shard_map/ppermute | solution.py:547
  50.6 1.8 %input_gradient.1 = bf16[512,128]{1,0:T(8,128)(2,1)} custom-call(s32[1]{0:T(128)} %bitcast.refs_0_.depth_ref, bf16[16,128]{1,0:T(8,128)(2,1)S(1)} %copy-done.3, bf16[5,5,2,16,128]{4,3,2,1,0:T(8,128)(2,1)S(1)} %get-tuple-element.16.last, bf16[27,128,128]{2,1,0:T(8,128)(2,1)S(1)} %copy-done.2), custom_call_target="tpu_custom_call" | custom-call | flops 603979776 | bytes 1409024 | tf_op jit(solution)/shard_map/input_gradient/pallas_call | solution.py:458
  52.4 0.6 %collective-permute-done.18 = bf16[2,112,128]{2,1,0:T(8,128)(2,1)S(1)} collective-permute-done((bf16[2,112,128]{2,1,0:T(8,128)(2,1)S(1)}, bf16[2,112,128]{2,1,0:T(8,128)(2,1)S(1)}, u32[]{:S(2)}, u32[]{:S(2)}) %collective-permute-start.18) | collective-permute-done | bytes 57376 | tf_op jit(solution)/shard_map/ppermute | solution.py:547
  53.0 0.6 %slice_bitcast_fusion = (f32[13824]{0:T(1024)}, f32[13824]{0:T(1024)}) fusion(f32[2,112,128]{2,1,0:T(8,128)S(1)} %bitcast_add_fusion.1), kind=kLoop, calls=%fused_computation.13 | loop fusion | bytes 221184 | tf_op jit(solution)/shard_map/reshape;squeeze | solution.py:588
  (7 shorter events, 0.0 us)
Async XLA Ops:
  0.6 7.5 %collective-permute-start.1 = (bf16[512,128]{1,0:T(8,128)(2,1)}, bf16[512,128]{1,0:T(8,128)(2,1)S(1)}, u32[]{:S(2)}, u32[]{:S(2)}) collective-permute-start(bf16[512,128]{1,0:T(8,128)(2,1)} %bitcast.25), channel_id=1, source_target_pairs={{0,2},{1,3},{2,0},{3,1},{4,6},{5,7},{6,4},{7,5},{8,10},{9,11},{10,... | collective-permute-start | bytes 393224 | tf_op jit(solution)/shard_map/ppermute | solution.py:547
  3.6 9.4 %collective-permute-start.4 = (bf16[512,128]{1,0:T(8,128)(2,1)}, bf16[512,128]{1,0:T(8,128)(2,1)S(1)}, u32[]{:S(2)}, u32[]{:S(2)}) collective-permute-start(bf16[512,128]{1,0:T(8,128)(2,1)} %bitcast.29), channel_id=1, source_target_pairs={{0,2},{1,3},{2,0},{3,1},{4,6},{5,7},{6,4},{7,5},{8,10},{9,11},{10,... | collective-permute-start | bytes 393224 | tf_op jit(solution)/shard_map/ppermute | solution.py:547
  3.7 7.3 %copy-start = (bf16[1,1,512,128]{3,2,1,0:T(8,128)(2,1)S(1)}, bf16[1,1,512,128]{3,2,1,0:T(8,128)(2,1)}, u32[]{:S(2)}) copy-start(bf16[1,1,512,128]{3,2,1,0:T(8,128)(2,1)} %param.6) | copy-start | bytes 393220
  3.7 7.3 %copy-start.1 = (bf16[1,1,512,128]{3,2,1,0:T(8,128)(2,1)S(1)}, bf16[1,1,512,128]{3,2,1,0:T(8,128)(2,1)}, u32[]{:S(2)}) copy-start(bf16[1,1,512,128]{3,2,1,0:T(8,128)(2,1)} %param.7) | copy-start | bytes 393220
  5.5 6.0 %collective-permute-start.10 = (bf16[400,128]{1,0:T(8,128)(2,1)}, bf16[400,128]{1,0:T(8,128)(2,1)S(1)}, u32[]{:S(2)}, u32[]{:S(2)}) collective-permute-start(bf16[400,128]{1,0:T(8,128)(2,1)} %get-tuple-element.15), channel_id=1, source_target_pairs={{4,8},{8,4},{12,16},{16,12},{20,24},{24,20},{5,9},{9,5},{13,17},{1... | collective-permute-start | bytes 307208 | tf_op jit(solution)/shard_map/ppermute | solution.py:555
  8.2 12.2 %copy-start.3 = (bf16[16,128]{1,0:T(8,128)(2,1)S(1)}, bf16[16,128]{1,0:T(8,128)(2,1)}, u32[]{:S(2)}) copy-start(bf16[16,128]{1,0:T(8,128)(2,1)} %get-tuple-element.11.refs_18_.own_table) | copy-start | bytes 12292
  8.2 6.2 %collective-permute-start.6 = (bf16[400,128]{1,0:T(8,128)(2,1)}, bf16[400,128]{1,0:T(8,128)(2,1)S(1)}, u32[]{:S(2)}, u32[]{:S(2)}) collective-permute-start(bf16[400,128]{1,0:T(8,128)(2,1)} %get-tuple-element.14), channel_id=1, source_target_pairs={{0,4},{4,0},{8,12},{12,8},{16,20},{20,16},{24,28},{28,24},{1,5},{5... | collective-permute-start | bytes 307208 | tf_op jit(solution)/shard_map/ppermute | solution.py:547
  11.0 4.9 %collective-permute-start = (bf16[512,128]{1,0:T(8,128)(2,1)S(1)}, bf16[512,128]{1,0:T(8,128)(2,1)S(1)}, u32[]{:S(2)}, u32[]{:S(2)}) collective-permute-start(bf16[512,128]{1,0:T(8,128)(2,1)S(1)} %bitcast.27), channel_id=1, source_target_pairs={{0,1},{1,0},{2,3},{3,2},{4,5},{5,4},{6,7},{7,6},{8,9},{9,8},{10,11... | collective-permute-start | bytes 393224 | tf_op jit(solution)/shard_map/ppermute | solution.py:547
  11.0 4.8 %collective-permute-start.3 = (bf16[512,128]{1,0:T(8,128)(2,1)S(1)}, bf16[512,128]{1,0:T(8,128)(2,1)S(1)}, u32[]{:S(2)}, u32[]{:S(2)}) collective-permute-start(bf16[512,128]{1,0:T(8,128)(2,1)S(1)} %bitcast.31), channel_id=1, source_target_pairs={{0,1},{1,0},{2,3},{3,2},{4,5},{5,4},{6,7},{7,6},{8,9},{9,8},{10,11... | collective-permute-start | bytes 393224 | tf_op jit(solution)/shard_map/ppermute | solution.py:547
  11.5 5.1 %collective-permute-start.12 = (bf16[400,128]{1,0:T(8,128)(2,1)S(1)}, bf16[400,128]{1,0:T(8,128)(2,1)S(1)}, u32[]{:S(2)}, u32[]{:S(2)}) collective-permute-start(bf16[400,128]{1,0:T(8,128)(2,1)S(1)} %collective-permute-done.10.refs_14_), channel_id=1, source_target_pairs={{0,2},{1,3},{2,0},{3,1},{4,6},{5,7},{6,4},{7,5},{8,10},{9,11},{10,... | collective-permute-start | bytes 307208 | tf_op jit(solution)/shard_map/ppermute | solution.py:547
  13.0 3.6 %collective-permute-start.11 = (bf16[400,128]{1,0:T(8,128)(2,1)S(1)}, bf16[400,128]{1,0:T(8,128)(2,1)S(1)}, u32[]{:S(2)}, u32[]{:S(2)}) collective-permute-start(bf16[400,128]{1,0:T(8,128)(2,1)S(1)} %collective-permute-done.10.refs_14_), channel_id=1, source_target_pairs={{0,1},{1,0},{2,3},{3,2},{4,5},{5,4},{6,7},{7,6},{8,9},{9,8},{10,11... | collective-permute-start | bytes 307208 | tf_op jit(solution)/shard_map/ppermute | solution.py:547
  14.4 4.7 %collective-permute-start.8 = (bf16[400,128]{1,0:T(8,128)(2,1)S(1)}, bf16[400,128]{1,0:T(8,128)(2,1)S(1)}, u32[]{:S(2)}, u32[]{:S(2)}) collective-permute-start(bf16[400,128]{1,0:T(8,128)(2,1)S(1)} %collective-permute-done.6.refs_10_), channel_id=1, source_target_pairs={{0,2},{1,3},{2,0},{3,1},{4,6},{5,7},{6,4},{7,5},{8,10},{9,11},{10,... | collective-permute-start | bytes 307208 | tf_op jit(solution)/shard_map/ppermute | solution.py:547
  15.9 3.2 %collective-permute-start.2 = (bf16[512,128]{1,0:T(8,128)(2,1)S(1)}, bf16[512,128]{1,0:T(8,128)(2,1)S(1)}, u32[]{:S(2)}, u32[]{:S(2)}) collective-permute-start(bf16[512,128]{1,0:T(8,128)(2,1)S(1)} %collective-permute-done.1.refs_4_), channel_id=1, source_target_pairs={{0,1},{1,0},{2,3},{3,2},{4,5},{5,4},{6,7},{7,6},{8,9},{9,8},{10,11... | collective-permute-start | bytes 393224 | tf_op jit(solution)/shard_map/ppermute | solution.py:547
  15.9 3.2 %collective-permute-start.5 = (bf16[512,128]{1,0:T(8,128)(2,1)S(1)}, bf16[512,128]{1,0:T(8,128)(2,1)S(1)}, u32[]{:S(2)}, u32[]{:S(2)}) collective-permute-start(bf16[512,128]{1,0:T(8,128)(2,1)S(1)} %collective-permute-done.4.refs_8_), channel_id=1, source_target_pairs={{0,1},{1,0},{2,3},{3,2},{4,5},{5,4},{6,7},{7,6},{8,9},{9,8},{10,11... | collective-permute-start | bytes 393224 | tf_op jit(solution)/shard_map/ppermute | solution.py:547
  16.6 2.5 %collective-permute-start.13 = (bf16[400,128]{1,0:T(8,128)(2,1)S(1)}, bf16[400,128]{1,0:T(8,128)(2,1)S(1)}, u32[]{:S(2)}, u32[]{:S(2)}) collective-permute-start(bf16[400,128]{1,0:T(8,128)(2,1)S(1)} %collective-permute-done.12.refs_16_), channel_id=1, source_target_pairs={{0,1},{1,0},{2,3},{3,2},{4,5},{5,4},{6,7},{7,6},{8,9},{9,8},{10,11... | collective-permute-start | bytes 307208 | tf_op jit(solution)/shard_map/ppermute | solution.py:547
  16.6 2.5 %collective-permute-start.7 = (bf16[400,128]{1,0:T(8,128)(2,1)S(1)}, bf16[400,128]{1,0:T(8,128)(2,1)S(1)}, u32[]{:S(2)}, u32[]{:S(2)}) collective-permute-start(bf16[400,128]{1,0:T(8,128)(2,1)S(1)} %collective-permute-done.6.refs_10_), channel_id=1, source_target_pairs={{0,1},{1,0},{2,3},{3,2},{4,5},{5,4},{6,7},{7,6},{8,9},{9,8},{10,11... | collective-permute-start | bytes 307208 | tf_op jit(solution)/shard_map/ppermute | solution.py:547
  19.0 1.3 %collective-permute-start.9 = (bf16[400,128]{1,0:T(8,128)(2,1)S(1)}, bf16[400,128]{1,0:T(8,128)(2,1)S(1)}, u32[]{:S(2)}, u32[]{:S(2)}) collective-permute-start(bf16[400,128]{1,0:T(8,128)(2,1)S(1)} %collective-permute-done.8.refs_12_), channel_id=1, source_target_pairs={{0,1},{1,0},{2,3},{3,2},{4,5},{5,4},{6,7},{7,6},{8,9},{9,8},{10,11... | collective-permute-start | bytes 307208 | tf_op jit(solution)/shard_map/ppermute | solution.py:547
  35.3 1.9 %collective-permute-start.14 = (bf16[4,2,2,112,128]{4,3,2,1,0:T(8,128)(2,1)S(1)}, bf16[4,2,2,112,128]{4,3,2,1,0:T(8,128)(2,1)S(1)}, u32[]{:S(2)}, u32[]{:S(2)}) collective-permute-start(bf16[4,2,2,112,128]{4,3,2,1,0:T(8,128)(2,1)S(1)} %get-tuple-element.18), channel_id=1, source_target_pairs={{0,1},{1,0},{2,3},{3,2},{4,5},{5,4},{6,7},{7,6},{8,9},{9,8},{10,11... | collective-permute-start | bytes 1376264 | tf_op jit(solution)/shard_map/ppermute | solution.py:547
  37.3 13.3 %copy-start.2 = (bf16[27,128,128]{2,1,0:T(8,128)(2,1)S(1)}, bf16[27,128,128]{2,1,0:T(8,128)(2,1)}, u32[]{:S(2)}) copy-start(bf16[27,128,128]{2,1,0:T(8,128)(2,1)} %far_first.1) | copy-start | bytes 2654212
  37.4 6.6 %collective-permute-start.15 = (bf16[2,2,112,128]{3,2,1,0:T(8,128)(2,1)S(1)}, bf16[2,2,112,128]{3,2,1,0:T(8,128)(2,1)S(1)}, u32[]{:S(2)}, u32[]{:S(2)}) collective-permute-start(bf16[2,2,112,128]{3,2,1,0:T(8,128)(2,1)S(1)} %get-tuple-element.19), channel_id=1, source_target_pairs={{0,4},{4,0},{8,12},{12,8},{16,20},{20,16},{24,28},{28,24},{1,5},{5... | collective-permute-start | bytes 344072 | tf_op jit(solution)/shard_map/ppermute | solution.py:547
  40.5 6.0 %collective-permute-start.16 = (bf16[2,2,112,128]{3,2,1,0:T(8,128)(2,1)S(1)}, bf16[2,2,112,128]{3,2,1,0:T(8,128)(2,1)S(1)}, u32[]{:S(2)}, u32[]{:S(2)}) collective-permute-start(bf16[2,2,112,128]{3,2,1,0:T(8,128)(2,1)S(1)} %get-tuple-element.21), channel_id=1, source_target_pairs={{0,8},{4,12},{8,0},{12,4},{16,24},{20,28},{24,16},{28,20},{1,9},{5... | collective-permute-start | bytes 344072 | tf_op jit(solution)/shard_map/ppermute | solution.py:547
  42.1 5.7 %collective-permute-start.17 = (bf16[2,2,112,128]{3,2,1,0:T(8,128)(2,1)S(1)}, bf16[2,2,112,128]{3,2,1,0:T(8,128)(2,1)S(1)}, u32[]{:S(2)}, u32[]{:S(2)}) collective-permute-start(bf16[2,2,112,128]{3,2,1,0:T(8,128)(2,1)S(1)} %get-tuple-element.20), channel_id=1, source_target_pairs={{0,12},{4,8},{8,4},{12,0},{16,28},{20,24},{24,20},{28,16},{1,13},{... | collective-permute-start | bytes 344072 | tf_op jit(solution)/shard_map/ppermute | solution.py:547
  47.9 5.1 %collective-permute-start.18 = (bf16[2,112,128]{2,1,0:T(8,128)(2,1)S(1)}, bf16[2,112,128]{2,1,0:T(8,128)(2,1)S(1)}, u32[]{:S(2)}, u32[]{:S(2)}) collective-permute-start(bf16[2,112,128]{2,1,0:T(8,128)(2,1)S(1)} %fusion.5), channel_id=1, source_target_pairs={{0,16},{4,20},{8,24},{12,28},{16,0},{20,4},{24,8},{28,12},{1,17},{... | collective-permute-start | bytes 172040 | tf_op jit(solution)/shard_map/ppermute | solution.py:547

commit v8 on v7

--- a/solution.py
+++ b/solution.py
@@ -296,18 +296,17 @@
     def take():
         return rest.pop(0)
 
-    volume, upstream, mask, lifted, result, grad_rows, first_kernel, second_kernel, near_own, near_up, sems = (
-        take() for _ in range(11)
+    volume, upstream, mask, lifted, result, grad_rows, first_kernel, second_kernel, sems = (
+        take() for _ in range(9)
     )
     fetches = [
         pltpu.make_async_copy(far, near, sems.at[at])
         for at, (far, near) in enumerate(
-            ((own[0], near_own), (up[0], near_up), (far_first, first_kernel), (far_second, second_kernel))
+            ((far_first, first_kernel), (far_second, second_kernel))
         )
     ]
     for fetch in fetches:
         fetch.start()
-    own[0], up[0] = near_own, near_up
     regions = []
     for number in range(tiles):
         halo = HALO - number
@@ -337,9 +336,7 @@
         y_upstream = (1 - low) * (TE + 2) + HALO - 2
         place_slots(codes, blocks, 0, y_feature, HALO, lifted, volume, mask, side)
         place_slots(codes, blocks, face, y_upstream, 2, lifted, upstream, None, side)
-    fetches[0].wait()
     place_slots(held, own, 0, HALO, TE, lifted, volume, mask, 1)
-    fetches[1].wait()
     place_slots(held, up, 0, HALO, TE, lifted, upstream, None, 1)
 
     starts = []
@@ -413,11 +410,11 @@
                     out[near_at, far_at, at] = rows.astype(BF)
 
     grad_rows[27 * channels :] = jnp.zeros_like(grad_rows[27 * channels :])
-    fetches[2].wait()
+    fetches[0].wait()
     for number in range(tiles):
         convolve_region(regions[number][0], first_kernel, False, result)
         finish_layer(number, 1, "act")
-    fetches[3].wait()
+    fetches[1].wait()
     for number in range(tiles):
         convolve_region(regions[number][1], second_kernel, False, result)
         finish_layer(number, 2, "delta_two")
@@ -498,9 +495,7 @@
         pltpu.VMEM((27 * channels + 16, channels), F32),
         pltpu.VMEM((27, channels, channels), BF),
         pltpu.VMEM((27, channels, channels), BF),
-        pltpu.VMEM((voxels, channels), BF),
-        pltpu.VMEM((voxels, channels), BF),
-        pltpu.SemaphoreType.DMA((4,)),
+        pltpu.SemaphoreType.DMA((2,)),
     ]
     for number in range(tiles):
         for layer in range(4):
@@ -525,7 +520,7 @@
             share,
             share,
         ],
-        in_specs=[smem, smem] + ([hbm] + [vmem] * (len(own) - 1)) * 2 + [vmem] * (len(pair) + len(cross) + 1) + [hbm, hbm],
+        in_specs=[smem, smem] + [vmem] * (len(own) + len(up) + len(pair) + len(cross) + 1) + [hbm, hbm],
         out_specs=[vmem] * 3,
         scratch_shapes=scratch,
         compiler_params=pltpu.CompilerParams(vmem_limit_bytes=VMEM_LIMIT),

time: 53.8 us -> 53.4 us (level)
  no operation moved by 1% of the time
where the time goes in v8:
time: 53.4 us; the launch traced here: 53.2 us
  starting transfers between devices  18.7 us (35%)
  Pallas kernels  18.2 us (34%)
  waiting for transfers between devices  14.7 us (28%)
  local copies, waits for them, and re-layouts  0.74 us (1%)
  between operations  0.74 us (1%)
    ppermute x18, starting transfers between devices, swap(): lax.ppermute(block, axis, [(i, i ^ bits) for i in range(lax.axis_size(axi...  18.1 us
    ppermute x18, waiting for transfers between devices, swap(): lax.ppermute(block, axis, [(i, i ^ bits) for i in range(lax.axis_size(axi...  14.7 us
    pallas_call x1, Pallas kernels, backward_call(): pl.pallas_call(body, out_shape=[jax.ShapeDtypeStruct((last // 2, last //...  14.5 us
    pallas_call x1, Pallas kernels, input_call(): pl.pallas_call(input_kernel, out_shape=jax.ShapeDtypeStruct((voxels, chan...  1.84 us
    pallas_call x1, Pallas kernels, sides_call(): pl.pallas_call(sides_kernel, out_shape=[side, side, jax.ShapeDtypeStruct(...  1.81 us
  transfers between devices with their start and end apart: 19, of which 10 were waited for; matrix products, arithmetic and copies ran while one was open for 0% of the time, Pallas kernels for 7%

profile of v8, /device:TPU:0, one launch (start us, length us, event | category | flops | bytes accessed | tf_op | source)
XLA Modules:
  0.0 53.2 jit_solution(2496814940745543453)
XLA Ops:
  0.6 3.0 %collective-permute-start.1 = (bf16[512,128]{1,0:T(8,128)(2,1)}, bf16[512,128]{1,0:T(8,128)(2,1)S(1)}, u32[]{:S(2)}, u32[]{:S(2)}) collective-permute-start(bf16[512,128]{1,0:T(8,128)(2,1)} %bitcast.25), channel_id=1, source_target_pairs={{0,2},{1,3},{2,0},{3,1},{4,6},{5,7},{6,4},{7,5},{8,10},{9,11},{10,... | collective-permute-start | bytes 393224 | tf_op jit(solution)/shard_map/ppermute | solution.py:542
  3.6 0.1 collective-permute-start.4
  3.7 1.8 %pack_sides.1 = (bf16[400,128]{1,0:T(8,128)(2,1)}, bf16[400,128]{1,0:T(8,128)(2,1)}, bf16[16,128]{1,0:T(8,128)(2,1)}) custom-call(s32[1,4]{1,0:T(1,128)} %tile.1, s32[1,4]{1,0:T(1,128)} %used.1, s32[1]{0:T(128)} %bitcast.1.odd.refs_1_, bf16[512,128]{1,0:T(8,128)(2,1)} %bitcast.26, bf16[512,128]{1,0:T(8,128)(2,1)} %bitcast.30), custom_call_target="tpu_custom_call" | custom-call | tf_op jit(solution)/shard_map/pack_sides/pallas_call | solution.py:274
  5.5 0.7 %collective-permute-start.10 = (bf16[400,128]{1,0:T(8,128)(2,1)}, bf16[400,128]{1,0:T(8,128)(2,1)S(1)}, u32[]{:S(2)}, u32[]{:S(2)}) collective-permute-start(bf16[400,128]{1,0:T(8,128)(2,1)} %get-tuple-element.15), channel_id=1, source_target_pairs={{4,8},{8,4},{12,16},{16,12},{20,24},{24,20},{5,9},{9,5},{13,17},{1... | collective-permute-start | bytes 307208 | tf_op jit(solution)/shard_map/ppermute | solution.py:550
  6.2 2.0 %collective-permute-done.1.refs_4_ = bf16[512,128]{1,0:T(8,128)(2,1)S(1)} collective-permute-done((bf16[512,128]{1,0:T(8,128)(2,1)}, bf16[512,128]{1,0:T(8,128)(2,1)S(1)}, u32[]{:S(2)}, u32[]{:S(2)}) %collective-permute-start.1) | collective-permute-done | bytes 131104 | tf_op jit(solution)/shard_map/ppermute | solution.py:542
  8.2 2.8 %collective-permute-start.6 = (bf16[400,128]{1,0:T(8,128)(2,1)}, bf16[400,128]{1,0:T(8,128)(2,1)S(1)}, u32[]{:S(2)}, u32[]{:S(2)}) collective-permute-start(bf16[400,128]{1,0:T(8,128)(2,1)} %get-tuple-element.14), channel_id=1, source_target_pairs={{0,4},{4,0},{8,12},{12,8},{16,20},{20,16},{24,28},{28,24},{1,5},{5... | collective-permute-start | bytes 307208 | tf_op jit(solution)/shard_map/ppermute | solution.py:542
  11.0 0.0 copy-done
  11.0 0.0 collective-permute-start
  11.0 0.5 collective-permute-start.3
  11.5 0.0 collective-permute-done.10.refs_14_
  11.5 1.5 %collective-permute-start.12 = (bf16[400,128]{1,0:T(8,128)(2,1)S(1)}, bf16[400,128]{1,0:T(8,128)(2,1)S(1)}, u32[]{:S(2)}, u32[]{:S(2)}) collective-permute-start(bf16[400,128]{1,0:T(8,128)(2,1)S(1)} %collective-permute-done.10.refs_14_), channel_id=1, source_target_pairs={{0,2},{1,3},{2,0},{3,1},{4,6},{5,7},{6,4},{7,5},{8,10},{9,11},{10,... | collective-permute-start | bytes 307208 | tf_op jit(solution)/shard_map/ppermute | solution.py:542
  13.0 0.0 collective-permute-done.4.refs_8_
  13.0 0.0 collective-permute-start.11
  13.0 1.3 %collective-permute-done.6.refs_10_ = bf16[400,128]{1,0:T(8,128)(2,1)S(1)} collective-permute-done((bf16[400,128]{1,0:T(8,128)(2,1)}, bf16[400,128]{1,0:T(8,128)(2,1)S(1)}, u32[]{:S(2)}, u32[]{:S(2)}) %collective-permute-start.6) | collective-permute-done | bytes 102432 | tf_op jit(solution)/shard_map/ppermute | solution.py:542
  14.4 1.5 %collective-permute-start.8 = (bf16[400,128]{1,0:T(8,128)(2,1)S(1)}, bf16[400,128]{1,0:T(8,128)(2,1)S(1)}, u32[]{:S(2)}, u32[]{:S(2)}) collective-permute-start(bf16[400,128]{1,0:T(8,128)(2,1)S(1)} %collective-permute-done.6.refs_10_), channel_id=1, source_target_pairs={{0,2},{1,3},{2,0},{3,1},{4,6},{5,7},{6,4},{7,5},{8,10},{9,11},{10,... | collective-permute-start | bytes 307208 | tf_op jit(solution)/shard_map/ppermute | solution.py:542
  15.9 0.0 collective-permute-done.refs_3_
  15.9 0.0 collective-permute-start.2
  15.9 0.0 collective-permute-done.3.refs_7_
  15.9 0.5 collective-permute-start.5
  16.4 0.2 collective-permute-done.12.refs_16_
  16.6 0.0 collective-permute-start.13
  16.6 0.0 collective-permute-done.11.refs_15_
  16.6 0.5 collective-permute-start.7
  17.1 1.9 %collective-permute-done.8.refs_12_ = bf16[400,128]{1,0:T(8,128)(2,1)S(1)} collective-permute-done((bf16[400,128]{1,0:T(8,128)(2,1)S(1)}, bf16[400,128]{1,0:T(8,128)(2,1)S(1)}, u32[]{:S(2)}, u32[]{:S(2)}) %collective-permute-start.8) | collective-permute-done | bytes 102432 | tf_op jit(solution)/shard_map/ppermute | solution.py:542
  19.0 0.0 collective-permute-start.9
  19.0 0.0 collective-permute-done.2.refs_5_
  19.0 0.0 collective-permute-done.5.refs_9_
  19.1 0.0 collective-permute-done.13.refs_17_
  19.1 0.0 collective-permute-done.7.refs_11_
  19.1 1.3 %collective-permute-done.9.refs_13_ = bf16[400,128]{1,0:T(8,128)(2,1)S(1)} collective-permute-done((bf16[400,128]{1,0:T(8,128)(2,1)S(1)}, bf16[400,128]{1,0:T(8,128)(2,1)S(1)}, u32[]{:S(2)}, u32[]{:S(2)}) %collective-permute-start.9) | collective-permute-done | bytes 102432 | tf_op jit(solution)/shard_map/ppermute | solution.py:542
  20.3 0.0 copy-done.3
  20.3 14.5 %tile_backward.1 = (bf16[5,5,2,16,128]{4,3,2,1,0:T(8,128)(2,1)S(1)}, bf16[4,2,2,112,128]{4,3,2,1,0:T(8,128)(2,1)S(1)}, bf16[4,2,2,112,128]{4,3,2,1,0:T(8,128)(2,1)S(1)}) custom-call(s32[1]{0:T(128)} %bitcast.refs_0_.depth_ref, s32[1]{0:T(128)} %bitcast.1.odd.refs_1_, bf16[512,128]{1,0:T(8,128)(2,1)S(1)} %bitcast.28, ...), custom_call_target="tpu_custom_call" | custom-call | flops 9059696640 | bytes 6553600 | tf_op jit(solution)/shard_map/tile_backward/pallas_call | solution.py:516
  34.9 0.2 collective-permute-start.14
  35.1 1.7 %collective-permute-done.14 = bf16[4,2,2,112,128]{4,3,2,1,0:T(8,128)(2,1)S(1)} collective-permute-done((bf16[4,2,2,112,128]{4,3,2,1,0:T(8,128)(2,1)S(1)}, bf16[4,2,2,112,128]{4,3,2,1,0:T(8,128)(2,1)S(1)}, u32[]{:S(2)}, u32[]{:S(2)}) %collective-permute-start.14) | collective-permute-done | bytes 458784 | tf_op jit(solution)/shard_map/ppermute | solution.py:542
  36.8 0.1 convert_add_fusion
  36.9 0.0 copy-start.2
  36.9 0.1 fusion.2
  36.9 3.2 %collective-permute-start.15 = (bf16[2,2,112,128]{3,2,1,0:T(8,128)(2,1)S(1)}, bf16[2,2,112,128]{3,2,1,0:T(8,128)(2,1)S(1)}, u32[]{:S(2)}, u32[]{:S(2)}) collective-permute-start(bf16[2,2,112,128]{3,2,1,0:T(8,128)(2,1)S(1)} %get-tuple-element.19), channel_id=1, source_target_pairs={{0,4},{4,0},{8,12},{12,8},{16,20},{20,16},{24,28},{28,24},{1,5},{5... | collective-permute-start | bytes 344072 | tf_op jit(solution)/shard_map/ppermute | solution.py:542
  40.1 1.6 %collective-permute-start.16 = (bf16[2,2,112,128]{3,2,1,0:T(8,128)(2,1)S(1)}, bf16[2,2,112,128]{3,2,1,0:T(8,128)(2,1)S(1)}, u32[]{:S(2)}, u32[]{:S(2)}) collective-permute-start(bf16[2,2,112,128]{3,2,1,0:T(8,128)(2,1)S(1)} %get-tuple-element.21), channel_id=1, source_target_pairs={{0,8},{4,12},{8,0},{12,4},{16,24},{20,28},{24,16},{28,20},{1,9},{5... | collective-permute-start | bytes 344072 | tf_op jit(solution)/shard_map/ppermute | solution.py:542
  41.7 0.0 collective-permute-start.17
  41.7 1.9 %collective-permute-done.15 = bf16[2,2,112,128]{3,2,1,0:T(8,128)(2,1)S(1)} collective-permute-done((bf16[2,2,112,128]{3,2,1,0:T(8,128)(2,1)S(1)}, bf16[2,2,112,128]{3,2,1,0:T(8,128)(2,1)S(1)}, u32[]{:S(2)}, u32[]{:S(2)}) %collective-permute-start.15) | collective-permute-done | bytes 114720 | tf_op jit(solution)/shard_map/ppermute | solution.py:542
  43.5 2.6 %collective-permute-done.16 = bf16[2,2,112,128]{3,2,1,0:T(8,128)(2,1)S(1)} collective-permute-done((bf16[2,2,112,128]{3,2,1,0:T(8,128)(2,1)S(1)}, bf16[2,2,112,128]{3,2,1,0:T(8,128)(2,1)S(1)}, u32[]{:S(2)}, u32[]{:S(2)}) %collective-permute-start.16) | collective-permute-done | bytes 114720 | tf_op jit(solution)/shard_map/ppermute | solution.py:542
  46.1 1.2 %collective-permute-done.17 = bf16[2,2,112,128]{3,2,1,0:T(8,128)(2,1)S(1)} collective-permute-done((bf16[2,2,112,128]{3,2,1,0:T(8,128)(2,1)S(1)}, bf16[2,2,112,128]{3,2,1,0:T(8,128)(2,1)S(1)}, u32[]{:S(2)}, u32[]{:S(2)}) %collective-permute-start.17) | collective-permute-done | bytes 114720 | tf_op jit(solution)/shard_map/ppermute | solution.py:542
  47.3 0.1 fusion.1
  47.4 2.7 %collective-permute-start.18 = (bf16[2,112,128]{2,1,0:T(8,128)(2,1)S(1)}, bf16[2,112,128]{2,1,0:T(8,128)(2,1)S(1)}, u32[]{:S(2)}, u32[]{:S(2)}) collective-permute-start(bf16[2,112,128]{2,1,0:T(8,128)(2,1)S(1)} %fusion.5), channel_id=1, source_target_pairs={{0,16},{4,20},{8,24},{12,28},{16,0},{20,4},{24,8},{28,12},{1,17},{... | collective-permute-start | bytes 172040 | tf_op jit(solution)/shard_map/ppermute | solution.py:542
  50.1 1.8 %input_gradient.1 = bf16[512,128]{1,0:T(8,128)(2,1)} custom-call(s32[1]{0:T(128)} %bitcast.refs_0_.depth_ref, bf16[16,128]{1,0:T(8,128)(2,1)S(1)} %copy-done.3, bf16[5,5,2,16,128]{4,3,2,1,0:T(8,128)(2,1)S(1)} %get-tuple-element.16.last, bf16[27,128,128]{2,1,0:T(8,128)(2,1)S(1)} %copy-done.2), custom_call_target="tpu_custom_call" | custom-call | flops 603979776 | bytes 1409024 | tf_op jit(solution)/shard_map/input_gradient/pallas_call | solution.py:455
  52.0 0.6 %collective-permute-done.18 = bf16[2,112,128]{2,1,0:T(8,128)(2,1)S(1)} collective-permute-done((bf16[2,112,128]{2,1,0:T(8,128)(2,1)S(1)}, bf16[2,112,128]{2,1,0:T(8,128)(2,1)S(1)}, u32[]{:S(2)}, u32[]{:S(2)}) %collective-permute-start.18) | collective-permute-done | bytes 57376 | tf_op jit(solution)/shard_map/ppermute | solution.py:542
  52.6 0.6 %slice_bitcast_fusion = (f32[13824]{0:T(1024)}, f32[13824]{0:T(1024)}) fusion(f32[2,112,128]{2,1,0:T(8,128)S(1)} %bitcast_add_fusion.1), kind=kLoop, calls=%fused_computation.13 | loop fusion | bytes 221184 | tf_op jit(solution)/shard_map/reshape;squeeze | solution.py:583
  (7 shorter events, 0.0 us)
Async XLA Ops:
  0.6 7.5 %collective-permute-start.1 = (bf16[512,128]{1,0:T(8,128)(2,1)}, bf16[512,128]{1,0:T(8,128)(2,1)S(1)}, u32[]{:S(2)}, u32[]{:S(2)}) collective-permute-start(bf16[512,128]{1,0:T(8,128)(2,1)} %bitcast.25), channel_id=1, source_target_pairs={{0,2},{1,3},{2,0},{3,1},{4,6},{5,7},{6,4},{7,5},{8,10},{9,11},{10,... | collective-permute-start | bytes 393224 | tf_op jit(solution)/shard_map/ppermute | solution.py:542
  3.6 9.4 %collective-permute-start.4 = (bf16[512,128]{1,0:T(8,128)(2,1)}, bf16[512,128]{1,0:T(8,128)(2,1)S(1)}, u32[]{:S(2)}, u32[]{:S(2)}) collective-permute-start(bf16[512,128]{1,0:T(8,128)(2,1)} %bitcast.29), channel_id=1, source_target_pairs={{0,2},{1,3},{2,0},{3,1},{4,6},{5,7},{6,4},{7,5},{8,10},{9,11},{10,... | collective-permute-start | bytes 393224 | tf_op jit(solution)/shard_map/ppermute | solution.py:542
  3.7 7.3 %copy-start = (bf16[1,1,512,128]{3,2,1,0:T(8,128)(2,1)S(1)}, bf16[1,1,512,128]{3,2,1,0:T(8,128)(2,1)}, u32[]{:S(2)}) copy-start(bf16[1,1,512,128]{3,2,1,0:T(8,128)(2,1)} %param.6) | copy-start | bytes 393220
  3.7 7.3 %copy-start.1 = (bf16[1,1,512,128]{3,2,1,0:T(8,128)(2,1)S(1)}, bf16[1,1,512,128]{3,2,1,0:T(8,128)(2,1)}, u32[]{:S(2)}) copy-start(bf16[1,1,512,128]{3,2,1,0:T(8,128)(2,1)} %param.7) | copy-start | bytes 393220
  5.5 6.0 %collective-permute-start.10 = (bf16[400,128]{1,0:T(8,128)(2,1)}, bf16[400,128]{1,0:T(8,128)(2,1)S(1)}, u32[]{:S(2)}, u32[]{:S(2)}) collective-permute-start(bf16[400,128]{1,0:T(8,128)(2,1)} %get-tuple-element.15), channel_id=1, source_target_pairs={{4,8},{8,4},{12,16},{16,12},{20,24},{24,20},{5,9},{9,5},{13,17},{1... | collective-permute-start | bytes 307208 | tf_op jit(solution)/shard_map/ppermute | solution.py:550
  8.2 12.2 %copy-start.3 = (bf16[16,128]{1,0:T(8,128)(2,1)S(1)}, bf16[16,128]{1,0:T(8,128)(2,1)}, u32[]{:S(2)}) copy-start(bf16[16,128]{1,0:T(8,128)(2,1)} %get-tuple-element.11.refs_18_.own_table) | copy-start | bytes 12292
  8.2 6.2 %collective-permute-start.6 = (bf16[400,128]{1,0:T(8,128)(2,1)}, bf16[400,128]{1,0:T(8,128)(2,1)S(1)}, u32[]{:S(2)}, u32[]{:S(2)}) collective-permute-start(bf16[400,128]{1,0:T(8,128)(2,1)} %get-tuple-element.14), channel_id=1, source_target_pairs={{0,4},{4,0},{8,12},{12,8},{16,20},{20,16},{24,28},{28,24},{1,5},{5... | collective-permute-start | bytes 307208 | tf_op jit(solution)/shard_map/ppermute | solution.py:542
  11.0 4.9 %collective-permute-start = (bf16[512,128]{1,0:T(8,128)(2,1)S(1)}, bf16[512,128]{1,0:T(8,128)(2,1)S(1)}, u32[]{:S(2)}, u32[]{:S(2)}) collective-permute-start(bf16[512,128]{1,0:T(8,128)(2,1)S(1)} %bitcast.27), channel_id=1, source_target_pairs={{0,1},{1,0},{2,3},{3,2},{4,5},{5,4},{6,7},{7,6},{8,9},{9,8},{10,11... | collective-permute-start | bytes 393224 | tf_op jit(solution)/shard_map/ppermute | solution.py:542
  11.0 4.8 %collective-permute-start.3 = (bf16[512,128]{1,0:T(8,128)(2,1)S(1)}, bf16[512,128]{1,0:T(8,128)(2,1)S(1)}, u32[]{:S(2)}, u32[]{:S(2)}) collective-permute-start(bf16[512,128]{1,0:T(8,128)(2,1)S(1)} %bitcast.31), channel_id=1, source_target_pairs={{0,1},{1,0},{2,3},{3,2},{4,5},{5,4},{6,7},{7,6},{8,9},{9,8},{10,11... | collective-permute-start | bytes 393224 | tf_op jit(solution)/shard_map/ppermute | solution.py:542
  11.5 5.1 %collective-permute-start.12 = (bf16[400,128]{1,0:T(8,128)(2,1)S(1)}, bf16[400,128]{1,0:T(8,128)(2,1)S(1)}, u32[]{:S(2)}, u32[]{:S(2)}) collective-permute-start(bf16[400,128]{1,0:T(8,128)(2,1)S(1)} %collective-permute-done.10.refs_14_), channel_id=1, source_target_pairs={{0,2},{1,3},{2,0},{3,1},{4,6},{5,7},{6,4},{7,5},{8,10},{9,11},{10,... | collective-permute-start | bytes 307208 | tf_op jit(solution)/shard_map/ppermute | solution.py:542
  13.0 3.6 %collective-permute-start.11 = (bf16[400,128]{1,0:T(8,128)(2,1)S(1)}, bf16[400,128]{1,0:T(8,128)(2,1)S(1)}, u32[]{:S(2)}, u32[]{:S(2)}) collective-permute-start(bf16[400,128]{1,0:T(8,128)(2,1)S(1)} %collective-permute-done.10.refs_14_), channel_id=1, source_target_pairs={{0,1},{1,0},{2,3},{3,2},{4,5},{5,4},{6,7},{7,6},{8,9},{9,8},{10,11... | collective-permute-start | bytes 307208 | tf_op jit(solution)/shard_map/ppermute | solution.py:542
  14.4 4.7 %collective-permute-start.8 = (bf16[400,128]{1,0:T(8,128)(2,1)S(1)}, bf16[400,128]{1,0:T(8,128)(2,1)S(1)}, u32[]{:S(2)}, u32[]{:S(2)}) collective-permute-start(bf16[400,128]{1,0:T(8,128)(2,1)S(1)} %collective-permute-done.6.refs_10_), channel_id=1, source_target_pairs={{0,2},{1,3},{2,0},{3,1},{4,6},{5,7},{6,4},{7,5},{8,10},{9,11},{10,... | collective-permute-start | bytes 307208 | tf_op jit(solution)/shard_map/ppermute | solution.py:542
  15.9 3.2 %collective-permute-start.2 = (bf16[512,128]{1,0:T(8,128)(2,1)S(1)}, bf16[512,128]{1,0:T(8,128)(2,1)S(1)}, u32[]{:S(2)}, u32[]{:S(2)}) collective-permute-start(bf16[512,128]{1,0:T(8,128)(2,1)S(1)} %collective-permute-done.1.refs_4_), channel_id=1, source_target_pairs={{0,1},{1,0},{2,3},{3,2},{4,5},{5,4},{6,7},{7,6},{8,9},{9,8},{10,11... | collective-permute-start | bytes 393224 | tf_op jit(solution)/shard_map/ppermute | solution.py:542
  15.9 3.2 %collective-permute-start.5 = (bf16[512,128]{1,0:T(8,128)(2,1)S(1)}, bf16[512,128]{1,0:T(8,128)(2,1)S(1)}, u32[]{:S(2)}, u32[]{:S(2)}) collective-permute-start(bf16[512,128]{1,0:T(8,128)(2,1)S(1)} %collective-permute-done.4.refs_8_), channel_id=1, source_target_pairs={{0,1},{1,0},{2,3},{3,2},{4,5},{5,4},{6,7},{7,6},{8,9},{9,8},{10,11... | collective-permute-start | bytes 393224 | tf_op jit(solution)/shard_map/ppermute | solution.py:542
  16.6 2.5 %collective-permute-start.13 = (bf16[400,128]{1,0:T(8,128)(2,1)S(1)}, bf16[400,128]{1,0:T(8,128)(2,1)S(1)}, u32[]{:S(2)}, u32[]{:S(2)}) collective-permute-start(bf16[400,128]{1,0:T(8,128)(2,1)S(1)} %collective-permute-done.12.refs_16_), channel_id=1, source_target_pairs={{0,1},{1,0},{2,3},{3,2},{4,5},{5,4},{6,7},{7,6},{8,9},{9,8},{10,11... | collective-permute-start | bytes 307208 | tf_op jit(solution)/shard_map/ppermute | solution.py:542
  16.6 2.5 %collective-permute-start.7 = (bf16[400,128]{1,0:T(8,128)(2,1)S(1)}, bf16[400,128]{1,0:T(8,128)(2,1)S(1)}, u32[]{:S(2)}, u32[]{:S(2)}) collective-permute-start(bf16[400,128]{1,0:T(8,128)(2,1)S(1)} %collective-permute-done.6.refs_10_), channel_id=1, source_target_pairs={{0,1},{1,0},{2,3},{3,2},{4,5},{5,4},{6,7},{7,6},{8,9},{9,8},{10,11... | collective-permute-start | bytes 307208 | tf_op jit(solution)/shard_map/ppermute | solution.py:542
  19.0 1.3 %collective-permute-start.9 = (bf16[400,128]{1,0:T(8,128)(2,1)S(1)}, bf16[400,128]{1,0:T(8,128)(2,1)S(1)}, u32[]{:S(2)}, u32[]{:S(2)}) collective-permute-start(bf16[400,128]{1,0:T(8,128)(2,1)S(1)} %collective-permute-done.8.refs_12_), channel_id=1, source_target_pairs={{0,1},{1,0},{2,3},{3,2},{4,5},{5,4},{6,7},{7,6},{8,9},{9,8},{10,11... | collective-permute-start | bytes 307208 | tf_op jit(solution)/shard_map/ppermute | solution.py:542
  34.9 1.9 %collective-permute-start.14 = (bf16[4,2,2,112,128]{4,3,2,1,0:T(8,128)(2,1)S(1)}, bf16[4,2,2,112,128]{4,3,2,1,0:T(8,128)(2,1)S(1)}, u32[]{:S(2)}, u32[]{:S(2)}) collective-permute-start(bf16[4,2,2,112,128]{4,3,2,1,0:T(8,128)(2,1)S(1)} %get-tuple-element.18), channel_id=1, source_target_pairs={{0,1},{1,0},{2,3},{3,2},{4,5},{5,4},{6,7},{7,6},{8,9},{9,8},{10,11... | collective-permute-start | bytes 1376264 | tf_op jit(solution)/shard_map/ppermute | solution.py:542
  36.9 13.3 %copy-start.2 = (bf16[27,128,128]{2,1,0:T(8,128)(2,1)S(1)}, bf16[27,128,128]{2,1,0:T(8,128)(2,1)}, u32[]{:S(2)}) copy-start(bf16[27,128,128]{2,1,0:T(8,128)(2,1)} %far_first.1) | copy-start | bytes 2654212
  36.9 6.6 %collective-permute-start.15 = (bf16[2,2,112,128]{3,2,1,0:T(8,128)(2,1)S(1)}, bf16[2,2,112,128]{3,2,1,0:T(8,128)(2,1)S(1)}, u32[]{:S(2)}, u32[]{:S(2)}) collective-permute-start(bf16[2,2,112,128]{3,2,1,0:T(8,128)(2,1)S(1)} %get-tuple-element.19), channel_id=1, source_target_pairs={{0,4},{4,0},{8,12},{12,8},{16,20},{20,16},{24,28},{28,24},{1,5},{5... | collective-permute-start | bytes 344072 | tf_op jit(solution)/shard_map/ppermute | solution.py:542
  40.1 6.0 %collective-permute-start.16 = (bf16[2,2,112,128]{3,2,1,0:T(8,128)(2,1)S(1)}, bf16[2,2,112,128]{3,2,1,0:T(8,128)(2,1)S(1)}, u32[]{:S(2)}, u32[]{:S(2)}) collective-permute-start(bf16[2,2,112,128]{3,2,1,0:T(8,128)(2,1)S(1)} %get-tuple-element.21), channel_id=1, source_target_pairs={{0,8},{4,12},{8,0},{12,4},{16,24},{20,28},{24,16},{28,20},{1,9},{5... | collective-permute-start | bytes 344072 | tf_op jit(solution)/shard_map/ppermute | solution.py:542
  41.7 5.7 %collective-permute-start.17 = (bf16[2,2,112,128]{3,2,1,0:T(8,128)(2,1)S(1)}, bf16[2,2,112,128]{3,2,1,0:T(8,128)(2,1)S(1)}, u32[]{:S(2)}, u32[]{:S(2)}) collective-permute-start(bf16[2,2,112,128]{3,2,1,0:T(8,128)(2,1)S(1)} %get-tuple-element.20), channel_id=1, source_target_pairs={{0,12},{4,8},{8,4},{12,0},{16,28},{20,24},{24,20},{28,16},{1,13},{... | collective-permute-start | bytes 344072 | tf_op jit(solution)/shard_map/ppermute | solution.py:542
  47.4 5.1 %collective-permute-start.18 = (bf16[2,112,128]{2,1,0:T(8,128)(2,1)S(1)}, bf16[2,112,128]{2,1,0:T(8,128)(2,1)S(1)}, u32[]{:S(2)}, u32[]{:S(2)}) collective-permute-start(bf16[2,112,128]{2,1,0:T(8,128)(2,1)S(1)} %fusion.5), channel_id=1, source_target_pairs={{0,16},{4,20},{8,24},{12,28},{16,0},{20,4},{24,8},{28,12},{1,17},{... | collective-permute-start | bytes 172040 | tf_op jit(solution)/shard_map/ppermute | solution.py:542
